TPU v7x, 128 devices: a whole 4x4x4 slice. The times are simulated.
128 devices in a mesh: dp: 8 (over z_hi, x), tensor: 16 (over z_lo, y, core).
Axes of the slice: x: 4, y: 4, z: 4 (z_hi: 2, z_lo: 2; z = z_hi * 2 + z_lo), core: 2. Of those that a mesh axis runs over, the one named last changes fastest.
Arguments:
- partials: bfloat16 [16, 4096, 16384], P('tensor', 'dp'), parts along dimension 1, may hold values from -6 to 6
- residual: bfloat16 [4096, 16384], P(('dp', 'tensor')), parts along dimension 0, may hold values from -6 to 6
- norm_gain: bfloat16 [16384], replicated, may hold values from 0.099609375 to 1.8984375
- qkv_weight: bfloat16 [16384, 10240], P(None, 'tensor'), may hold values from -0.046875 to 0.046875
Outputs:
- new_stream: bfloat16 [4096, 16384], P(('dp', 'tensor')), parts along dimension 0
- projected: bfloat16 [4096, 10240], P('dp', 'tensor'), parts along dimension 0
There are 8 independent parts, one for each index of `dp`. A program takes and returns all parts, laid end to end along the dimension named above; an argument that names none is the same for every part. Nothing has to cross between parts.
All inputs are finite; a program needn't handle non-finite values.
Results may differ from a plain program's by a relative error of at most 0.024.
Values may be sent and summed in bfloat16 or wider, within the bound.
No kernel may reach another device: no remote copies, remote signals or barrier semaphores. Data moves between devices by JAX's collectives and lax.ppermute only.
A program may use at most 256 MiB of HBM per device.

v0:
```python
import jax
import jax.numpy as jnp
from jax import lax
from jax.sharding import PartitionSpec as P


def rms_normed(stream, norm_gain):
    meansq = jnp.mean(stream * stream, axis=-1, keepdims=True)
    return (stream * lax.rsqrt(meansq + 1e-05) * norm_gain.astype(jnp.float32)).astype(jnp.bfloat16)


def per_device(partials, residual, norm_gain, qkv_weight):
    partial_term = partials[0].astype(jnp.float32)
    summed = lax.psum_scatter(
        partial_term.astype(jnp.bfloat16), "tensor", scatter_dimension=0, tiled=True
    ).astype(jnp.float32)
    stream = residual.astype(jnp.float32) + summed
    normed = rms_normed(stream, norm_gain)
    projected = jnp.dot(
        lax.all_gather(normed, "tensor", axis=0, tiled=True),
        qkv_weight,
        preferred_element_type=jnp.float32,
    )
    return (stream.astype(jnp.bfloat16), projected.astype(jnp.bfloat16))


def solution(mesh):
    in_specs = (P("tensor", "dp", None), P(("dp", "tensor"), None), P(), P(None, "tensor"))
    out_specs = (P(("dp", "tensor"), None), P("dp", "tensor"))
    return jax.shard_map(
        per_device, mesh=mesh, in_specs=in_specs, out_specs=out_specs, check_vma=False
    )
```

profile of v0, /device:TPU:1, one launch (start us, length us, event | category | flops | bytes accessed | tf_op | source)
XLA Modules:
  0.0 233.8 jit_solution(4579417330428846239)
XLA Ops:
  7.2 0.0 reduce-scatter.2.cloned.1.call-start
  7.2 0.0 copy-start.2
  7.2 0.0 copy-start
  7.2 0.7 reduce-scatter.2.cloned.1.call-update
  7.9 0.0 all-gather.2.cloned.1.call-start
  7.9 0.0 copy-done.2
  8.0 102.5 %reduce-scatter.2.cloned.1.call-done = bf16[32,16384]{1,0:T(8,128)(2,1)} async-done(((bf16[512,16384]{1,0:T(8,128)(2,1)}), bf16[32,16384]{1,0:T(8,128)(2,1)}) %reduce-scatter.2.cloned.1.call-update) | async-done | bytes 1048592 | tf_op jit(solution)/shard_map/reduce_scatter | solution.py:14
  110.5 0.0 copy-done
  110.5 0.0 copy-start.1
  110.5 1.8 multiply_reduce_fusion
  112.2 0.0 copy-done.1
  112.2 1.7 multiply_convert_fusion
  114.0 0.0 all-gather.2.cloned.1.call-update
  114.0 92.4 %all-gather.2.cloned.1.call-done = bf16[512,16384]{1,0:T(8,128)(2,1)} async-done(((bf16[32,16384]{1,0:T(8,128)(2,1)}), bf16[512,16384]{1,0:T(8,128)(2,1)}) %all-gather.2.cloned.1.call-update) | async-done | bytes 16777232 | tf_op jit(solution)/shard_map/all_gather | solution.py:20
  206.4 20.6 %convolution_convert_fusion = bf16[512,640]{1,0:T(8,128)(2,1)} fusion(bf16[512,16384]{1,0:T(8,128)(2,1)} %all-gather.2.cloned.1.call-done, bf16[16384,640]{1,0:T(8,128)(2,1)} %param.7), kind=kOutput, calls=%fused_computation.4 | convolution fusion | flops 10737745920 | bytes 38404096 | tf_op jit(solution)/shard_map/dot_general | solution.py:19
  (2 shorter events, 0.0 us)
Async XLA Ops:
  7.2 103.3 %reduce-scatter.2.cloned.1.call-start = ((), (), s32[]{:S(2)}) async-start(), calls=%async_computation.1 | async-start | bytes 17825792 | tf_op jit(solution)/shard_map/reduce_scatter | solution.py:14
  7.2 0.8 copy-start.2
  7.2 103.2 %copy-start = (bf16[32,16384]{1,0:T(8,128)(2,1)S(1)}, bf16[32,16384]{1,0:T(8,128)(2,1)}, u32[]{:S(2)}) copy-start(bf16[32,16384]{1,0:T(8,128)(2,1)} %param.5) | copy-start | bytes 3145732
  7.9 198.5 %all-gather.2.cloned.1.call-start = ((), (), s32[]{:S(2)}) async-start(), calls=%async_computation.2 | async-start | bytes 17825792 | tf_op jit(solution)/shard_map/all_gather | solution.py:20
  110.5 1.8 copy-start.1
Sparse Core Ops, SparseCore 0:
  10.4 100.0 reduce-scatter.1
  114.1 92.2 all-gather.1
where the time goes:
time: 234 us
  waiting for transfers between devices  196 us (84%)
  matrix products  20.6 us (9%)
  between operations  14.1 us (6%)
  other arithmetic  3.51 us (2%)
    reduce_scatter x1, waiting for transfers between devices, per_device(): lax.psum_scatter(partial_term.astype(jnp.bfloat16), 'tensor', scatter_dim...  102 us
    all_gather x1, waiting for transfers between devices, per_device(): lax.all_gather(normed, 'tensor', axis=0, tiled=True)  92.4 us
    dot_general x1, matrix products, per_device(): jnp.dot(lax.all_gather(normed, 'tensor', axis=0, tiled=True), qkv_weight,...  20.6 us
  transfers between devices with their start and end apart: 2, of which 2 were waited for; matrix products, arithmetic and copies ran while one was open for 0% of the time, Pallas kernels for 0%

commit v1 on v0

v1 whole, which is shorter than its diff:
```python
import functools

import jax
import jax.numpy as jnp
from jax import lax
from jax.experimental import pallas as pl
from jax.experimental.pallas import tpu as pltpu
from jax.sharding import PartitionSpec as P

NZ, NY, NC = 2, 4, 2
ROWS = 32
D = 16384
COLS = 640
STEP = 256
NOTE = 128
ANY = pl.BlockSpec(memory_space=pl.ANY)
HBM = pl.BlockSpec(memory_space=pltpu.HBM)
SMEM = pl.BlockSpec(memory_space=pltpu.SMEM)
VMEM = pl.BlockSpec(memory_space=pltpu.VMEM)
VMEM_BYTES = 48 * 1024 * 1024


def index_of(z, y, c):
    return (z * NY + y % NY) * NC + c


def pairs(move):
    return [
        (index_of(z, y, c), index_of(*move(z, y, c)))
        for z in range(NZ)
        for y in range(NY)
        for c in range(NC)
    ]


MOVES = {"a": (0, 1), "b": (0, 3), "z": (1, 0)}
TO = {d: pairs(lambda z, y, c, m=m: (z ^ m[0], y ^ m[1], c)) for d, m in MOVES.items()}
TO_CORE = pairs(lambda z, y, c: (z, y, 1 - c))


def send(x, where):
    return lax.ppermute(x, "tensor", where)


def bf16(x):
    return x.astype(jnp.bfloat16)


def shape(*dims, dtype=jnp.bfloat16):
    return jax.ShapeDtypeStruct(dims, dtype)


class Copies:
    def __init__(self, sems):
        self.sems, self.count = sems, 0

    def start(self, source, target):
        copy = pltpu.make_async_copy(source, target, self.sems.at[self.count])
        self.count += 1
        copy.start()
        return copy


def by_columns(width, body):
    steps = width // STEP
    unroll = next(u for u in (3, 7, 5, 2, 1) if steps % u == 0)

    def at(i, carry):
        return body(pl.ds(pl.multiple_of(i * STEP, STEP), STEP), carry)

    return functools.partial(lax.fori_loop, 0, steps, at, unroll=unroll)


def total_of(sources, columns):
    total = sources[0][:, columns].astype(jnp.float32)
    for ref in sources[1:]:
        total = total + ref[:, columns].astype(jnp.float32)
    return total


def call(name, kernel, ins, outs, scratch, copies, after, aliases={}, pinned=()):
    return pl.pallas_call(
        kernel,
        in_specs=[SMEM]
        + [HBM if i in pinned else ANY for i in range(1, len(ins))]
        + [ANY] * len(after),
        out_specs=[ANY] * len(outs),
        name=name,
        out_shape=outs,
        scratch_shapes=scratch + [pltpu.SemaphoreType.DMA((copies,))],
        input_output_aliases=aliases,
        compiler_params=pltpu.CompilerParams(vmem_limit_bytes=VMEM_BYTES),
        cost_estimate=pl.CostEstimate(flops=0, bytes_accessed=1024, transcendentals=0),
    )(*ins, *after)


def copied(name, ins, outs, items, after, pinned=()):
    n = len(ins)

    def kernel(*refs):
        place, sources = refs[0], refs[1:n]
        targets, sems = refs[n + len(after) : -1], refs[-1]
        copies = Copies(sems)
        going = [
            copies.start(source, targets[k].at[index])
            for k, index, source in items(place, sources)
        ]
        for copy in going:
            copy.wait()

    return call(name, kernel, ins, outs, [], 36, after, pinned=pinned)


def added(name, ins, outs, items, after):
    n = len(ins)
    plan = items(None, [None] * (n - 1))
    most = max(len(sources) for _, _, sources, _ in plan)
    widest = max(width for _, _, _, width in plan)

    def kernel(*refs):
        place, sources = refs[0], refs[1:n]
        targets = refs[n + len(after) : n + len(after) + len(outs)]
        taken, made, sems = refs[-3:]
        copies = Copies(sems)
        todo, storing = [], []
        for i, (k, index, blocks, width) in enumerate(items(place, sources)):
            slots = [taken.at[i, j, :, pl.ds(0, width)] for j in range(len(blocks))]
            loads = [copies.start(b, s) for b, s in zip(blocks, slots)]
            todo.append((k, index, slots, loads, width))
        for i, (k, index, slots, loads, width) in enumerate(todo):
            for copy in loads:
                copy.wait()

            def body(columns, carry, i=i, slots=slots):
                made[i, :, columns] = bf16(total_of(slots, columns))
                return carry

            by_columns(width, body)(0)
            here = made.at[i, :, pl.ds(0, width)]
            storing.append(copies.start(here, targets[k].at[index]))
        for copy in storing:
            copy.wait()

    scratch = [
        pltpu.VMEM((len(plan), most, ROWS, widest), jnp.bfloat16),
        pltpu.VMEM((len(plan), ROWS, widest), jnp.bfloat16),
    ]
    return call(name, kernel, ins, outs, scratch, len(plan) * (most + 1), after, pinned=(1,))


class Part:
    def __init__(self, start, features, dims, note=0):
        self.start, self.features, self.note = start, features, note
        self.sent = features + note
        self.columns = pl.ds(start, features)
        self.dims = dims

    def apart(self, *steps):
        z = y = 0
        for d, step in zip(self.dims, steps):
            if step:
                z, y = z ^ MOVES[d][0], y ^ MOVES[d][1]
        return z, y


class Stream:
    def __init__(self, *parts):
        self.parts = parts
        self.start = parts[0].start
        self.features = sum(p.features for p in parts)
        self.note = sum(p.note for p in parts)

    def sent(self, part):
        return pl.ds(part.start - self.start, part.sent)


def row_block(place, apart):
    z, y = place[0], place[1]
    return lax.bitwise_xor(z, apart[0]) * NY + lax.bitwise_xor(y, apart[1])


def block(place, apart, dc):
    c = place[2]
    return row_block(place, apart) * NC + lax.bitwise_xor(c, dc)


def give(place, terms, wanted, after):
    width = sum(stream.features for stream, _ in wanted)

    def items(at, refs):
        (x,) = refs
        found, offset = [], 0
        for stream, first in wanted:
            for part in stream.parts:
                to = pl.ds(offset + part.start - stream.start, part.features)
                found += [
                    (
                        0,
                        (e2 * 2 + e3, slice(None), to),
                        x.at[block(at, part.apart(first, e2, e3), 1), :, part.columns],
                    )
                    for e2 in (1, 0)
                    for e3 in (0, 1)
                ]
            offset += stream.features
        return found

    count = 4 * sum(len(stream.parts) for stream, _ in wanted)

    def kernel(*refs):
        at, x = refs[:2]
        target, held, sems = refs[-3:]
        copies = Copies(sems)
        todo = []
        for _, index, source in items(at, (x,)):
            todo.append((index, copies.start(source, held.at[index])))
        storing = []
        for index, copy in todo:
            copy.wait()
            storing.append(copies.start(held.at[index], target.at[index]))
        for copy in storing:
            copy.wait()

    scratch = [pltpu.VMEM((4, ROWS, width), jnp.bfloat16)]
    out = shape(4, ROWS, width)
    return call("give", kernel, [place, terms], [out], scratch, 2 * count, after, pinned=(1,))


def pair_sum(at, x, r, offset, part, e1, e2, e3):
    if x is None:
        return [None, None]
    mine = x.at[block(at, part.apart(e1, e2, e3), 0), :, part.columns]
    return [mine, r.at[e2 * 2 + e3, :, pl.ds(offset + part.start, part.features)]]


def pick(ref, index):
    return None if ref is None else ref.at[index]


def first_step(place, terms, got, offset, stream, after):
    def items(at, refs):
        return [
            (k, e2 * 2 + e3, pair_sum(at, refs[0], refs[1], offset, part, 1, e2, e3), part.features)
            for k, part in enumerate(stream.parts)
            for e2 in (1, 0)
            for e3 in (0, 1)
        ]

    outs = [shape(4, ROWS, part.features) for part in stream.parts]
    return added("first", [place, terms, got], outs, items, after)


def second_step(place, terms, rest, one, stream, after):
    def items(at, refs):
        x, r, v = refs[0], refs[1], refs[2:5]
        return [
            (k, e3, pair_sum(at, x, r, 0, part, 0, 1, e3) + [pick(v[k], 2 + e3)], part.features)
            for k, part in enumerate(stream.parts)
            for e3 in (0, 1)
        ]

    outs = [shape(2, ROWS, part.features) for part in stream.parts]
    return added("second", [place, terms, rest, *one], outs, items, after)


def third_step(place, terms, rest, one, two, stream, after):
    def items(at, refs):
        x, r, v, w = refs[0], refs[1], refs[2:5], refs[5:8]
        return [
            (
                k,
                slice(None),
                pair_sum(at, x, r, 0, part, 0, 0, 1) + [pick(v[k], 1), pick(w[k], 1)],
                part.features,
            )
            for k, part in enumerate(stream.parts)
        ]

    outs = [shape(ROWS, part.features) for part in stream.parts]
    return added("third", [place, terms, rest, *one, *two], outs, items, after)


def finish(place, terms, rest, one, two, three, stream, residual, gain, so_far, after):
    ins = [place, terms, rest, *one, *two, *three, residual, gain, *so_far]
    widest = max(part.features for part in stream.parts)
    there = pl.ds(stream.start, stream.features)

    def kernel(*refs):
        at, x = refs[0], refs[1]
        r, v, w, u = refs[2], refs[3:6], refs[6:9], refs[9:12]
        residual_ref, gain_ref = refs[12:14]
        base = len(ins) + len(after)
        stream_out, gained_out, squares_out = refs[base], refs[base + 1 : base + 4], refs[base + 4]
        taken, old, gains, news, made, sums, sems = refs[base + 5 :]
        copies = Copies(sems)
        first = [
            copies.start(residual_ref.at[:, there], old),
            copies.start(gain_ref.at[:, there], gains),
        ]
        if so_far:
            first.append(copies.start(refs[15], sums))
        else:
            sums[...] = jnp.zeros_like(sums)
        loads, slots = [], []
        for k, part in enumerate(stream.parts):
            blocks = pair_sum(at, x, r, 0, part, 0, 0, 0)
            blocks = blocks + [v[k].at[0], w[k].at[0], u[k]]
            slots.append([taken.at[k, j, :, pl.ds(0, part.features)] for j in range(5)])
            loads.append([copies.start(b, s) for b, s in zip(blocks, slots[k])])
        for copy in first:
            copy.wait()
        total = sums[...]
        storing = []
        for k, part in enumerate(stream.parts):
            for copy in loads[k]:
                copy.wait()

            def body(columns, carry, k=k, offset=part.start - stream.start):
                here = pl.ds(pl.multiple_of(offset + columns.start, 128), STEP)
                x = total_of(slots[k], columns) + old[:, here].astype(jnp.float32)
                news[:, here] = bf16(x)
                made[k, :, columns] = bf16(x * gains[:, here])
                square = x * x
                return carry + square[:, :128] + square[:, 128:]

            total = by_columns(part.features, body)(total)
            if not part.note:
                here = made.at[k, :, pl.ds(0, part.features)]
                storing.append(copies.start(here, gained_out[k]))
        sums[...] = total
        storing.append(copies.start(news, stream_out.at[:, there]))
        storing.append(copies.start(sums, squares_out))
        for k, part in enumerate(stream.parts):
            if part.note:
                mean = jnp.sum(total, axis=1, keepdims=True) / D
                scale = jnp.broadcast_to(lax.rsqrt(mean + 1e-05), (ROWS, NOTE))
                high = bf16(scale).astype(jnp.float32)
                middle = bf16(scale - high).astype(jnp.float32)
                low = scale - high - middle
                lane = lax.broadcasted_iota(jnp.int32, (ROWS, NOTE), 1)
                parts = jnp.where(lane == 0, high, jnp.where(lane == 1, middle, low))
                made[k, :, pl.ds(part.features, NOTE)] = bf16(jnp.where(lane < 3, parts, 0.0))
                here = made.at[k, :, pl.ds(0, part.sent)]
                storing.append(copies.start(here, gained_out[k]))
        for copy in storing:
            copy.wait()

    outs = [shape(ROWS, D)]
    outs += [shape(ROWS, part.sent) for part in stream.parts]
    outs += [shape(ROWS, 128, dtype=jnp.float32)]
    scratch = [
        pltpu.VMEM((3, 5, ROWS, widest), jnp.bfloat16),
        pltpu.VMEM((ROWS, stream.features), jnp.bfloat16),
        pltpu.VMEM((1, stream.features), jnp.float32),
        pltpu.VMEM((ROWS, stream.features), jnp.bfloat16),
        pltpu.VMEM((3, ROWS, widest + NOTE), jnp.bfloat16),
        pltpu.VMEM((ROWS, 128), jnp.float32),
    ]
    aliases = {14: 0} if so_far else {}
    out = call("finish", kernel, ins, outs, scratch, 3 * 5 + 8, after, aliases, pinned=(1,))
    return out[1:4], (out[0], out[4])


def two_blocks(place, own, far, stream, after):
    def items(at, refs):
        return [(k, e, refs[e * 3 + k]) for e in range(2) for k in range(3)]

    outs = [shape(2, ROWS, part.sent) for part in stream.parts]
    return copied("two", [place, *own, *far], outs, items, after)


def four_blocks(place, near, far, stream, after):
    def items(at, refs):
        found = []
        for k, part in enumerate(stream.parts):
            for e in range(2):
                some = pl.ds(2 * e, 2)
                found.append((k, some, refs[e * 3 + k]))
                found.append((3, (some, slice(None), stream.sent(part)), refs[e * 3 + k]))
        return found

    outs = [shape(4, ROWS, part.sent) for part in stream.parts]
    outs.append(shape(4, ROWS, stream.features + stream.note))
    out = copied("four", [place, *near, *far], outs, items, after)
    return out[:3], out[3]


def multiplied(place, near, far, beside, other_far, weight, total, stream, depth, after):
    tiles = stream.features // depth
    slots = 2
    last = bool(stream.note)
    half = NC * NZ * NY * ROWS // 2
    ins = [*near, *far, beside, *other_far]
    more = [] if total is None else [total]

    def kernel(place_ref, *refs):
        sources, weight_ref = refs[:10], refs[10]
        total_ref = None if total is None else refs[11]
        at = 11 + len(more) + len(after)
        result = refs[at]
        rows, held, sems = refs[at + 1], refs[at + 2], refs[-1]
        out = refs[at + 3] if last else result
        copies = Copies(sems)

        def load(t):
            there = pl.ds(stream.start + t * depth, depth)
            return copies.start(weight_ref.at[there], held.at[t % slots])

        loads = [load(t) for t in range(slots)]
        taking = []
        for k, part in enumerate(stream.parts):
            columns = stream.sent(part)
            for e2 in range(2):
                for e3 in range(2):
                    e = e2 * 2 + e3
                    blocks = (
                        (0, 0, sources[k].at[e]),
                        (0, 1, sources[6].at[e, :, columns]),
                        (1, 0, sources[3 + k].at[e]),
                        (1, 1, sources[7 + k].at[e]),
                    )
                    for e1, c, source in blocks:
                        z, y = part.apart(e1, e2, e3)
                        to = pl.ds(((z * NY + y) * NC + c) * ROWS, ROWS)
                        taking.append(copies.start(source, rows.at[to, columns]))
        for copy in taking:
            copy.wait()
        for t in range(tiles):
            loads[t].wait()
            here = pl.ds(t * depth, depth)
            for m in range(2):
                some = pl.ds(m * half, half)
                product = jnp.dot(
                    rows[some, here], held[t % slots], preferred_element_type=jnp.float32
                )
                if t == 0:
                    out[some, :] = product if total_ref is None else total_ref[some, :] + product
                else:
                    out[some, :] += product
            if t + slots < tiles:
                loads.append(load(t + slots))
        if last:
            for z in range(NZ):
                for y in range(NY):
                    for c in range(NC):
                        to = row_block(place_ref, (z, y)) * NC + lax.bitwise_xor(place_ref[2], c)
                        to = pl.ds(pl.multiple_of(to * ROWS, ROWS), ROWS)
                        here = pl.ds(((z * NY + y) * NC + c) * ROWS, ROWS)
                        note = rows[here, pl.ds(stream.features, NOTE)].astype(jnp.float32)
                        scale = jnp.sum(note, axis=1, keepdims=True)
                        result[to, :] = bf16(out[here, :] * scale)

    dtype = jnp.bfloat16 if last else jnp.float32
    scratch = [
        pltpu.VMEM((2 * half, stream.features + stream.note), jnp.bfloat16),
        pltpu.VMEM((slots, depth, COLS), jnp.bfloat16),
    ]
    if last:
        scratch.append(pltpu.VMEM((2 * half, COLS), jnp.float32))
    return pl.pallas_call(
        kernel,
        in_specs=[SMEM] + [ANY] * 10 + [HBM] + [VMEM] * len(more) + [ANY] * len(after),
        name="multiply",
        out_specs=VMEM,
        out_shape=shape(2 * half, COLS, dtype=dtype),
        scratch_shapes=scratch + [pltpu.SemaphoreType.DMA((48 + tiles,))],
        compiler_params=pltpu.CompilerParams(vmem_limit_bytes=VMEM_BYTES),
        cost_estimate=pl.CostEstimate(flops=0, bytes_accessed=1024, transcendentals=0),
    )(place, *ins, weight, *more, *after)


ORDERS = (("a", "b", "z"), ("b", "z", "a"), ("z", "a", "b"))


def stream_of(start, sizes, note):
    parts = []
    for i, (size, dims) in enumerate(zip(sizes, ORDERS)):
        parts.append(Part(start, size, dims, note if i == len(sizes) - 1 else 0))
        start += size
    return Stream(*parts)


FIRST = stream_of(0, (3072, 3072, 3072), 0)
SECOND = stream_of(9216, (2304, 2304, 2560), NOTE)


def per_device(partials, residual, norm_gain, qkv_weight):
    t = lax.axis_index("tensor")
    core, y, z = t % 2, (t // 2) % 4, t // 8
    place = jnp.stack([z, y, core]).astype(jnp.int32)
    terms = partials.reshape(NZ * NY * NC, ROWS, D)
    gain = norm_gain.astype(jnp.float32).reshape(1, D)

    def along(step, arrays):
        return [send(x, TO[ORDERS[k][step]]) for k, x in enumerate(arrays)]

    def across(arrays):
        return [send(x, TO_CORE) for x in arrays]

    a, b = FIRST, SECOND
    a_give = give(place, terms, [(a, 1)], [])
    a_got = across(a_give)[0]
    give_rest = give(place, terms, [(a, 0), (b, 0), (b, 1)], [a_give[0]])
    give_rest, _ = lax.optimization_barrier((give_rest[0], a_got))
    rest = send(give_rest, TO_CORE)
    a_out = first_step(place, terms, a_got, 0, a, [give_rest])
    a_one = along(0, a_out)
    b_out = first_step(place, terms, rest, D - b.start, b, [a_out[0]])
    b_one = along(0, b_out)
    a_out = second_step(place, terms, rest, a_one, a, [b_out[0]])
    a_two = along(1, a_out)
    b_out = second_step(place, terms, rest, b_one, b, [a_out[0]])
    b_two = along(1, b_out)
    a_out = third_step(place, terms, rest, a_one, a_two, a, [b_out[0]])
    a_three = along(2, a_out)
    b_out = third_step(place, terms, rest, b_one, b_two, b, [a_out[0]])
    b_three = along(2, b_out)
    a_rows, so_far = finish(
        place, terms, rest, a_one, a_two, a_three, a, residual, gain, (), [b_out[0]]
    )
    a_far = along(2, a_rows)
    b_rows, (stream, _) = finish(
        place, terms, rest, b_one, b_two, b_three, b, residual, gain, so_far, []
    )
    b_far = along(2, b_rows)
    a_near = two_blocks(place, a_rows, a_far, a, [b_rows[0]])
    a_far = along(1, a_near)
    b_near = two_blocks(place, b_rows, b_far, b, [a_near[0]])
    b_far = along(1, b_near)
    a_near, a_beside = four_blocks(place, a_near, a_far, a, [b_near[0]])
    a_far = along(0, a_near)
    a_beside = send(a_beside, TO_CORE)
    b_near, b_beside = four_blocks(place, b_near, b_far, b, [a_near[0]])
    b_far = along(0, b_near)
    b_beside = send(b_beside, TO_CORE)

    a_all = (a_near, a_far, a_beside, across(a_far))
    total = multiplied(place, *a_all, qkv_weight, None, a, 1536, [b_near[0]])
    b_all = (b_near, b_far, b_beside, across(b_far))
    return stream, multiplied(place, *b_all, qkv_weight, total, b, 1792, [])


def solution(mesh):
    in_specs = (P("tensor", "dp", None), P(("dp", "tensor"), None), P(), P(None, "tensor"))
    out_specs = (P(("dp", "tensor"), None), P("dp", "tensor"))
    return jax.shard_map(
        per_device, mesh=mesh, in_specs=in_specs, out_specs=out_specs, check_vma=False
    )
```

time: 234 us -> 193 us (0.82)
  waiting for transfers between devices: 196 us -> 37.7 us
  Pallas kernels: 0 us -> 75.2 us
  starting transfers between devices: 0.08 us -> 74.9 us
  matrix products: 20.6 us -> 0 us
  between operations: 14.1 us -> 1.08 us
  local copies, waits for them, and re-layouts: 0.03 us -> 3.54 us
  other arithmetic: 3.51 us -> 0.08 us
    reduce_scatter x1 -> x0, waiting for transfers between devices: 102 us -> none  [per_device(): lax.psum_scatter(partial_term.astype(jnp.bfloat16), 'tensor', scatter_dim...]
    all_gather x1 -> x0, waiting for transfers between devices: 92.4 us -> none  [per_device(): lax.all_gather(normed, 'tensor', axis=0, tiled=True)]
    pallas_call x0 -> x16, Pallas kernels: none -> 75.2 us  [the longest x14 49.3 us: call(): pl.pallas_call(kernel, in_specs=[SMEM] + [HBM if i in pinned else ANY for...]
    ppermute x0 -> x46, starting transfers between devices: none -> 74.9 us  [send(): return lax.ppermute(x, 'tensor', where)]
    ppermute x0 -> x46, waiting for transfers between devices: none -> 37.7 us  [send(): return lax.ppermute(x, 'tensor', where)]
    dot_general x1 -> x0, matrix products: 20.6 us -> none  [per_device(): jnp.dot(lax.all_gather(normed, 'tensor', axis=0, tiled=True), qkv_weight,...]
    unnamed x6 -> x12, local copies, waits for them, and re-layouts: 0.03 us -> 3.54 us
  transfers between devices with their start and end apart: 2 -> 46, of which waited for: 2 -> 18; matrix products, arithmetic and copies ran while one was open for 0% -> 0% of each run, Pallas kernels for 0% -> 29%
where the time goes in v1:
time: 193 us; the launch traced here: 192 us
  Pallas kernels  75.2 us (39%)
  starting transfers between devices  74.9 us (39%)
  waiting for transfers between devices  37.7 us (20%)
  local copies, waits for them, and re-layouts  3.54 us (2%)
    ppermute x46, starting transfers between devices, send(): return lax.ppermute(x, 'tensor', where)  74.9 us
    pallas_call x14, Pallas kernels, call(): pl.pallas_call(kernel, in_specs=[SMEM] + [HBM if i in pinned else ANY for...  49.3 us
    ppermute x46, waiting for transfers between devices, send(): return lax.ppermute(x, 'tensor', where)  37.7 us
    pallas_call x2, Pallas kernels, multiplied(): pl.pallas_call(kernel, in_specs=[SMEM] + [ANY] * 10 + [HBM] + [VMEM] * le...  25.9 us
  transfers between devices with their start and end apart: 46, of which 18 were waited for; matrix products, arithmetic and copies ran while one was open for 0% of the time, Pallas kernels for 29%

profile of v1, /device:TPU:1, one launch (start us, length us, event | category | flops | bytes accessed | tf_op | source)
XLA Modules:
  0.0 192.5 jit_solution(841369824455078837)
XLA Ops:
  0.7 2.6 %give.2.refs_2_ = bf16[4,32,9216]{2,1,0:T(8,128)(2,1)S(1)} custom-call(s32[3]{0:T(128)S(1)} %pad_add_fusion.refs_0_.place_ref, bf16[16,32,16384]{2,1,0:T(8,128)(2,1)} %bitcast.7), custom_call_target="tpu_custom_call" | custom-call | bytes 1024 | tf_op jit(solution)/shard_map/give/pallas_call | solution.py:82
  4.8 6.2 %give.3.refs_3_ = bf16[4,32,23552]{2,1,0:T(8,128)(2,1)} custom-call(s32[3]{0:T(128)S(1)} %pad_add_fusion.refs_0_.place_ref, bf16[16,32,16384]{2,1,0:T(8,128)(2,1)} %bitcast.8, bf16[4,32,9216]{2,1,0:T(8,128)(2,1)S(1)} %give.2.refs_2_), custom_call_target="tpu_custom_call" | custom-call | bytes 1024 | tf_op jit(solution)/shard_map/give/pallas_call | solution.py:82
  11.1 5.9 %first.2 = (bf16[4,32,3072]{2,1,0:T(8,128)(2,1)S(1)}, bf16[4,32,3072]{2,1,0:T(8,128)(2,1)S(1)}, bf16[4,32,3072]{2,1,0:T(8,128)(2,1)S(1)}) custom-call(s32[3]{0:T(128)S(1)} %pad_add_fusion.refs_0_.place_ref, bf16[16,32,16384]{2,1,0:T(8,128)(2,1)} %bitcast.9, bf16[4,32,9216]{2,1,0:T(8,128)(2,1)S(1)} %collective-permute-done.refs_2_, ...), custom_call_target="tpu_custom_call" | custom-call | bytes 1024 | tf_op jit(solution)/shard_map/first/pallas_call | solution.py:82
  18.4 1.9 collective-permute-start.6
  22.0 3.8 %first.3 = (bf16[4,32,2304]{2,1,0:T(8,128)(2,1)S(1)}, bf16[4,32,2304]{2,1,0:T(8,128)(2,1)S(1)}, bf16[4,32,2560]{2,1,0:T(8,128)(2,1)S(1)}) custom-call(s32[3]{0:T(128)S(1)} %pad_add_fusion.refs_0_.place_ref, bf16[16,32,16384]{2,1,0:T(8,128)(2,1)} %bitcast.10, bf16[4,32,23552]{2,1,0:T(8,128)(2,1)} %collective-permute-done.1.refs_2_, ...), custom_call_target="tpu_custom_call" | custom-call | bytes 1024 | tf_op jit(solution)/shard_map/first/pallas_call | solution.py:82
  28.1 7.6 %collective-permute-done.5.refs_3_ = bf16[4,32,3072]{2,1,0:T(8,128)(2,1)S(1)} collective-permute-done((bf16[4,32,3072]{2,1,0:T(8,128)(2,1)S(1)}, bf16[4,32,3072]{2,1,0:T(8,128)(2,1)S(1)}, u32[]{:S(2)}, u32[]{:S(2)}) %collective-permute-start.5) | collective-permute-done | bytes 786464 | tf_op jit(solution)/shard_map/ppermute | solution.py:42
  35.7 2.8 %collective-permute-start.3 = (bf16[4,32,2304]{2,1,0:T(8,128)(2,1)S(1)}, bf16[4,32,2304]{2,1,0:T(8,128)(2,1)S(1)}, u32[]{:S(2)}, u32[]{:S(2)}) collective-permute-start(bf16[4,32,2304]{2,1,0:T(8,128)(2,1)S(1)} %get-tuple-element.47), channel_id=1, source_target_pairs={{0,6},{1,7},{2,4},{3,5},{4,2},{5,3},{6,0},{7,1},{8,14},{9,15},{10,... | collective-permute-start | bytes 1769480 | tf_op jit(solution)/shard_map/ppermute | solution.py:42
  38.7 4.6 %second.2 = (bf16[2,32,3072]{2,1,0:T(8,128)(2,1)S(1)}, bf16[2,32,3072]{2,1,0:T(8,128)(2,1)S(1)}, bf16[2,32,3072]{2,1,0:T(8,128)(2,1)S(1)}) custom-call(s32[3]{0:T(128)S(1)} %pad_add_fusion.refs_0_.place_ref, bf16[16,32,16384]{2,1,0:T(8,128)(2,1)} %bitcast.11, bf16[4,32,23552]{2,1,0:T(8,128)(2,1)} %collective-permute-done.1.refs_2_, ...), custom_call_target="tpu_custom_call" | custom-call | bytes 1024 | tf_op jit(solution)/shard_map/second/pallas_call | solution.py:82
  46.1 2.2 %collective-permute-done.2.refs_3_ = bf16[4,32,2304]{2,1,0:T(8,128)(2,1)S(1)} collective-permute-done((bf16[4,32,2304]{2,1,0:T(8,128)(2,1)S(1)}, bf16[4,32,2304]{2,1,0:T(8,128)(2,1)S(1)}, u32[]{:S(2)}, u32[]{:S(2)}) %collective-permute-start.2) | collective-permute-done | bytes 589856 | tf_op jit(solution)/shard_map/ppermute | solution.py:42
  49.7 3.0 %collective-permute-done.4.refs_5_ = bf16[4,32,2560]{2,1,0:T(8,128)(2,1)S(1)} collective-permute-done((bf16[4,32,2560]{2,1,0:T(8,128)(2,1)S(1)}, bf16[4,32,2560]{2,1,0:T(8,128)(2,1)S(1)}, u32[]{:S(2)}, u32[]{:S(2)}) %collective-permute-start.4) | collective-permute-done | bytes 655392 | tf_op jit(solution)/shard_map/ppermute | solution.py:42
  52.7 2.8 %second.3 = (bf16[2,32,2304]{2,1,0:T(8,128)(2,1)S(1)}, bf16[2,32,2304]{2,1,0:T(8,128)(2,1)S(1)}, bf16[2,32,2560]{2,1,0:T(8,128)(2,1)S(1)}) custom-call(s32[3]{0:T(128)S(1)} %pad_add_fusion.refs_0_.place_ref, bf16[16,32,16384]{2,1,0:T(8,128)(2,1)} %bitcast.12, bf16[4,32,23552]{2,1,0:T(8,128)(2,1)} %collective-permute-done.1.refs_2_, ...), custom_call_target="tpu_custom_call" | custom-call | bytes 1024 | tf_op jit(solution)/shard_map/second/pallas_call | solution.py:82
  61.1 3.6 %third.2 = (bf16[32,3072]{1,0:T(8,128)(2,1)S(1)}, bf16[32,3072]{1,0:T(8,128)(2,1)S(1)}, bf16[32,3072]{1,0:T(8,128)(2,1)S(1)}) custom-call(s32[3]{0:T(128)S(1)} %pad_add_fusion.refs_0_.place_ref, bf16[16,32,16384]{2,1,0:T(8,128)(2,1)} %bitcast.13, bf16[4,32,23552]{2,1,0:T(8,128)(2,1)} %collective-permute-done.1.refs_2_, ...), custom_call_target="tpu_custom_call" | custom-call | bytes 1024 | tf_op jit(solution)/shard_map/third/pallas_call | solution.py:82
  67.4 2.3 %third.3 = (bf16[32,2304]{1,0:T(8,128)(2,1)S(1)}, bf16[32,2304]{1,0:T(8,128)(2,1)S(1)}, bf16[32,2560]{1,0:T(8,128)(2,1)S(1)}) custom-call(s32[3]{0:T(128)S(1)} %pad_add_fusion.refs_0_.place_ref, bf16[16,32,16384]{2,1,0:T(8,128)(2,1)} %bitcast.14, bf16[4,32,23552]{2,1,0:T(8,128)(2,1)} %collective-permute-done.1.refs_2_, ...), custom_call_target="tpu_custom_call" | custom-call | bytes 1024 | tf_op jit(solution)/shard_map/third/pallas_call | solution.py:82
  72.2 4.9 %finish.2 = (bf16[32,16384]{1,0:T(8,128)(2,1)}, bf16[32,3072]{1,0:T(8,128)(2,1)S(1)}, bf16[32,3072]{1,0:T(8,128)(2,1)S(1)}, bf16[32,3072]{1,0:T(8,128)(2,1)S(1)}, f32[32,128]{1,0:T(8,128)S(1)}) custom-call(s32[3]{0:T(128)S(1)} %pad_add_fusion.refs_0_.place_ref, bf16[16,32,16384]{2,1,0:T(8,128)(2,1)} %bitcast.15, ...), custom_call_target="tpu_custom_call" | custom-call | bytes 1024 | tf_op jit(solution)/shard_map/finish/pallas_call | solution.py:82
  81.1 4.0 %collective-permute-done.15.refs_10_ = bf16[32,2304]{1,0:T(8,128)(2,1)S(1)} collective-permute-done((bf16[32,2304]{1,0:T(8,128)(2,1)S(1)}, bf16[32,2304]{1,0:T(8,128)(2,1)S(1)}, u32[]{:S(2)}, u32[]{:S(2)}) %collective-permute-start.15) | collective-permute-done | bytes 147488 | tf_op jit(solution)/shard_map/ppermute | solution.py:42
  85.9 3.2 %finish.3 = (bf16[32,16384]{1,0:T(8,128)(2,1)}, bf16[32,2304]{1,0:T(8,128)(2,1)S(1)}, bf16[32,2304]{1,0:T(8,128)(2,1)S(1)}, bf16[32,2688]{1,0:T(8,128)(2,1)S(1)}, f32[32,128]{1,0:T(8,128)}) custom-call(s32[3]{0:T(128)S(1)} %pad_add_fusion.refs_0_.place_ref, bf16[16,32,16384]{2,1,0:T(8,128)(2,1)} %bitcast.16, ...), custom_call_target="tpu_custom_call", output_to_operand_aliasing={{0}: (14, {})} | custom-call | bytes 1024 | tf_op jit(solution)/shard_map/finish/pallas_call | solution.py:82
  89.1 2.4 %two.2 = (bf16[2,32,3072]{2,1,0:T(8,128)(2,1)S(1)}, bf16[2,32,3072]{2,1,0:T(8,128)(2,1)S(1)}, bf16[2,32,3072]{2,1,0:T(8,128)(2,1)S(1)}) custom-call(s32[3]{0:T(128)S(1)} %pad_add_fusion.refs_0_.place_ref, bf16[32,3072]{1,0:T(8,128)(2,1)S(1)} %get-tuple-element.69.refs_1_, bf16[32,3072]{1,0:T(8,128)(2,1)S(1)} %get-tuple-element.70.refs_2_, ...), custom_call_target="tpu_custom_call" | custom-call | bytes 1024 | tf_op jit(solution)/shard_map/two/pallas_call | solution.py:82
  92.8 1.9 collective-permute-start.22
  98.7 2.6 %collective-permute-done.22.refs_6_ = bf16[32,2688]{1,0:T(8,128)(2,1)S(1)} collective-permute-done((bf16[32,2688]{1,0:T(8,128)(2,1)S(1)}, bf16[32,2688]{1,0:T(8,128)(2,1)S(1)}, u32[]{:S(2)}, u32[]{:S(2)}) %collective-permute-start.22) | collective-permute-done | bytes 172064 | tf_op jit(solution)/shard_map/ppermute | solution.py:42
  101.3 2.1 %two.3 = (bf16[2,32,2304]{2,1,0:T(8,128)(2,1)S(1)}, bf16[2,32,2304]{2,1,0:T(8,128)(2,1)S(1)}, bf16[2,32,2688]{2,1,0:T(8,128)(2,1)S(1)}) custom-call(s32[3]{0:T(128)S(1)} %pad_add_fusion.refs_0_.place_ref, bf16[32,2304]{1,0:T(8,128)(2,1)S(1)} %get-tuple-element.66.refs_7_.refs_1_, bf16[32,2304]{1,0:T(8,128)(2,1)S(1)} %get-tuple-element.67.refs_2_, ...), custom_call_target="tpu_custom_call" | custom-call | bytes 1024 | tf_op jit(solution)/shard_map/two/pallas_call | solution.py:82
  104.8 2.8 %four.2 = (bf16[4,32,3072]{2,1,0:T(8,128)(2,1)S(1)}, bf16[4,32,3072]{2,1,0:T(8,128)(2,1)S(1)}, bf16[4,32,3072]{2,1,0:T(8,128)(2,1)S(1)}, bf16[4,32,9216]{2,1,0:T(8,128)(2,1)}) custom-call(s32[3]{0:T(128)S(1)} %pad_add_fusion.refs_0_.place_ref, bf16[2,32,3072]{2,1,0:T(8,128)(2,1)S(1)} %get-tuple-element.72.refs_7_.refs_1_, ...), custom_call_target="tpu_custom_call" | custom-call | bytes 1024 | tf_op jit(solution)/shard_map/four/pallas_call | solution.py:82
  107.6 5.3 %collective-permute-done.26.refs_4_ = bf16[2,32,2304]{2,1,0:T(8,128)(2,1)S(1)} collective-permute-done((bf16[2,32,2304]{2,1,0:T(8,128)(2,1)S(1)}, bf16[2,32,2304]{2,1,0:T(8,128)(2,1)S(1)}, u32[]{:S(2)}, u32[]{:S(2)}) %collective-permute-start.26) | collective-permute-done | bytes 294944 | tf_op jit(solution)/shard_map/ppermute | solution.py:42
  113.6 2.2 %four.3 = (bf16[4,32,2304]{2,1,0:T(8,128)(2,1)S(1)}, bf16[4,32,2304]{2,1,0:T(8,128)(2,1)S(1)}, bf16[4,32,2688]{2,1,0:T(8,128)(2,1)S(1)}, bf16[4,32,7296]{2,1,0:T(8,128)(2,1)}) custom-call(s32[3]{0:T(128)S(1)} %pad_add_fusion.refs_0_.place_ref, bf16[2,32,2304]{2,1,0:T(8,128)(2,1)S(1)} %get-tuple-element.73.refs_7_.refs_1_, ...), custom_call_target="tpu_custom_call" | custom-call | bytes 1024 | tf_op jit(solution)/shard_map/four/pallas_call | solution.py:82
  118.3 13.7 %collective-permute-start.42 = (bf16[4,32,9216]{2,1,0:T(8,128)(2,1)}, bf16[4,32,9216]{2,1,0:T(8,128)(2,1)S(1)}, u32[]{:S(2)}, u32[]{:S(2)}) collective-permute-start(bf16[4,32,9216]{2,1,0:T(8,128)(2,1)} %get-tuple-element.85), channel_id=1, source_target_pairs={{0,1},{1,0},{2,3},{3,2},{4,5},{5,4},{6,7},{7,6},{8,9},{9,8},{10,11... | collective-permute-start | bytes 7077896 | tf_op jit(solution)/shard_map/ppermute | solution.py:42
  132.2 2.2 %collective-permute-start.40 = (bf16[4,32,3072]{2,1,0:T(8,128)(2,1)S(1)}, bf16[4,32,3072]{2,1,0:T(8,128)(2,1)S(1)}, u32[]{:S(2)}, u32[]{:S(2)}) collective-permute-start(bf16[4,32,3072]{2,1,0:T(8,128)(2,1)S(1)} %get-tuple-element.83.refs_1_), channel_id=1, source_target_pairs={{0,6},{1,7},{2,4},{3,5},{4,2},{5,3},{6,0},{7,1},{8,14},{9,15},{10,... | collective-permute-start | bytes 2359304 | tf_op jit(solution)/shard_map/ppermute | solution.py:42
  134.4 1.7 collective-permute-start.41
  136.1 12.4 %collective-permute-start.35 = (bf16[4,32,7296]{2,1,0:T(8,128)(2,1)}, bf16[4,32,7296]{2,1,0:T(8,128)(2,1)S(1)}, u32[]{:S(2)}, u32[]{:S(2)}) collective-permute-start(bf16[4,32,7296]{2,1,0:T(8,128)(2,1)} %get-tuple-element.82), channel_id=1, source_target_pairs={{0,1},{1,0},{2,3},{3,2},{4,5},{5,4},{6,7},{7,6},{8,9},{9,8},{10,11... | collective-permute-start | bytes 5603336 | tf_op jit(solution)/shard_map/ppermute | solution.py:42
  148.5 3.1 %collective-permute-done.39.refs_3_ = bf16[4,32,3072]{2,1,0:T(8,128)(2,1)S(1)} collective-permute-done((bf16[4,32,3072]{2,1,0:T(8,128)(2,1)S(1)}, bf16[4,32,3072]{2,1,0:T(8,128)(2,1)S(1)}, u32[]{:S(2)}, u32[]{:S(2)}) %collective-permute-start.39) | collective-permute-done | bytes 786464 | tf_op jit(solution)/shard_map/ppermute | solution.py:42
  151.6 5.2 %collective-permute-start.43 = (bf16[4,32,3072]{2,1,0:T(8,128)(2,1)S(1)}, bf16[4,32,3072]{2,1,0:T(8,128)(2,1)S(1)}, u32[]{:S(2)}, u32[]{:S(2)}) collective-permute-start(bf16[4,32,3072]{2,1,0:T(8,128)(2,1)S(1)} %collective-permute-done.39.refs_3_), channel_id=1, source_target_pairs={{0,1},{1,0},{2,3},{3,2},{4,5},{5,4},{6,7},{7,6},{8,9},{9,8},{10,11... | collective-permute-start | bytes 2359304 | tf_op jit(solution)/shard_map/ppermute | solution.py:42
  156.8 2.5 %collective-permute-start.44 = (bf16[4,32,3072]{2,1,0:T(8,128)(2,1)S(1)}, bf16[4,32,3072]{2,1,0:T(8,128)(2,1)S(1)}, u32[]{:S(2)}, u32[]{:S(2)}) collective-permute-start(bf16[4,32,3072]{2,1,0:T(8,128)(2,1)S(1)} %collective-permute-done.40.refs_4_), channel_id=1, source_target_pairs={{0,1},{1,0},{2,3},{3,2},{4,5},{5,4},{6,7},{7,6},{8,9},{9,8},{10,11... | collective-permute-start | bytes 2359304 | tf_op jit(solution)/shard_map/ppermute | solution.py:42
  165.1 13.9 %multiply.2.refs_11_ = f32[512,640]{1,0:T(8,128)} custom-call(s32[3]{0:T(128)S(1)} %pad_add_fusion.refs_0_.place_ref, bf16[4,32,3072]{2,1,0:T(8,128)(2,1)S(1)} %get-tuple-element.78.refs_7_.refs_0_, bf16[4,32,3072]{2,1,0:T(8,128)(2,1)S(1)} %get-tuple-element.83.refs_1_, bf16[4,32,3072]{2,1,0:T(8,128)(2,1)S(1)} %get-tuple-element.84.refs_2_, ...), custom_call_target="tpu_custom_call" | custom-call | bytes 1024 | tf_op jit(solution)/shard_map/multiply/pallas_call | solution.py:460
  180.2 12.1 %multiply.3 = bf16[512,640]{1,0:T(8,128)(2,1)} custom-call(s32[3]{0:T(128)S(1)} %pad_add_fusion.refs_0_.place_ref, bf16[4,32,2304]{2,1,0:T(8,128)(2,1)S(1)} %get-tuple-element.79.refs_11_.refs_0_, bf16[4,32,2304]{2,1,0:T(8,128)(2,1)S(1)} %get-tuple-element.80.refs_1_, bf16[4,32,2688]{2,1,0:T(8,128)(2,1)S(1)} %get-tuple-element.81.refs_2_, ...), custom_call_target="tpu_custom_call" | custom-call | bytes 1024 | tf_op jit(solution)/shard_map/multiply/pallas_call | solution.py:460
  (90 shorter events, 44.2 us)
Async XLA Ops:
  11.0 11.0 %collective-permute-start.1 = (bf16[4,32,23552]{2,1,0:T(8,128)(2,1)}, bf16[4,32,23552]{2,1,0:T(8,128)(2,1)}, u32[]{:S(2)}, u32[]{:S(2)}) collective-permute-start(bf16[4,32,23552]{2,1,0:T(8,128)(2,1)} %give.3.refs_3_), channel_id=1, source_target_pairs={{0,1},{1,0},{2,3},{3,2},{4,5},{5,4},{6,7},{7,6},{8,9},{9,8},{10,11... | collective-permute-start | bytes 18087944 | tf_op jit(solution)/shard_map/ppermute | solution.py:42
  17.0 18.7 %collective-permute-start.5 = (bf16[4,32,3072]{2,1,0:T(8,128)(2,1)S(1)}, bf16[4,32,3072]{2,1,0:T(8,128)(2,1)S(1)}, u32[]{:S(2)}, u32[]{:S(2)}) collective-permute-start(bf16[4,32,3072]{2,1,0:T(8,128)(2,1)S(1)} %get-tuple-element.45.refs_3_), channel_id=1, source_target_pairs={{0,2},{1,3},{2,0},{3,1},{4,6},{5,7},{6,4},{7,5},{8,10},{9,11},{10,... | collective-permute-start | bytes 2359304 | tf_op jit(solution)/shard_map/ppermute | solution.py:42
  18.4 20.1 %collective-permute-start.6 = (bf16[4,32,3072]{2,1,0:T(8,128)(2,1)S(1)}, bf16[4,32,3072]{2,1,0:T(8,128)(2,1)S(1)}, u32[]{:S(2)}, u32[]{:S(2)}) collective-permute-start(bf16[4,32,3072]{2,1,0:T(8,128)(2,1)S(1)} %get-tuple-element.49), channel_id=1, source_target_pairs={{0,6},{1,7},{2,4},{3,5},{4,2},{5,3},{6,0},{7,1},{8,14},{9,15},{10,... | collective-permute-start | bytes 2359304 | tf_op jit(solution)/shard_map/ppermute | solution.py:42
  20.3 18.4 %collective-permute-start.7 = (bf16[4,32,3072]{2,1,0:T(8,128)(2,1)S(1)}, bf16[4,32,3072]{2,1,0:T(8,128)(2,1)S(1)}, u32[]{:S(2)}, u32[]{:S(2)}) collective-permute-start(bf16[4,32,3072]{2,1,0:T(8,128)(2,1)S(1)} %get-tuple-element.50), channel_id=1, source_target_pairs={{0,8},{1,9},{2,10},{3,11},{4,12},{5,13},{6,14},{7,15},{8,0},{9,1},... | collective-permute-start | bytes 2359304 | tf_op jit(solution)/shard_map/ppermute | solution.py:42
  25.8 22.5 %collective-permute-start.2 = (bf16[4,32,2304]{2,1,0:T(8,128)(2,1)S(1)}, bf16[4,32,2304]{2,1,0:T(8,128)(2,1)S(1)}, u32[]{:S(2)}, u32[]{:S(2)}) collective-permute-start(bf16[4,32,2304]{2,1,0:T(8,128)(2,1)S(1)} %get-tuple-element.46.refs_6_), channel_id=1, source_target_pairs={{0,2},{1,3},{2,0},{3,1},{4,6},{5,7},{6,4},{7,5},{8,10},{9,11},{10,... | collective-permute-start | bytes 1769480 | tf_op jit(solution)/shard_map/ppermute | solution.py:42
  26.5 26.3 %collective-permute-start.4 = (bf16[4,32,2560]{2,1,0:T(8,128)(2,1)S(1)}, bf16[4,32,2560]{2,1,0:T(8,128)(2,1)S(1)}, u32[]{:S(2)}, u32[]{:S(2)}) collective-permute-start(bf16[4,32,2560]{2,1,0:T(8,128)(2,1)S(1)} %get-tuple-element.48), channel_id=1, source_target_pairs={{0,8},{1,9},{2,10},{3,11},{4,12},{5,13},{6,14},{7,15},{8,0},{9,1},... | collective-permute-start | bytes 1966088 | tf_op jit(solution)/shard_map/ppermute | solution.py:42
  35.7 14.0 %collective-permute-start.3 = (bf16[4,32,2304]{2,1,0:T(8,128)(2,1)S(1)}, bf16[4,32,2304]{2,1,0:T(8,128)(2,1)S(1)}, u32[]{:S(2)}, u32[]{:S(2)}) collective-permute-start(bf16[4,32,2304]{2,1,0:T(8,128)(2,1)S(1)} %get-tuple-element.47), channel_id=1, source_target_pairs={{0,6},{1,7},{2,4},{3,5},{4,2},{5,3},{6,0},{7,1},{8,14},{9,15},{10,... | collective-permute-start | bytes 1769480 | tf_op jit(solution)/shard_map/ppermute | solution.py:42
  43.3 14.9 %collective-permute-start.11 = (bf16[2,32,3072]{2,1,0:T(8,128)(2,1)S(1)}, bf16[2,32,3072]{2,1,0:T(8,128)(2,1)S(1)}, u32[]{:S(2)}, u32[]{:S(2)}) collective-permute-start(bf16[2,32,3072]{2,1,0:T(8,128)(2,1)S(1)} %get-tuple-element.51.refs_6_), channel_id=1, source_target_pairs={{0,6},{1,7},{2,4},{3,5},{4,2},{5,3},{6,0},{7,1},{8,14},{9,15},{10,... | collective-permute-start | bytes 1179656 | tf_op jit(solution)/shard_map/ppermute | solution.py:42
  44.5 16.6 %collective-permute-start.12 = (bf16[2,32,3072]{2,1,0:T(8,128)(2,1)S(1)}, bf16[2,32,3072]{2,1,0:T(8,128)(2,1)S(1)}, u32[]{:S(2)}, u32[]{:S(2)}) collective-permute-start(bf16[2,32,3072]{2,1,0:T(8,128)(2,1)S(1)} %get-tuple-element.55), channel_id=1, source_target_pairs={{0,8},{1,9},{2,10},{3,11},{4,12},{5,13},{6,14},{7,15},{8,0},{9,1},... | collective-permute-start | bytes 1179656 | tf_op jit(solution)/shard_map/ppermute | solution.py:42
  48.3 12.9 %collective-permute-start.13 = (bf16[2,32,3072]{2,1,0:T(8,128)(2,1)S(1)}, bf16[2,32,3072]{2,1,0:T(8,128)(2,1)S(1)}, u32[]{:S(2)}, u32[]{:S(2)}) collective-permute-start(bf16[2,32,3072]{2,1,0:T(8,128)(2,1)S(1)} %get-tuple-element.56), channel_id=1, source_target_pairs={{0,2},{1,3},{2,0},{3,1},{4,6},{5,7},{6,4},{7,5},{8,10},{9,11},{10,... | collective-permute-start | bytes 1179656 | tf_op jit(solution)/shard_map/ppermute | solution.py:42
  55.6 10.9 %collective-permute-start.8 = (bf16[2,32,2304]{2,1,0:T(8,128)(2,1)S(1)}, bf16[2,32,2304]{2,1,0:T(8,128)(2,1)S(1)}, u32[]{:S(2)}, u32[]{:S(2)}) collective-permute-start(bf16[2,32,2304]{2,1,0:T(8,128)(2,1)S(1)} %get-tuple-element.52.refs_9_), channel_id=1, source_target_pairs={{0,6},{1,7},{2,4},{3,5},{4,2},{5,3},{6,0},{7,1},{8,14},{9,15},{10,... | collective-permute-start | bytes 884744 | tf_op jit(solution)/shard_map/ppermute | solution.py:42
  56.4 11.0 %collective-permute-start.10 = (bf16[2,32,2560]{2,1,0:T(8,128)(2,1)S(1)}, bf16[2,32,2560]{2,1,0:T(8,128)(2,1)S(1)}, u32[]{:S(2)}, u32[]{:S(2)}) collective-permute-start(bf16[2,32,2560]{2,1,0:T(8,128)(2,1)S(1)} %get-tuple-element.54), channel_id=1, source_target_pairs={{0,2},{1,3},{2,0},{3,1},{4,6},{5,7},{6,4},{7,5},{8,10},{9,11},{10,... | collective-permute-start | bytes 983048 | tf_op jit(solution)/shard_map/ppermute | solution.py:42
  58.1 9.3 %collective-permute-start.9 = (bf16[2,32,2304]{2,1,0:T(8,128)(2,1)S(1)}, bf16[2,32,2304]{2,1,0:T(8,128)(2,1)S(1)}, u32[]{:S(2)}, u32[]{:S(2)}) collective-permute-start(bf16[2,32,2304]{2,1,0:T(8,128)(2,1)S(1)} %get-tuple-element.53), channel_id=1, source_target_pairs={{0,8},{1,9},{2,10},{3,11},{4,12},{5,13},{6,14},{7,15},{8,0},{9,1},... | collective-permute-start | bytes 884744 | tf_op jit(solution)/shard_map/ppermute | solution.py:42
  69.7 11.3 %collective-permute-start.14 = (bf16[32,2304]{1,0:T(8,128)(2,1)S(1)}, bf16[32,2304]{1,0:T(8,128)(2,1)S(1)}, u32[]{:S(2)}, u32[]{:S(2)}) collective-permute-start(bf16[32,2304]{1,0:T(8,128)(2,1)S(1)} %get-tuple-element.58.refs_14_), channel_id=1, source_target_pairs={{0,8},{1,9},{2,10},{3,11},{4,12},{5,13},{6,14},{7,15},{8,0},{9,1},... | collective-permute-start | bytes 442376 | tf_op jit(solution)/shard_map/ppermute | solution.py:42
  77.1 12.0 %collective-permute-start.23 = (bf16[32,3072]{1,0:T(8,128)(2,1)S(1)}, bf16[32,3072]{1,0:T(8,128)(2,1)S(1)}, u32[]{:S(2)}, u32[]{:S(2)}) collective-permute-start(bf16[32,3072]{1,0:T(8,128)(2,1)S(1)} %get-tuple-element.69.refs_1_), channel_id=1, source_target_pairs={{0,8},{1,9},{2,10},{3,11},{4,12},{5,13},{6,14},{7,15},{8,0},{9,1},... | collective-permute-start | bytes 589832 | tf_op jit(solution)/shard_map/ppermute | solution.py:42
  78.0 11.2 %collective-permute-start.24 = (bf16[32,3072]{1,0:T(8,128)(2,1)S(1)}, bf16[32,3072]{1,0:T(8,128)(2,1)S(1)}, u32[]{:S(2)}, u32[]{:S(2)}) collective-permute-start(bf16[32,3072]{1,0:T(8,128)(2,1)S(1)} %get-tuple-element.70.refs_2_), channel_id=1, source_target_pairs={{0,2},{1,3},{2,0},{3,1},{4,6},{5,7},{6,4},{7,5},{8,10},{9,11},{10,... | collective-permute-start | bytes 589832 | tf_op jit(solution)/shard_map/ppermute | solution.py:42
  78.4 10.8 %collective-permute-start.25 = (bf16[32,3072]{1,0:T(8,128)(2,1)S(1)}, bf16[32,3072]{1,0:T(8,128)(2,1)S(1)}, u32[]{:S(2)}, u32[]{:S(2)}) collective-permute-start(bf16[32,3072]{1,0:T(8,128)(2,1)S(1)} %get-tuple-element.71.refs_3_), channel_id=1, source_target_pairs={{0,6},{1,7},{2,4},{3,5},{4,2},{5,3},{6,0},{7,1},{8,14},{9,15},{10,... | collective-permute-start | bytes 589832 | tf_op jit(solution)/shard_map/ppermute | solution.py:42
  91.5 13.0 %collective-permute-start.29 = (bf16[2,32,3072]{2,1,0:T(8,128)(2,1)S(1)}, bf16[2,32,3072]{2,1,0:T(8,128)(2,1)S(1)}, u32[]{:S(2)}, u32[]{:S(2)}) collective-permute-start(bf16[2,32,3072]{2,1,0:T(8,128)(2,1)S(1)} %get-tuple-element.72.refs_7_.refs_1_), channel_id=1, source_target_pairs={{0,6},{1,7},{2,4},{3,5},{4,2},{5,3},{6,0},{7,1},{8,14},{9,15},{10,... | collective-permute-start | bytes 1179656 | tf_op jit(solution)/shard_map/ppermute | solution.py:42
  94.8 10.0 %collective-permute-start.30 = (bf16[2,32,3072]{2,1,0:T(8,128)(2,1)S(1)}, bf16[2,32,3072]{2,1,0:T(8,128)(2,1)S(1)}, u32[]{:S(2)}, u32[]{:S(2)}) collective-permute-start(bf16[2,32,3072]{2,1,0:T(8,128)(2,1)S(1)} %get-tuple-element.76.refs_2_), channel_id=1, source_target_pairs={{0,8},{1,9},{2,10},{3,11},{4,12},{5,13},{6,14},{7,15},{8,0},{9,1},... | collective-permute-start | bytes 1179656 | tf_op jit(solution)/shard_map/ppermute | solution.py:42
  103.4 10.2 %collective-permute-start.28 = (bf16[2,32,2688]{2,1,0:T(8,128)(2,1)S(1)}, bf16[2,32,2688]{2,1,0:T(8,128)(2,1)S(1)}, u32[]{:S(2)}, u32[]{:S(2)}) collective-permute-start(bf16[2,32,2688]{2,1,0:T(8,128)(2,1)S(1)} %get-tuple-element.75.refs_3_), channel_id=1, source_target_pairs={{0,2},{1,3},{2,0},{3,1},{4,6},{5,7},{6,4},{7,5},{8,10},{9,11},{10,... | collective-permute-start | bytes 1032200 | tf_op jit(solution)/shard_map/ppermute | solution.py:42
  103.5 9.4 %collective-permute-start.26 = (bf16[2,32,2304]{2,1,0:T(8,128)(2,1)S(1)}, bf16[2,32,2304]{2,1,0:T(8,128)(2,1)S(1)}, u32[]{:S(2)}, u32[]{:S(2)}) collective-permute-start(bf16[2,32,2304]{2,1,0:T(8,128)(2,1)S(1)} %get-tuple-element.73.refs_7_.refs_1_), channel_id=1, source_target_pairs={{0,6},{1,7},{2,4},{3,5},{4,2},{5,3},{6,0},{7,1},{8,14},{9,15},{10,... | collective-permute-start | bytes 884744 | tf_op jit(solution)/shard_map/ppermute | solution.py:42
  115.8 16.3 %collective-permute-start.32 = (bf16[4,32,2304]{2,1,0:T(8,128)(2,1)S(1)}, bf16[4,32,2304]{2,1,0:T(8,128)(2,1)S(1)}, u32[]{:S(2)}, u32[]{:S(2)}) collective-permute-start(bf16[4,32,2304]{2,1,0:T(8,128)(2,1)S(1)} %get-tuple-element.79.refs_11_.refs_0_), channel_id=1, source_target_pairs={{0,2},{1,3},{2,0},{3,1},{4,6},{5,7},{6,4},{7,5},{8,10},{9,11},{10,... | collective-permute-start | bytes 1769480 | tf_op jit(solution)/shard_map/ppermute | solution.py:42
  116.6 17.8 %collective-permute-start.33 = (bf16[4,32,2304]{2,1,0:T(8,128)(2,1)S(1)}, bf16[4,32,2304]{2,1,0:T(8,128)(2,1)S(1)}, u32[]{:S(2)}, u32[]{:S(2)}) collective-permute-start(bf16[4,32,2304]{2,1,0:T(8,128)(2,1)S(1)} %get-tuple-element.80.refs_1_), channel_id=1, source_target_pairs={{0,6},{1,7},{2,4},{3,5},{4,2},{5,3},{6,0},{7,1},{8,14},{9,15},{10,... | collective-permute-start | bytes 1769480 | tf_op jit(solution)/shard_map/ppermute | solution.py:42
  118.3 17.8 %collective-permute-start.34 = (bf16[4,32,2688]{2,1,0:T(8,128)(2,1)S(1)}, bf16[4,32,2688]{2,1,0:T(8,128)(2,1)S(1)}, u32[]{:S(2)}, u32[]{:S(2)}) collective-permute-start(bf16[4,32,2688]{2,1,0:T(8,128)(2,1)S(1)} %get-tuple-element.81.refs_2_), channel_id=1, source_target_pairs={{0,8},{1,9},{2,10},{3,11},{4,12},{5,13},{6,14},{7,15},{8,0},{9,1},... | collective-permute-start | bytes 2064392 | tf_op jit(solution)/shard_map/ppermute | solution.py:42
  118.3 45.3 %collective-permute-start.42 = (bf16[4,32,9216]{2,1,0:T(8,128)(2,1)}, bf16[4,32,9216]{2,1,0:T(8,128)(2,1)S(1)}, u32[]{:S(2)}, u32[]{:S(2)}) collective-permute-start(bf16[4,32,9216]{2,1,0:T(8,128)(2,1)} %get-tuple-element.85), channel_id=1, source_target_pairs={{0,1},{1,0},{2,3},{3,2},{4,5},{5,4},{6,7},{7,6},{8,9},{9,8},{10,11... | collective-permute-start | bytes 7077896 | tf_op jit(solution)/shard_map/ppermute | solution.py:42
  132.0 19.6 %collective-permute-start.39 = (bf16[4,32,3072]{2,1,0:T(8,128)(2,1)S(1)}, bf16[4,32,3072]{2,1,0:T(8,128)(2,1)S(1)}, u32[]{:S(2)}, u32[]{:S(2)}) collective-permute-start(bf16[4,32,3072]{2,1,0:T(8,128)(2,1)S(1)} %get-tuple-element.78.refs_7_.refs_0_), channel_id=1, source_target_pairs={{0,2},{1,3},{2,0},{3,1},{4,6},{5,7},{6,4},{7,5},{8,10},{9,11},{10,... | collective-permute-start | bytes 2359304 | tf_op jit(solution)/shard_map/ppermute | solution.py:42
  132.2 24.7 %collective-permute-start.40 = (bf16[4,32,3072]{2,1,0:T(8,128)(2,1)S(1)}, bf16[4,32,3072]{2,1,0:T(8,128)(2,1)S(1)}, u32[]{:S(2)}, u32[]{:S(2)}) collective-permute-start(bf16[4,32,3072]{2,1,0:T(8,128)(2,1)S(1)} %get-tuple-element.83.refs_1_), channel_id=1, source_target_pairs={{0,6},{1,7},{2,4},{3,5},{4,2},{5,3},{6,0},{7,1},{8,14},{9,15},{10,... | collective-permute-start | bytes 2359304 | tf_op jit(solution)/shard_map/ppermute | solution.py:42
  134.4 25.0 %collective-permute-start.41 = (bf16[4,32,3072]{2,1,0:T(8,128)(2,1)S(1)}, bf16[4,32,3072]{2,1,0:T(8,128)(2,1)S(1)}, u32[]{:S(2)}, u32[]{:S(2)}) collective-permute-start(bf16[4,32,3072]{2,1,0:T(8,128)(2,1)S(1)} %get-tuple-element.84.refs_2_), channel_id=1, source_target_pairs={{0,8},{1,9},{2,10},{3,11},{4,12},{5,13},{6,14},{7,15},{8,0},{9,1},... | collective-permute-start | bytes 2359304 | tf_op jit(solution)/shard_map/ppermute | solution.py:42
  136.1 42.9 %collective-permute-start.35 = (bf16[4,32,7296]{2,1,0:T(8,128)(2,1)}, bf16[4,32,7296]{2,1,0:T(8,128)(2,1)S(1)}, u32[]{:S(2)}, u32[]{:S(2)}) collective-permute-start(bf16[4,32,7296]{2,1,0:T(8,128)(2,1)} %get-tuple-element.82), channel_id=1, source_target_pairs={{0,1},{1,0},{2,3},{3,2},{4,5},{5,4},{6,7},{7,6},{8,9},{9,8},{10,11... | collective-permute-start | bytes 5603336 | tf_op jit(solution)/shard_map/ppermute | solution.py:42
  160.5 18.5 %collective-permute-start.38 = (bf16[4,32,2688]{2,1,0:T(8,128)(2,1)S(1)}, bf16[4,32,2688]{2,1,0:T(8,128)(2,1)S(1)}, u32[]{:S(2)}, u32[]{:S(2)}) collective-permute-start(bf16[4,32,2688]{2,1,0:T(8,128)(2,1)S(1)} %collective-permute-done.34.refs_5_), channel_id=1, source_target_pairs={{0,1},{1,0},{2,3},{3,2},{4,5},{5,4},{6,7},{7,6},{8,9},{9,8},{10,11... | collective-permute-start | bytes 2064392 | tf_op jit(solution)/shard_map/ppermute | solution.py:42
  161.3 17.7 %collective-permute-start.36 = (bf16[4,32,2304]{2,1,0:T(8,128)(2,1)S(1)}, bf16[4,32,2304]{2,1,0:T(8,128)(2,1)S(1)}, u32[]{:S(2)}, u32[]{:S(2)}) collective-permute-start(bf16[4,32,2304]{2,1,0:T(8,128)(2,1)S(1)} %collective-permute-done.32.refs_3_), channel_id=1, source_target_pairs={{0,1},{1,0},{2,3},{3,2},{4,5},{5,4},{6,7},{7,6},{8,9},{9,8},{10,11... | collective-permute-start | bytes 1769480 | tf_op jit(solution)/shard_map/ppermute | solution.py:42
  163.3 15.7 %collective-permute-start.37 = (bf16[4,32,2304]{2,1,0:T(8,128)(2,1)S(1)}, bf16[4,32,2304]{2,1,0:T(8,128)(2,1)S(1)}, u32[]{:S(2)}, u32[]{:S(2)}) collective-permute-start(bf16[4,32,2304]{2,1,0:T(8,128)(2,1)S(1)} %collective-permute-done.33.refs_4_), channel_id=1, source_target_pairs={{0,1},{1,0},{2,3},{3,2},{4,5},{5,4},{6,7},{7,6},{8,9},{9,8},{10,11... | collective-permute-start | bytes 1769480 | tf_op jit(solution)/shard_map/ppermute | solution.py:42
  (20 other events, 102.7 us)

commit v2 on v1

--- a/solution.py
+++ b/solution.py
@@ -14,10 +14,12 @@
 STEP = 256
 NOTE = 128
 ANY = pl.BlockSpec(memory_space=pl.ANY)
-HBM = pl.BlockSpec(memory_space=pltpu.HBM)
 SMEM = pl.BlockSpec(memory_space=pltpu.SMEM)
 VMEM = pl.BlockSpec(memory_space=pltpu.VMEM)
-VMEM_BYTES = 48 * 1024 * 1024
+MIB = 1024 * 1024
+SUM_BYTES = 45 * MIB
+ROW_BYTES = 16 * MIB
+PRODUCT_BYTES = 41 * MIB
 
 
 def index_of(z, y, c):
@@ -78,23 +80,21 @@
     return total
 
 
-def call(name, kernel, ins, outs, scratch, copies, after, aliases={}, pinned=()):
+def call(name, kernel, ins, outs, scratch, copies, after, aliases={}, limit=SUM_BYTES):
     return pl.pallas_call(
         kernel,
-        in_specs=[SMEM]
-        + [HBM if i in pinned else ANY for i in range(1, len(ins))]
-        + [ANY] * len(after),
+        in_specs=[SMEM] + [ANY] * (len(ins) - 1 + len(after)),
         out_specs=[ANY] * len(outs),
         name=name,
         out_shape=outs,
         scratch_shapes=scratch + [pltpu.SemaphoreType.DMA((copies,))],
         input_output_aliases=aliases,
-        compiler_params=pltpu.CompilerParams(vmem_limit_bytes=VMEM_BYTES),
+        compiler_params=pltpu.CompilerParams(vmem_limit_bytes=limit),
         cost_estimate=pl.CostEstimate(flops=0, bytes_accessed=1024, transcendentals=0),
     )(*ins, *after)
 
 
-def copied(name, ins, outs, items, after, pinned=()):
+def copied(name, ins, outs, items, after):
     n = len(ins)
 
     def kernel(*refs):
@@ -108,7 +108,7 @@
         for copy in going:
             copy.wait()
 
-    return call(name, kernel, ins, outs, [], 36, after, pinned=pinned)
+    return call(name, kernel, ins, outs, [], 36, after, limit=ROW_BYTES)
 
 
 def added(name, ins, outs, items, after):
@@ -145,7 +145,7 @@
         pltpu.VMEM((len(plan), most, ROWS, widest), jnp.bfloat16),
         pltpu.VMEM((len(plan), ROWS, widest), jnp.bfloat16),
     ]
-    return call(name, kernel, ins, outs, scratch, len(plan) * (most + 1), after, pinned=(1,))
+    return call(name, kernel, ins, outs, scratch, len(plan) * (most + 1), after)
 
 
 class Part:
@@ -164,14 +164,18 @@
 
 
 class Stream:
-    def __init__(self, *parts):
+    def __init__(self, parts, before):
         self.parts = parts
         self.start = parts[0].start
         self.features = sum(p.features for p in parts)
         self.note = sum(p.note for p in parts)
+        self.before = before
 
     def sent(self, part):
         return pl.ds(part.start - self.start, part.sent)
+
+    def place_of(self, k):
+        return pl.ds(self.before[k], self.parts[k].sent)
 
 
 def row_block(place, apart):
@@ -223,7 +227,7 @@
 
     scratch = [pltpu.VMEM((4, ROWS, width), jnp.bfloat16)]
     out = shape(4, ROWS, width)
-    return call("give", kernel, [place, terms], [out], scratch, 2 * count, after, pinned=(1,))
+    return call("give", kernel, [place, terms], [out], scratch, 2 * count, after)
 
 
 def pair_sum(at, x, r, offset, part, e1, e2, e3):
@@ -298,7 +302,7 @@
             copies.start(gain_ref.at[:, there], gains),
         ]
         if so_far:
-            first.append(copies.start(refs[15], sums))
+            first.append(copies.start(refs[18], sums))
         else:
             sums[...] = jnp.zeros_like(sums)
         loads, slots = [], []
@@ -326,7 +330,7 @@
             total = by_columns(part.features, body)(total)
             if not part.note:
                 here = made.at[k, :, pl.ds(0, part.features)]
-                storing.append(copies.start(here, gained_out[k]))
+                storing.append(copies.start(here, gained_out[k].at[:, stream.place_of(k)]))
         sums[...] = total
         storing.append(copies.start(news, stream_out.at[:, there]))
         storing.append(copies.start(sums, squares_out))
@@ -341,12 +345,12 @@
                 parts = jnp.where(lane == 0, high, jnp.where(lane == 1, middle, low))
                 made[k, :, pl.ds(part.features, NOTE)] = bf16(jnp.where(lane < 3, parts, 0.0))
                 here = made.at[k, :, pl.ds(0, part.sent)]
-                storing.append(copies.start(here, gained_out[k]))
+                storing.append(copies.start(here, gained_out[k].at[:, stream.place_of(k)]))
         for copy in storing:
             copy.wait()
 
     outs = [shape(ROWS, D)]
-    outs += [shape(ROWS, part.sent) for part in stream.parts]
+    outs += [shape(ROWS, w) for w in WIDTHS]
     outs += [shape(ROWS, 128, dtype=jnp.float32)]
     scratch = [
         pltpu.VMEM((3, 5, ROWS, widest), jnp.bfloat16),
@@ -356,115 +360,114 @@
         pltpu.VMEM((3, ROWS, widest + NOTE), jnp.bfloat16),
         pltpu.VMEM((ROWS, 128), jnp.float32),
     ]
-    aliases = {14: 0} if so_far else {}
-    out = call("finish", kernel, ins, outs, scratch, 3 * 5 + 8, after, aliases, pinned=(1,))
-    return out[1:4], (out[0], out[4])
-
-
-def two_blocks(place, own, far, stream, after):
-    def items(at, refs):
-        return [(k, e, refs[e * 3 + k]) for e in range(2) for k in range(3)]
-
-    outs = [shape(2, ROWS, part.sent) for part in stream.parts]
-    return copied("two", [place, *own, *far], outs, items, after)
-
-
-def four_blocks(place, near, far, stream, after):
+    aliases = {14: 0, 15: 1, 16: 2, 17: 3} if so_far else {}
+    out = call("finish", kernel, ins, outs, scratch, 3 * 5 + 8, after, aliases)
+    return out
+
+
+def four_blocks(place, held, stream, after):
     def items(at, refs):
         found = []
         for k, part in enumerate(stream.parts):
-            for e in range(2):
-                some = pl.ds(2 * e, 2)
-                found.append((k, some, refs[e * 3 + k]))
-                found.append((3, (some, slice(None), stream.sent(part)), refs[e * 3 + k]))
+            for e in range(4):
+                source = refs[e * 3 + k].at[:, stream.place_of(k)]
+                found.append((k, e, source))
+                found.append((3, (e, slice(None), stream.sent(part)), source))
         return found
 
     outs = [shape(4, ROWS, part.sent) for part in stream.parts]
     outs.append(shape(4, ROWS, stream.features + stream.note))
-    out = copied("four", [place, *near, *far], outs, items, after)
+    out = copied("four", [place, *held], outs, items, after)
     return out[:3], out[3]
 
 
-def multiplied(place, near, far, beside, other_far, weight, total, stream, depth, after):
-    tiles = stream.features // depth
-    slots = 2
-    last = bool(stream.note)
-    half = NC * NZ * NY * ROWS // 2
-    ins = [*near, *far, beside, *other_far]
+def multiplied(place, side, own, other, weight, total, stream, notes, after):
+    last = bool(notes)
+    half = NZ * NY * ROWS
+    ins = [*own, *other, *notes]
+    n = len(ins)
     more = [] if total is None else [total]
 
+    def position(part, e1, e2, e3, c):
+        z, y = part.apart(e1, e2, e3)
+        return pl.ds((c * NZ * NY + z * NY + y) * ROWS, ROWS)
+
     def kernel(place_ref, *refs):
-        sources, weight_ref = refs[:10], refs[10]
-        total_ref = None if total is None else refs[11]
-        at = 11 + len(more) + len(after)
-        result = refs[at]
+        weight_ref = refs[n]
+        total_ref = None if total is None else refs[n + 1]
+        at = n + 1 + len(more) + len(after)
+        target = refs[at]
         rows, held, sems = refs[at + 1], refs[at + 2], refs[-1]
-        out = refs[at + 3] if last else result
+        out = refs[at + 3] if last else target
         copies = Copies(sems)
-
-        def load(t):
-            there = pl.ds(stream.start + t * depth, depth)
-            return copies.start(weight_ref.at[there], held.at[t % slots])
-
-        loads = [load(t) for t in range(slots)]
-        taking = []
+        loads = []
         for k, part in enumerate(stream.parts):
             columns = stream.sent(part)
-            for e2 in range(2):
-                for e3 in range(2):
-                    e = e2 * 2 + e3
-                    blocks = (
-                        (0, 0, sources[k].at[e]),
-                        (0, 1, sources[6].at[e, :, columns]),
-                        (1, 0, sources[3 + k].at[e]),
-                        (1, 1, sources[7 + k].at[e]),
-                    )
-                    for e1, c, source in blocks:
-                        z, y = part.apart(e1, e2, e3)
-                        to = pl.ds(((z * NY + y) * NC + c) * ROWS, ROWS)
-                        taking.append(copies.start(source, rows.at[to, columns]))
-        for copy in taking:
-            copy.wait()
-        for t in range(tiles):
-            loads[t].wait()
-            here = pl.ds(t * depth, depth)
-            for m in range(2):
-                some = pl.ds(m * half, half)
-                product = jnp.dot(
-                    rows[some, here], held[t % slots], preferred_element_type=jnp.float32
-                )
-                if t == 0:
-                    out[some, :] = product if total_ref is None else total_ref[some, :] + product
-                else:
-                    out[some, :] += product
-            if t + slots < tiles:
-                loads.append(load(t + slots))
+            there = pl.ds(part.start, part.features)
+            here = pl.ds(part.start - stream.start, part.features)
+            going = [copies.start(weight_ref.at[there], held.at[here])]
+            for e in range(4):
+                to = rows.at[pl.ds(e * ROWS, ROWS), columns]
+                going.append(copies.start(refs[k].at[e], to))
+                source = refs[3 + k].at[e] if len(other) > 1 else refs[3].at[e, :, columns]
+                to = rows.at[pl.ds((4 + e) * ROWS, ROWS), columns]
+                going.append(copies.start(source, to))
+            loads.append(going)
         if last:
-            for z in range(NZ):
-                for y in range(NY):
+            part = stream.parts[2]
+            near, beside, notes_held = refs[n - 2], refs[n - 1], refs[at + 4]
+            first = [
+                copies.start(near.at[:, :, pl.ds(part.features, NOTE)], notes_held.at[0]),
+                copies.start(beside.at[:, :, pl.ds(stream.features, NOTE)], notes_held.at[1]),
+            ]
+        if total_ref is None:
+            out[...] = jnp.zeros_like(out)
+        else:
+            out[...] = total_ref[...]
+        for k, part in enumerate(stream.parts):
+            for copy in loads[k]:
+                copy.wait()
+            here = pl.ds(part.start - stream.start, part.features)
+            product = jnp.dot(rows[:, here], held[here, :], preferred_element_type=jnp.float32)
+            for c in range(NC):
+                for e in range(4):
+                    some = (c * 4 + e) * ROWS
+                    out[position(part, side, e // 2, e % 2, c), :] += product[some : some + ROWS]
+        if last:
+            for copy in first:
+                copy.wait()
+            part = stream.parts[2]
+            for e1 in range(2):
+                for e in range(4):
                     for c in range(NC):
-                        to = row_block(place_ref, (z, y)) * NC + lax.bitwise_xor(place_ref[2], c)
+                        if e1 == side:
+                            some = pl.ds((c * 4 + e) * ROWS, ROWS)
+                            note = rows[some, pl.ds(stream.features, NOTE)]
+                        else:
+                            note = notes_held[c, e]
+                        scale = jnp.sum(note.astype(jnp.float32), axis=1, keepdims=True)
+                        apart = part.apart(e1, e // 2, e % 2)
+                        to = row_block(place_ref, apart) * NC + lax.bitwise_xor(place_ref[2], c)
                         to = pl.ds(pl.multiple_of(to * ROWS, ROWS), ROWS)
-                        here = pl.ds(((z * NY + y) * NC + c) * ROWS, ROWS)
-                        note = rows[here, pl.ds(stream.features, NOTE)].astype(jnp.float32)
-                        scale = jnp.sum(note, axis=1, keepdims=True)
-                        result[to, :] = bf16(out[here, :] * scale)
-
-    dtype = jnp.bfloat16 if last else jnp.float32
+                        here = position(part, e1, e // 2, e % 2, c)
+                        target[to, :] = bf16(out[here, :] * scale)
+
     scratch = [
-        pltpu.VMEM((2 * half, stream.features + stream.note), jnp.bfloat16),
-        pltpu.VMEM((slots, depth, COLS), jnp.bfloat16),
+        pltpu.VMEM((half, stream.features + stream.note), jnp.bfloat16),
+        pltpu.VMEM((stream.features, COLS), jnp.bfloat16),
     ]
     if last:
         scratch.append(pltpu.VMEM((2 * half, COLS), jnp.float32))
+        scratch.append(pltpu.VMEM((NC, 4, ROWS, NOTE), jnp.bfloat16))
+    dtype = jnp.bfloat16 if last else jnp.float32
     return pl.pallas_call(
         kernel,
-        in_specs=[SMEM] + [ANY] * 10 + [HBM] + [VMEM] * len(more) + [ANY] * len(after),
+        in_specs=[SMEM] + [ANY] * (n + 1) + [VMEM] * len(more) + [ANY] * len(after),
         name="multiply",
         out_specs=VMEM,
         out_shape=shape(2 * half, COLS, dtype=dtype),
-        scratch_shapes=scratch + [pltpu.SemaphoreType.DMA((48 + tiles,))],
-        compiler_params=pltpu.CompilerParams(vmem_limit_bytes=VMEM_BYTES),
+        scratch_shapes=scratch + [pltpu.SemaphoreType.DMA((29,))],
+        compiler_params=pltpu.CompilerParams(vmem_limit_bytes=PRODUCT_BYTES),
         cost_estimate=pl.CostEstimate(flops=0, bytes_accessed=1024, transcendentals=0),
     )(place, *ins, weight, *more, *after)
 
@@ -472,16 +475,17 @@
 ORDERS = (("a", "b", "z"), ("b", "z", "a"), ("z", "a", "b"))
 
 
-def stream_of(start, sizes, note):
+def stream_of(start, sizes, note, before):
     parts = []
     for i, (size, dims) in enumerate(zip(sizes, ORDERS)):
         parts.append(Part(start, size, dims, note if i == len(sizes) - 1 else 0))
         start += size
-    return Stream(*parts)
-
-
-FIRST = stream_of(0, (3072, 3072, 3072), 0)
-SECOND = stream_of(9216, (2304, 2304, 2560), NOTE)
+    return Stream(parts, before)
+
+
+FIRST = stream_of(0, (3072, 3072, 3072), 0, (0, 0, 0))
+SECOND = stream_of(9216, (2304, 2304, 2560), NOTE, (3072, 3072, 3072))
+WIDTHS = [a.sent + b.sent for a, b in zip(FIRST.parts, SECOND.parts)]
 
 
 def per_device(partials, residual, norm_gain, qkv_weight):
@@ -515,29 +519,33 @@
     a_three = along(2, a_out)
     b_out = third_step(place, terms, rest, b_one, b_two, b, [a_out[0]])
     b_three = along(2, b_out)
-    a_rows, so_far = finish(
+    so_far = finish(
         place, terms, rest, a_one, a_two, a_three, a, residual, gain, (), [b_out[0]]
     )
-    a_far = along(2, a_rows)
-    b_rows, (stream, _) = finish(
+    stream, *rows, _ = finish(
         place, terms, rest, b_one, b_two, b_three, b, residual, gain, so_far, []
     )
-    b_far = along(2, b_rows)
-    a_near = two_blocks(place, a_rows, a_far, a, [b_rows[0]])
-    a_far = along(1, a_near)
-    b_near = two_blocks(place, b_rows, b_far, b, [a_near[0]])
-    b_far = along(1, b_near)
-    a_near, a_beside = four_blocks(place, a_near, a_far, a, [b_near[0]])
+    rows_z = along(2, rows)
+    rows_y = along(1, rows)
+    rows_zy = along(1, rows_z)
+    held = [*rows, *rows_z, *rows_y, *rows_zy]
+    a_near, a_beside = four_blocks(place, held, a, [])
     a_far = along(0, a_near)
     a_beside = send(a_beside, TO_CORE)
-    b_near, b_beside = four_blocks(place, b_near, b_far, b, [a_near[0]])
+    b_near, b_beside = four_blocks(place, held, b, [a_near[0]])
     b_far = along(0, b_near)
     b_beside = send(b_beside, TO_CORE)
 
-    a_all = (a_near, a_far, a_beside, across(a_far))
-    total = multiplied(place, *a_all, qkv_weight, None, a, 1536, [b_near[0]])
-    b_all = (b_near, b_far, b_beside, across(b_far))
-    return stream, multiplied(place, *b_all, qkv_weight, total, b, 1792, [])
+    near = functools.partial(multiplied, place, 0)
+    far = functools.partial(multiplied, place, 1)
+    total = near(a_near, [a_beside], qkv_weight, None, a, [], [b_near[0]])
+    total = near(b_near, [b_beside], qkv_weight, total, b, [], [])
+    *a_ready, _ = lax.optimization_barrier((*a_far, total))
+    total = far(a_far, across(a_ready), qkv_weight, total, a, [], [])
+    *b_ready, _ = lax.optimization_barrier((*b_far, total))
+    notes = [b_near[2], b_beside]
+    projected = far(b_far, across(b_ready), qkv_weight, total, b, notes, [])
+    return stream, projected
 
 
 def solution(mesh):

time: 193 us -> 169 us (0.88)
  starting transfers between devices: 74.9 us -> 49.1 us
  waiting for transfers between devices: 37.7 us -> 46 us
  local copies, waits for them, and re-layouts: 3.54 us -> 0.02 us
  Pallas kernels: 75.2 us -> 72.6 us
    ppermute x46 -> x43, starting transfers between devices: 74.9 us -> 49.1 us  [send(): return lax.ppermute(x, 'tensor', where)]
    ppermute x46 -> x43, waiting for transfers between devices: 37.7 us -> 46 us  [send(): return lax.ppermute(x, 'tensor', where)]
    unnamed x12 -> x10, local copies, waits for them, and re-layouts: 3.54 us -> 0.02 us
    pallas_call x16, Pallas kernels: 75.2 us -> 72.6 us  [the longest x12 45.1 us: call(): pl.pallas_call(kernel, in_specs=[SMEM] + [ANY] * (len(ins) - 1 + len(afte...]
  transfers between devices with their start and end apart: 46 -> 43, of which waited for: 18 -> 22; matrix products, arithmetic and copies ran while one was open for 0% -> 0% of each run, Pallas kernels for 29% -> 34%
where the time goes in v2:
time: 169 us
  Pallas kernels  72.6 us (43%)
  starting transfers between devices  49.1 us (29%)
  waiting for transfers between devices  46 us (27%)
    ppermute x43, starting transfers between devices, send(): return lax.ppermute(x, 'tensor', where)  49.1 us
    ppermute x43, waiting for transfers between devices, send(): return lax.ppermute(x, 'tensor', where)  46 us
    pallas_call x12, Pallas kernels, call(): pl.pallas_call(kernel, in_specs=[SMEM] + [ANY] * (len(ins) - 1 + len(afte...  45.1 us
    pallas_call x4, Pallas kernels, multiplied(): pl.pallas_call(kernel, in_specs=[SMEM] + [ANY] * (n + 1) + [VMEM] * len(m...  27.5 us
  transfers between devices with their start and end apart: 43, of which 22 were waited for; matrix products, arithmetic and copies ran while one was open for 0% of the time, Pallas kernels for 34%

profile of v2, /device:TPU:1, one launch (start us, length us, event | category | flops | bytes accessed | tf_op | source)
XLA Modules:
  0.0 168.9 jit_solution(6545229050358316010)
XLA Ops:
  0.7 2.6 %give.2.refs_2_ = bf16[4,32,9216]{2,1,0:T(8,128)(2,1)S(1)} custom-call(s32[3]{0:T(128)S(1)} %pad_add_fusion.refs_0_.place_ref, bf16[16,32,16384]{2,1,0:T(8,128)(2,1)} %bitcast.9), custom_call_target="tpu_custom_call" | custom-call | bytes 1024 | tf_op jit(solution)/shard_map/give/pallas_call | solution.py:84
  4.8 6.2 %give.3.refs_3_ = bf16[4,32,23552]{2,1,0:T(8,128)(2,1)} custom-call(s32[3]{0:T(128)S(1)} %pad_add_fusion.refs_0_.place_ref, bf16[16,32,16384]{2,1,0:T(8,128)(2,1)} %bitcast.10, bf16[4,32,9216]{2,1,0:T(8,128)(2,1)S(1)} %give.2.refs_2_), custom_call_target="tpu_custom_call" | custom-call | bytes 1024 | tf_op jit(solution)/shard_map/give/pallas_call | solution.py:84
  11.1 5.9 %first.2 = (bf16[4,32,3072]{2,1,0:T(8,128)(2,1)S(1)}, bf16[4,32,3072]{2,1,0:T(8,128)(2,1)S(1)}, bf16[4,32,3072]{2,1,0:T(8,128)(2,1)S(1)}) custom-call(s32[3]{0:T(128)S(1)} %pad_add_fusion.refs_0_.place_ref, bf16[16,32,16384]{2,1,0:T(8,128)(2,1)} %bitcast.11, bf16[4,32,9216]{2,1,0:T(8,128)(2,1)S(1)} %collective-permute-done.refs_2_, ...), custom_call_target="tpu_custom_call" | custom-call | bytes 1024 | tf_op jit(solution)/shard_map/first/pallas_call | solution.py:84
  18.4 1.9 %collective-permute-start.6 = (bf16[4,32,3072]{2,1,0:T(8,128)(2,1)S(1)}, bf16[4,32,3072]{2,1,0:T(8,128)(2,1)S(1)}, u32[]{:S(2)}, u32[]{:S(2)}) collective-permute-start(bf16[4,32,3072]{2,1,0:T(8,128)(2,1)S(1)} %get-tuple-element.49), channel_id=1, source_target_pairs={{0,6},{1,7},{2,4},{3,5},{4,2},{5,3},{6,0},{7,1},{8,14},{9,15},{10,... | collective-permute-start | bytes 2359304 | tf_op jit(solution)/shard_map/ppermute | solution.py:44
  22.0 4.6 %first.3 = (bf16[4,32,2304]{2,1,0:T(8,128)(2,1)S(1)}, bf16[4,32,2304]{2,1,0:T(8,128)(2,1)S(1)}, bf16[4,32,2560]{2,1,0:T(8,128)(2,1)S(1)}) custom-call(s32[3]{0:T(128)S(1)} %pad_add_fusion.refs_0_.place_ref, bf16[16,32,16384]{2,1,0:T(8,128)(2,1)} %bitcast.12, bf16[4,32,23552]{2,1,0:T(8,128)(2,1)S(1)} %collective-permute-done.1.refs_2_, ...), custom_call_target="tpu_custom_call" | custom-call | bytes 1024 | tf_op jit(solution)/shard_map/first/pallas_call | solution.py:84
  28.8 6.9 %collective-permute-done.5.refs_3_ = bf16[4,32,3072]{2,1,0:T(8,128)(2,1)S(1)} collective-permute-done((bf16[4,32,3072]{2,1,0:T(8,128)(2,1)S(1)}, bf16[4,32,3072]{2,1,0:T(8,128)(2,1)S(1)}, u32[]{:S(2)}, u32[]{:S(2)}) %collective-permute-start.5) | collective-permute-done | bytes 786464 | tf_op jit(solution)/shard_map/ppermute | solution.py:44
  35.7 2.8 %collective-permute-start.3 = (bf16[4,32,2304]{2,1,0:T(8,128)(2,1)S(1)}, bf16[4,32,2304]{2,1,0:T(8,128)(2,1)S(1)}, u32[]{:S(2)}, u32[]{:S(2)}) collective-permute-start(bf16[4,32,2304]{2,1,0:T(8,128)(2,1)S(1)} %get-tuple-element.47), channel_id=1, source_target_pairs={{0,6},{1,7},{2,4},{3,5},{4,2},{5,3},{6,0},{7,1},{8,14},{9,15},{10,... | collective-permute-start | bytes 1769480 | tf_op jit(solution)/shard_map/ppermute | solution.py:44
  38.7 4.6 %second.2 = (bf16[2,32,3072]{2,1,0:T(8,128)(2,1)S(1)}, bf16[2,32,3072]{2,1,0:T(8,128)(2,1)S(1)}, bf16[2,32,3072]{2,1,0:T(8,128)(2,1)S(1)}) custom-call(s32[3]{0:T(128)S(1)} %pad_add_fusion.refs_0_.place_ref, bf16[16,32,16384]{2,1,0:T(8,128)(2,1)} %bitcast.13, bf16[4,32,23552]{2,1,0:T(8,128)(2,1)} %copy-done, ...), custom_call_target="tpu_custom_call" | custom-call | bytes 1024 | tf_op jit(solution)/shard_map/second/pallas_call | solution.py:84
  46.2 2.2 %collective-permute-done.2.refs_3_ = bf16[4,32,2304]{2,1,0:T(8,128)(2,1)S(1)} collective-permute-done((bf16[4,32,2304]{2,1,0:T(8,128)(2,1)S(1)}, bf16[4,32,2304]{2,1,0:T(8,128)(2,1)S(1)}, u32[]{:S(2)}, u32[]{:S(2)}) %collective-permute-start.2) | collective-permute-done | bytes 589856 | tf_op jit(solution)/shard_map/ppermute | solution.py:44
  49.7 3.0 %collective-permute-done.4.refs_5_ = bf16[4,32,2560]{2,1,0:T(8,128)(2,1)S(1)} collective-permute-done((bf16[4,32,2560]{2,1,0:T(8,128)(2,1)S(1)}, bf16[4,32,2560]{2,1,0:T(8,128)(2,1)S(1)}, u32[]{:S(2)}, u32[]{:S(2)}) %collective-permute-start.4) | collective-permute-done | bytes 655392 | tf_op jit(solution)/shard_map/ppermute | solution.py:44
  52.7 2.8 %second.3 = (bf16[2,32,2304]{2,1,0:T(8,128)(2,1)S(1)}, bf16[2,32,2304]{2,1,0:T(8,128)(2,1)S(1)}, bf16[2,32,2560]{2,1,0:T(8,128)(2,1)S(1)}) custom-call(s32[3]{0:T(128)S(1)} %pad_add_fusion.refs_0_.place_ref, bf16[16,32,16384]{2,1,0:T(8,128)(2,1)} %bitcast.14, bf16[4,32,23552]{2,1,0:T(8,128)(2,1)S(1)} %bitcast.6, ...), custom_call_target="tpu_custom_call" | custom-call | bytes 1024 | tf_op jit(solution)/shard_map/second/pallas_call | solution.py:84
  61.2 3.6 %third.2 = (bf16[32,3072]{1,0:T(8,128)(2,1)S(1)}, bf16[32,3072]{1,0:T(8,128)(2,1)S(1)}, bf16[32,3072]{1,0:T(8,128)(2,1)S(1)}) custom-call(s32[3]{0:T(128)S(1)} %pad_add_fusion.refs_0_.place_ref, bf16[16,32,16384]{2,1,0:T(8,128)(2,1)} %bitcast.15, bf16[4,32,23552]{2,1,0:T(8,128)(2,1)} %copy-done, bf16[4,32,3072]{2,1,0:T(8,128)(2,1)S(1)} %collective-permute-done.5.refs_3_, ...), custom_call_target="tpu_custom_call" | custom-call | bytes 1024 | tf_op jit(solution)/shard_map/third/pallas_call | solution.py:84
  67.4 2.3 %third.3 = (bf16[32,2304]{1,0:T(8,128)(2,1)S(1)}, bf16[32,2304]{1,0:T(8,128)(2,1)S(1)}, bf16[32,2560]{1,0:T(8,128)(2,1)S(1)}) custom-call(s32[3]{0:T(128)S(1)} %pad_add_fusion.refs_0_.place_ref, bf16[16,32,16384]{2,1,0:T(8,128)(2,1)} %bitcast.16, bf16[4,32,23552]{2,1,0:T(8,128)(2,1)} %copy-done, bf16[4,32,2304]{2,1,0:T(8,128)(2,1)S(1)} %collective-permute-done.2.refs_3_, ...), custom_call_target="tpu_custom_call" | custom-call | bytes 1024 | tf_op jit(solution)/shard_map/third/pallas_call | solution.py:84
  72.2 4.9 %finish.2 = (bf16[32,16384]{1,0:T(8,128)(2,1)}, bf16[32,5376]{1,0:T(8,128)(2,1)S(1)}, bf16[32,5376]{1,0:T(8,128)(2,1)S(1)}, bf16[32,5760]{1,0:T(8,128)(2,1)S(1)}, f32[32,128]{1,0:T(8,128)S(1)}) custom-call(s32[3]{0:T(128)S(1)} %pad_add_fusion.refs_0_.place_ref, bf16[16,32,16384]{2,1,0:T(8,128)(2,1)} %bitcast.17, bf16[4,32,23552]{2,1,0:T(8,128)(2,1)} %copy-done, ...), custom_call_target="tpu_custom_call" | custom-call | bytes 1024 | tf_op jit(solution)/shard_map/finish/pallas_call | solution.py:84
  77.2 3.3 %finish.3 = (bf16[32,16384]{1,0:T(8,128)(2,1)}, bf16[32,5376]{1,0:T(8,128)(2,1)S(1)}, bf16[32,5376]{1,0:T(8,128)(2,1)S(1)}, bf16[32,5760]{1,0:T(8,128)(2,1)S(1)}, f32[32,128]{1,0:T(8,128)}) custom-call(s32[3]{0:T(128)S(1)} %pad_add_fusion.refs_0_.place_ref, ...), custom_call_target="tpu_custom_call", output_to_operand_aliasing={{0}: (14, {}), {1}: (15, {}), {2}: (16, {}), {3}: (17, {})} | custom-call | bytes 1024 | tf_op jit(solution)/shard_map/finish/pallas_call | solution.py:84
  80.5 2.1 %collective-permute-start.22 = (bf16[32,5760]{1,0:T(8,128)(2,1)S(1)}, bf16[32,5760]{1,0:T(8,128)(2,1)S(1)}, u32[]{:S(2)}, u32[]{:S(2)}) collective-permute-start(bf16[32,5760]{1,0:T(8,128)(2,1)S(1)} %get-tuple-element.71.refs_3_), channel_id=1, source_target_pairs={{0,6},{1,7},{2,4},{3,5},{4,2},{5,3},{6,0},{7,1},{8,14},{9,15},{10,... | collective-permute-start | bytes 1105928 | tf_op jit(solution)/shard_map/ppermute | solution.py:44
  85.3 2.8 %collective-permute-done.22.refs_6_ = bf16[32,5760]{1,0:T(8,128)(2,1)S(1)} collective-permute-done((bf16[32,5760]{1,0:T(8,128)(2,1)S(1)}, bf16[32,5760]{1,0:T(8,128)(2,1)S(1)}, u32[]{:S(2)}, u32[]{:S(2)}) %collective-permute-start.22) | collective-permute-done | bytes 368672 | tf_op jit(solution)/shard_map/ppermute | solution.py:44
  90.5 2.4 %collective-permute-done.23.refs_7_ = bf16[32,5376]{1,0:T(8,128)(2,1)S(1)} collective-permute-done((bf16[32,5376]{1,0:T(8,128)(2,1)S(1)}, bf16[32,5376]{1,0:T(8,128)(2,1)S(1)}, u32[]{:S(2)}, u32[]{:S(2)}) %collective-permute-start.23) | collective-permute-done | bytes 344096 | tf_op jit(solution)/shard_map/ppermute | solution.py:44
  94.6 3.0 %collective-permute-done.24.refs_8_ = bf16[32,5376]{1,0:T(8,128)(2,1)S(1)} collective-permute-done((bf16[32,5376]{1,0:T(8,128)(2,1)S(1)}, bf16[32,5376]{1,0:T(8,128)(2,1)S(1)}, u32[]{:S(2)}, u32[]{:S(2)}) %collective-permute-start.24) | collective-permute-done | bytes 344096 | tf_op jit(solution)/shard_map/ppermute | solution.py:44
  97.6 3.1 %collective-permute-done.26.refs_10_ = bf16[32,5376]{1,0:T(8,128)(2,1)S(1)} collective-permute-done((bf16[32,5376]{1,0:T(8,128)(2,1)S(1)}, bf16[32,5376]{1,0:T(8,128)(2,1)S(1)}, u32[]{:S(2)}, u32[]{:S(2)}) %collective-permute-start.26) | collective-permute-done | bytes 344096 | tf_op jit(solution)/shard_map/ppermute | solution.py:44
  102.5 2.4 %four.2 = (bf16[4,32,3072]{2,1,0:T(8,128)(2,1)S(1)}, bf16[4,32,3072]{2,1,0:T(8,128)(2,1)S(1)}, bf16[4,32,3072]{2,1,0:T(8,128)(2,1)S(1)}, bf16[4,32,9216]{2,1,0:T(8,128)(2,1)S(1)}) custom-call(s32[3]{0:T(128)S(1)} %pad_add_fusion.refs_0_.place_ref, bf16[32,5376]{1,0:T(8,128)(2,1)S(1)} %get-tuple-element.69.refs_1_, ...), custom_call_target="tpu_custom_call" | custom-call | bytes 1024 | tf_op jit(solution)/shard_map/four/pallas_call | solution.py:84
  104.9 8.9 %collective-permute-start.36 = (bf16[4,32,9216]{2,1,0:T(8,128)(2,1)S(1)}, bf16[4,32,9216]{2,1,0:T(8,128)(2,1)S(1)}, u32[]{:S(2)}, u32[]{:S(2)}) collective-permute-start(bf16[4,32,9216]{2,1,0:T(8,128)(2,1)S(1)} %get-tuple-element.79), channel_id=1, source_target_pairs={{0,1},{1,0},{2,3},{3,2},{4,5},{5,4},{6,7},{7,6},{8,9},{9,8},{10,11... | collective-permute-start | bytes 7077896 | tf_op jit(solution)/shard_map/ppermute | solution.py:44
  113.8 2.1 %four.3 = (bf16[4,32,2304]{2,1,0:T(8,128)(2,1)S(1)}, bf16[4,32,2304]{2,1,0:T(8,128)(2,1)S(1)}, bf16[4,32,2688]{2,1,0:T(8,128)(2,1)S(1)}, bf16[4,32,7296]{2,1,0:T(8,128)(2,1)S(1)}) custom-call(s32[3]{0:T(128)S(1)} %pad_add_fusion.refs_0_.place_ref, bf16[32,5376]{1,0:T(8,128)(2,1)S(1)} %get-tuple-element.69.refs_1_, ...), custom_call_target="tpu_custom_call" | custom-call | bytes 1024 | tf_op jit(solution)/shard_map/four/pallas_call | solution.py:84
  116.7 2.7 %collective-permute-start.33 = (bf16[4,32,3072]{2,1,0:T(8,128)(2,1)S(1)}, bf16[4,32,3072]{2,1,0:T(8,128)(2,1)S(1)}, u32[]{:S(2)}, u32[]{:S(2)}) collective-permute-start(bf16[4,32,3072]{2,1,0:T(8,128)(2,1)S(1)} %get-tuple-element.76.refs_1_), channel_id=1, source_target_pairs={{0,6},{1,7},{2,4},{3,5},{4,2},{5,3},{6,0},{7,1},{8,14},{9,15},{10,... | collective-permute-start | bytes 2359304 | tf_op jit(solution)/shard_map/ppermute | solution.py:44
  119.4 7.1 %multiply.4.refs_5_ = f32[512,640]{1,0:T(8,128)S(1)} custom-call(s32[3]{0:T(128)S(1)} %pad_add_fusion.refs_0_.place_ref, bf16[4,32,3072]{2,1,0:T(8,128)(2,1)S(1)} %get-tuple-element.72.refs_13_.refs_0_, bf16[4,32,3072]{2,1,0:T(8,128)(2,1)S(1)} %get-tuple-element.76.refs_1_, bf16[4,32,3072]{2,1,0:T(8,128)(2,1)S(1)} %get-tuple-element.77.refs_2_, ...), custom_call_target="tpu_custom_call" | custom-call | bytes 1024 | tf_op jit(solution)/shard_map/multiply/pallas_call | solution.py:463
  126.5 6.1 %multiply.5.refs_7_ = f32[512,640]{1,0:T(8,128)S(1)} custom-call(s32[3]{0:T(128)S(1)} %pad_add_fusion.refs_0_.place_ref, bf16[4,32,2304]{2,1,0:T(8,128)(2,1)S(1)} %get-tuple-element.73.refs_5_.refs_0_, bf16[4,32,2304]{2,1,0:T(8,128)(2,1)S(1)} %get-tuple-element.74.refs_1_, bf16[4,32,2688]{2,1,0:T(8,128)(2,1)S(1)} %get-tuple-element.75.refs_2_.refs_6_, ...), custom_call_target="tpu_custom_call" | custom-call | bytes 1024 | tf_op jit(solution)/shard_map/multiply/pallas_call | solution.py:463
  132.6 2.2 %collective-permute-done.32.refs_0_ = bf16[4,32,3072]{2,1,0:T(8,128)(2,1)S(1)} collective-permute-done((bf16[4,32,3072]{2,1,0:T(8,128)(2,1)S(1)}, bf16[4,32,3072]{2,1,0:T(8,128)(2,1)S(1)}, u32[]{:S(2)}, u32[]{:S(2)}) %collective-permute-start.32) | collective-permute-done | bytes 786464 | tf_op jit(solution)/shard_map/ppermute | solution.py:44
  143.5 7.1 %multiply.6.refs_9_ = f32[512,640]{1,0:T(8,128)S(1)} custom-call(s32[3]{0:T(128)S(1)} %pad_add_fusion.refs_0_.place_ref, bf16[4,32,3072]{2,1,0:T(8,128)(2,1)S(1)} %collective-permute-done.32.refs_0_, bf16[4,32,3072]{2,1,0:T(8,128)(2,1)S(1)} %collective-permute-done.33.refs_1_, bf16[4,32,3072]{2,1,0:T(8,128)(2,1)S(1)} %collective-permute-done.34.refs_2_, ...), custom_call_target="tpu_custom_call" | custom-call | bytes 1024 | tf_op jit(solution)/shard_map/multiply/pallas_call | solution.py:463
  150.6 3.8 %collective-permute-done.29.refs_0_ = bf16[4,32,2304]{2,1,0:T(8,128)(2,1)S(1)} collective-permute-done((bf16[4,32,2304]{2,1,0:T(8,128)(2,1)S(1)}, bf16[4,32,2304]{2,1,0:T(8,128)(2,1)S(1)}, u32[]{:S(2)}, u32[]{:S(2)}) %collective-permute-start.29) | collective-permute-done | bytes 589856 | tf_op jit(solution)/shard_map/ppermute | solution.py:44
  154.5 2.5 %collective-permute-done.30.refs_1_ = bf16[4,32,2304]{2,1,0:T(8,128)(2,1)S(1)} collective-permute-done((bf16[4,32,2304]{2,1,0:T(8,128)(2,1)S(1)}, bf16[4,32,2304]{2,1,0:T(8,128)(2,1)S(1)}, u32[]{:S(2)}, u32[]{:S(2)}) %collective-permute-start.30) | collective-permute-done | bytes 589856 | tf_op jit(solution)/shard_map/ppermute | solution.py:44
  158.7 2.1 %collective-permute-done.40.refs_3_ = bf16[4,32,2304]{2,1,0:T(8,128)(2,1)S(1)} collective-permute-done((bf16[4,32,2304]{2,1,0:T(8,128)(2,1)S(1)}, bf16[4,32,2304]{2,1,0:T(8,128)(2,1)S(1)}, u32[]{:S(2)}, u32[]{:S(2)}) %collective-permute-start.40) | collective-permute-done | bytes 589856 | tf_op jit(solution)/shard_map/ppermute | solution.py:44
  161.6 7.1 %multiply.7 = bf16[512,640]{1,0:T(8,128)(2,1)} custom-call(s32[3]{0:T(128)S(1)} %pad_add_fusion.refs_0_.place_ref, bf16[4,32,2304]{2,1,0:T(8,128)(2,1)S(1)} %collective-permute-done.29.refs_0_, bf16[4,32,2304]{2,1,0:T(8,128)(2,1)S(1)} %collective-permute-done.30.refs_1_, bf16[4,32,2688]{2,1,0:T(8,128)(2,1)S(1)} %collective-permute-done.31.refs_2_, ...), custom_call_target="tpu_custom_call" | custom-call | bytes 1024 | tf_op jit(solution)/shard_map/multiply/pallas_call | solution.py:463
  (83 shorter events, 42.8 us)
Async XLA Ops:
  3.3 7.7 %collective-permute-start = (bf16[4,32,9216]{2,1,0:T(8,128)(2,1)S(1)}, bf16[4,32,9216]{2,1,0:T(8,128)(2,1)S(1)}, u32[]{:S(2)}, u32[]{:S(2)}) collective-permute-start(bf16[4,32,9216]{2,1,0:T(8,128)(2,1)S(1)} %give.2.refs_2_), channel_id=1, source_target_pairs={{0,1},{1,0},{2,3},{3,2},{4,5},{5,4},{6,7},{7,6},{8,9},{9,8},{10,11... | collective-permute-start | bytes 7077896 | tf_op jit(solution)/shard_map/ppermute | solution.py:44
  11.0 11.0 %collective-permute-start.1 = (bf16[4,32,23552]{2,1,0:T(8,128)(2,1)}, bf16[4,32,23552]{2,1,0:T(8,128)(2,1)S(1)}, u32[]{:S(2)}, u32[]{:S(2)}) collective-permute-start(bf16[4,32,23552]{2,1,0:T(8,128)(2,1)} %give.3.refs_3_), channel_id=1, source_target_pairs={{0,1},{1,0},{2,3},{3,2},{4,5},{5,4},{6,7},{7,6},{8,9},{9,8},{10,11... | collective-permute-start | bytes 18087944 | tf_op jit(solution)/shard_map/ppermute | solution.py:44
  17.0 18.7 %collective-permute-start.5 = (bf16[4,32,3072]{2,1,0:T(8,128)(2,1)S(1)}, bf16[4,32,3072]{2,1,0:T(8,128)(2,1)S(1)}, u32[]{:S(2)}, u32[]{:S(2)}) collective-permute-start(bf16[4,32,3072]{2,1,0:T(8,128)(2,1)S(1)} %get-tuple-element.45.refs_3_), channel_id=1, source_target_pairs={{0,2},{1,3},{2,0},{3,1},{4,6},{5,7},{6,4},{7,5},{8,10},{9,11},{10,... | collective-permute-start | bytes 2359304 | tf_op jit(solution)/shard_map/ppermute | solution.py:44
  18.4 20.1 %collective-permute-start.6 = (bf16[4,32,3072]{2,1,0:T(8,128)(2,1)S(1)}, bf16[4,32,3072]{2,1,0:T(8,128)(2,1)S(1)}, u32[]{:S(2)}, u32[]{:S(2)}) collective-permute-start(bf16[4,32,3072]{2,1,0:T(8,128)(2,1)S(1)} %get-tuple-element.49), channel_id=1, source_target_pairs={{0,6},{1,7},{2,4},{3,5},{4,2},{5,3},{6,0},{7,1},{8,14},{9,15},{10,... | collective-permute-start | bytes 2359304 | tf_op jit(solution)/shard_map/ppermute | solution.py:44
  20.3 18.3 %collective-permute-start.7 = (bf16[4,32,3072]{2,1,0:T(8,128)(2,1)S(1)}, bf16[4,32,3072]{2,1,0:T(8,128)(2,1)S(1)}, u32[]{:S(2)}, u32[]{:S(2)}) collective-permute-start(bf16[4,32,3072]{2,1,0:T(8,128)(2,1)S(1)} %get-tuple-element.50), channel_id=1, source_target_pairs={{0,8},{1,9},{2,10},{3,11},{4,12},{5,13},{6,14},{7,15},{8,0},{9,1},... | collective-permute-start | bytes 2359304 | tf_op jit(solution)/shard_map/ppermute | solution.py:44
  26.6 21.7 %collective-permute-start.2 = (bf16[4,32,2304]{2,1,0:T(8,128)(2,1)S(1)}, bf16[4,32,2304]{2,1,0:T(8,128)(2,1)S(1)}, u32[]{:S(2)}, u32[]{:S(2)}) collective-permute-start(bf16[4,32,2304]{2,1,0:T(8,128)(2,1)S(1)} %get-tuple-element.46.refs_6_), channel_id=1, source_target_pairs={{0,2},{1,3},{2,0},{3,1},{4,6},{5,7},{6,4},{7,5},{8,10},{9,11},{10,... | collective-permute-start | bytes 1769480 | tf_op jit(solution)/shard_map/ppermute | solution.py:44
  27.2 25.6 %collective-permute-start.4 = (bf16[4,32,2560]{2,1,0:T(8,128)(2,1)S(1)}, bf16[4,32,2560]{2,1,0:T(8,128)(2,1)S(1)}, u32[]{:S(2)}, u32[]{:S(2)}) collective-permute-start(bf16[4,32,2560]{2,1,0:T(8,128)(2,1)S(1)} %get-tuple-element.48), channel_id=1, source_target_pairs={{0,8},{1,9},{2,10},{3,11},{4,12},{5,13},{6,14},{7,15},{8,0},{9,1},... | collective-permute-start | bytes 1966088 | tf_op jit(solution)/shard_map/ppermute | solution.py:44
  35.7 14.0 %collective-permute-start.3 = (bf16[4,32,2304]{2,1,0:T(8,128)(2,1)S(1)}, bf16[4,32,2304]{2,1,0:T(8,128)(2,1)S(1)}, u32[]{:S(2)}, u32[]{:S(2)}) collective-permute-start(bf16[4,32,2304]{2,1,0:T(8,128)(2,1)S(1)} %get-tuple-element.47), channel_id=1, source_target_pairs={{0,6},{1,7},{2,4},{3,5},{4,2},{5,3},{6,0},{7,1},{8,14},{9,15},{10,... | collective-permute-start | bytes 1769480 | tf_op jit(solution)/shard_map/ppermute | solution.py:44
  43.3 14.9 %collective-permute-start.11 = (bf16[2,32,3072]{2,1,0:T(8,128)(2,1)S(1)}, bf16[2,32,3072]{2,1,0:T(8,128)(2,1)S(1)}, u32[]{:S(2)}, u32[]{:S(2)}) collective-permute-start(bf16[2,32,3072]{2,1,0:T(8,128)(2,1)S(1)} %get-tuple-element.51.refs_6_), channel_id=1, source_target_pairs={{0,6},{1,7},{2,4},{3,5},{4,2},{5,3},{6,0},{7,1},{8,14},{9,15},{10,... | collective-permute-start | bytes 1179656 | tf_op jit(solution)/shard_map/ppermute | solution.py:44
  44.5 16.6 %collective-permute-start.12 = (bf16[2,32,3072]{2,1,0:T(8,128)(2,1)S(1)}, bf16[2,32,3072]{2,1,0:T(8,128)(2,1)S(1)}, u32[]{:S(2)}, u32[]{:S(2)}) collective-permute-start(bf16[2,32,3072]{2,1,0:T(8,128)(2,1)S(1)} %get-tuple-element.55), channel_id=1, source_target_pairs={{0,8},{1,9},{2,10},{3,11},{4,12},{5,13},{6,14},{7,15},{8,0},{9,1},... | collective-permute-start | bytes 1179656 | tf_op jit(solution)/shard_map/ppermute | solution.py:44
  48.3 12.8 %collective-permute-start.13 = (bf16[2,32,3072]{2,1,0:T(8,128)(2,1)S(1)}, bf16[2,32,3072]{2,1,0:T(8,128)(2,1)S(1)}, u32[]{:S(2)}, u32[]{:S(2)}) collective-permute-start(bf16[2,32,3072]{2,1,0:T(8,128)(2,1)S(1)} %get-tuple-element.56), channel_id=1, source_target_pairs={{0,2},{1,3},{2,0},{3,1},{4,6},{5,7},{6,4},{7,5},{8,10},{9,11},{10,... | collective-permute-start | bytes 1179656 | tf_op jit(solution)/shard_map/ppermute | solution.py:44
  55.5 11.0 %collective-permute-start.8 = (bf16[2,32,2304]{2,1,0:T(8,128)(2,1)S(1)}, bf16[2,32,2304]{2,1,0:T(8,128)(2,1)S(1)}, u32[]{:S(2)}, u32[]{:S(2)}) collective-permute-start(bf16[2,32,2304]{2,1,0:T(8,128)(2,1)S(1)} %get-tuple-element.52.refs_9_), channel_id=1, source_target_pairs={{0,6},{1,7},{2,4},{3,5},{4,2},{5,3},{6,0},{7,1},{8,14},{9,15},{10,... | collective-permute-start | bytes 884744 | tf_op jit(solution)/shard_map/ppermute | solution.py:44
  56.4 11.1 %collective-permute-start.10 = (bf16[2,32,2560]{2,1,0:T(8,128)(2,1)S(1)}, bf16[2,32,2560]{2,1,0:T(8,128)(2,1)S(1)}, u32[]{:S(2)}, u32[]{:S(2)}) collective-permute-start(bf16[2,32,2560]{2,1,0:T(8,128)(2,1)S(1)} %get-tuple-element.54), channel_id=1, source_target_pairs={{0,2},{1,3},{2,0},{3,1},{4,6},{5,7},{6,4},{7,5},{8,10},{9,11},{10,... | collective-permute-start | bytes 983048 | tf_op jit(solution)/shard_map/ppermute | solution.py:44
  58.1 9.3 %collective-permute-start.9 = (bf16[2,32,2304]{2,1,0:T(8,128)(2,1)S(1)}, bf16[2,32,2304]{2,1,0:T(8,128)(2,1)S(1)}, u32[]{:S(2)}, u32[]{:S(2)}) collective-permute-start(bf16[2,32,2304]{2,1,0:T(8,128)(2,1)S(1)} %get-tuple-element.53), channel_id=1, source_target_pairs={{0,8},{1,9},{2,10},{3,11},{4,12},{5,13},{6,14},{7,15},{8,0},{9,1},... | collective-permute-start | bytes 884744 | tf_op jit(solution)/shard_map/ppermute | solution.py:44
  64.7 7.1 %collective-permute-start.17 = (bf16[32,3072]{1,0:T(8,128)(2,1)S(1)}, bf16[32,3072]{1,0:T(8,128)(2,1)S(1)}, u32[]{:S(2)}, u32[]{:S(2)}) collective-permute-start(bf16[32,3072]{1,0:T(8,128)(2,1)S(1)} %get-tuple-element.57.refs_9_), channel_id=1, source_target_pairs={{0,8},{1,9},{2,10},{3,11},{4,12},{5,13},{6,14},{7,15},{8,0},{9,1},... | collective-permute-start | bytes 589832 | tf_op jit(solution)/shard_map/ppermute | solution.py:44
  69.8 7.4 %collective-permute-start.16 = (bf16[32,2560]{1,0:T(8,128)(2,1)S(1)}, bf16[32,2560]{1,0:T(8,128)(2,1)S(1)}, u32[]{:S(2)}, u32[]{:S(2)}) collective-permute-start(bf16[32,2560]{1,0:T(8,128)(2,1)S(1)} %get-tuple-element.60), channel_id=1, source_target_pairs={{0,6},{1,7},{2,4},{3,5},{4,2},{5,3},{6,0},{7,1},{8,14},{9,15},{10,... | collective-permute-start | bytes 491528 | tf_op jit(solution)/shard_map/ppermute | solution.py:44
  80.5 7.7 %collective-permute-start.22 = (bf16[32,5760]{1,0:T(8,128)(2,1)S(1)}, bf16[32,5760]{1,0:T(8,128)(2,1)S(1)}, u32[]{:S(2)}, u32[]{:S(2)}) collective-permute-start(bf16[32,5760]{1,0:T(8,128)(2,1)S(1)} %get-tuple-element.71.refs_3_), channel_id=1, source_target_pairs={{0,6},{1,7},{2,4},{3,5},{4,2},{5,3},{6,0},{7,1},{8,14},{9,15},{10,... | collective-permute-start | bytes 1105928 | tf_op jit(solution)/shard_map/ppermute | solution.py:44
  82.8 6.5 %collective-permute-start.21 = (bf16[32,5376]{1,0:T(8,128)(2,1)S(1)}, bf16[32,5376]{1,0:T(8,128)(2,1)S(1)}, u32[]{:S(2)}, u32[]{:S(2)}) collective-permute-start(bf16[32,5376]{1,0:T(8,128)(2,1)S(1)} %get-tuple-element.70.refs_2_), channel_id=1, source_target_pairs={{0,2},{1,3},{2,0},{3,1},{4,6},{5,7},{6,4},{7,5},{8,10},{9,11},{10,... | collective-permute-start | bytes 1032200 | tf_op jit(solution)/shard_map/ppermute | solution.py:44
  83.2 9.6 %collective-permute-start.23 = (bf16[32,5376]{1,0:T(8,128)(2,1)S(1)}, bf16[32,5376]{1,0:T(8,128)(2,1)S(1)}, u32[]{:S(2)}, u32[]{:S(2)}) collective-permute-start(bf16[32,5376]{1,0:T(8,128)(2,1)S(1)} %get-tuple-element.69.refs_1_), channel_id=1, source_target_pairs={{0,6},{1,7},{2,4},{3,5},{4,2},{5,3},{6,0},{7,1},{8,14},{9,15},{10,... | collective-permute-start | bytes 1032200 | tf_op jit(solution)/shard_map/ppermute | solution.py:44
  85.0 12.6 %collective-permute-start.25 = (bf16[32,5760]{1,0:T(8,128)(2,1)S(1)}, bf16[32,5760]{1,0:T(8,128)(2,1)S(1)}, u32[]{:S(2)}, u32[]{:S(2)}) collective-permute-start(bf16[32,5760]{1,0:T(8,128)(2,1)S(1)} %get-tuple-element.71.refs_3_), channel_id=1, source_target_pairs={{0,2},{1,3},{2,0},{3,1},{4,6},{5,7},{6,4},{7,5},{8,10},{9,11},{10,... | collective-permute-start | bytes 1105928 | tf_op jit(solution)/shard_map/ppermute | solution.py:44
  88.1 14.4 %collective-permute-start.28 = (bf16[32,5760]{1,0:T(8,128)(2,1)S(1)}, bf16[32,5760]{1,0:T(8,128)(2,1)S(1)}, u32[]{:S(2)}, u32[]{:S(2)}) collective-permute-start(bf16[32,5760]{1,0:T(8,128)(2,1)S(1)} %collective-permute-done.22.refs_6_), channel_id=1, source_target_pairs={{0,2},{1,3},{2,0},{3,1},{4,6},{5,7},{6,4},{7,5},{8,10},{9,11},{10,... | collective-permute-start | bytes 1105928 | tf_op jit(solution)/shard_map/ppermute | solution.py:44
  88.7 8.9 %collective-permute-start.24 = (bf16[32,5376]{1,0:T(8,128)(2,1)S(1)}, bf16[32,5376]{1,0:T(8,128)(2,1)S(1)}, u32[]{:S(2)}, u32[]{:S(2)}) collective-permute-start(bf16[32,5376]{1,0:T(8,128)(2,1)S(1)} %get-tuple-element.70.refs_2_), channel_id=1, source_target_pairs={{0,8},{1,9},{2,10},{3,11},{4,12},{5,13},{6,14},{7,15},{8,0},{9,1},... | collective-permute-start | bytes 1032200 | tf_op jit(solution)/shard_map/ppermute | solution.py:44
  89.3 11.4 %collective-permute-start.26 = (bf16[32,5376]{1,0:T(8,128)(2,1)S(1)}, bf16[32,5376]{1,0:T(8,128)(2,1)S(1)}, u32[]{:S(2)}, u32[]{:S(2)}) collective-permute-start(bf16[32,5376]{1,0:T(8,128)(2,1)S(1)} %collective-permute-done.20.refs_4_), channel_id=1, source_target_pairs={{0,6},{1,7},{2,4},{3,5},{4,2},{5,3},{6,0},{7,1},{8,14},{9,15},{10,... | collective-permute-start | bytes 1032200 | tf_op jit(solution)/shard_map/ppermute | solution.py:44
  92.9 9.6 %collective-permute-start.27 = (bf16[32,5376]{1,0:T(8,128)(2,1)S(1)}, bf16[32,5376]{1,0:T(8,128)(2,1)S(1)}, u32[]{:S(2)}, u32[]{:S(2)}) collective-permute-start(bf16[32,5376]{1,0:T(8,128)(2,1)S(1)} %collective-permute-done.21.refs_5_), channel_id=1, source_target_pairs={{0,8},{1,9},{2,10},{3,11},{4,12},{5,13},{6,14},{7,15},{8,0},{9,1},... | collective-permute-start | bytes 1032200 | tf_op jit(solution)/shard_map/ppermute | solution.py:44
  104.9 14.5 %collective-permute-start.36 = (bf16[4,32,9216]{2,1,0:T(8,128)(2,1)S(1)}, bf16[4,32,9216]{2,1,0:T(8,128)(2,1)S(1)}, u32[]{:S(2)}, u32[]{:S(2)}) collective-permute-start(bf16[4,32,9216]{2,1,0:T(8,128)(2,1)S(1)} %get-tuple-element.79), channel_id=1, source_target_pairs={{0,1},{1,0},{2,3},{3,2},{4,5},{5,4},{6,7},{7,6},{8,9},{9,8},{10,11... | collective-permute-start | bytes 7077896 | tf_op jit(solution)/shard_map/ppermute | solution.py:44
  115.9 10.6 %collective-permute-start.35 = (bf16[4,32,7296]{2,1,0:T(8,128)(2,1)S(1)}, bf16[4,32,7296]{2,1,0:T(8,128)(2,1)S(1)}, u32[]{:S(2)}, u32[]{:S(2)}) collective-permute-start(bf16[4,32,7296]{2,1,0:T(8,128)(2,1)S(1)} %get-tuple-element.78), channel_id=1, source_target_pairs={{0,1},{1,0},{2,3},{3,2},{4,5},{5,4},{6,7},{7,6},{8,9},{9,8},{10,11... | collective-permute-start | bytes 5603336 | tf_op jit(solution)/shard_map/ppermute | solution.py:44
  116.0 18.8 %collective-permute-start.32 = (bf16[4,32,3072]{2,1,0:T(8,128)(2,1)S(1)}, bf16[4,32,3072]{2,1,0:T(8,128)(2,1)S(1)}, u32[]{:S(2)}, u32[]{:S(2)}) collective-permute-start(bf16[4,32,3072]{2,1,0:T(8,128)(2,1)S(1)} %get-tuple-element.72.refs_13_.refs_0_), channel_id=1, source_target_pairs={{0,2},{1,3},{2,0},{3,1},{4,6},{5,7},{6,4},{7,5},{8,10},{9,11},{10,... | collective-permute-start | bytes 2359304 | tf_op jit(solution)/shard_map/ppermute | solution.py:44
  116.7 19.6 %collective-permute-start.33 = (bf16[4,32,3072]{2,1,0:T(8,128)(2,1)S(1)}, bf16[4,32,3072]{2,1,0:T(8,128)(2,1)S(1)}, u32[]{:S(2)}, u32[]{:S(2)}) collective-permute-start(bf16[4,32,3072]{2,1,0:T(8,128)(2,1)S(1)} %get-tuple-element.76.refs_1_), channel_id=1, source_target_pairs={{0,6},{1,7},{2,4},{3,5},{4,2},{5,3},{6,0},{7,1},{8,14},{9,15},{10,... | collective-permute-start | bytes 2359304 | tf_op jit(solution)/shard_map/ppermute | solution.py:44
  119.4 18.1 %collective-permute-start.34 = (bf16[4,32,3072]{2,1,0:T(8,128)(2,1)S(1)}, bf16[4,32,3072]{2,1,0:T(8,128)(2,1)S(1)}, u32[]{:S(2)}, u32[]{:S(2)}) collective-permute-start(bf16[4,32,3072]{2,1,0:T(8,128)(2,1)S(1)} %get-tuple-element.77.refs_2_), channel_id=1, source_target_pairs={{0,8},{1,9},{2,10},{3,11},{4,12},{5,13},{6,14},{7,15},{8,0},{9,1},... | collective-permute-start | bytes 2359304 | tf_op jit(solution)/shard_map/ppermute | solution.py:44
  139.8 17.2 %collective-permute-start.31 = (bf16[4,32,2688]{2,1,0:T(8,128)(2,1)S(1)}, bf16[4,32,2688]{2,1,0:T(8,128)(2,1)S(1)}, u32[]{:S(2)}, u32[]{:S(2)}) collective-permute-start(bf16[4,32,2688]{2,1,0:T(8,128)(2,1)S(1)} %get-tuple-element.75.refs_2_.refs_6_), channel_id=1, source_target_pairs={{0,8},{1,9},{2,10},{3,11},{4,12},{5,13},{6,14},{7,15},{8,0},{9,1},... | collective-permute-start | bytes 2064392 | tf_op jit(solution)/shard_map/ppermute | solution.py:44
  139.8 14.6 %collective-permute-start.29 = (bf16[4,32,2304]{2,1,0:T(8,128)(2,1)S(1)}, bf16[4,32,2304]{2,1,0:T(8,128)(2,1)S(1)}, u32[]{:S(2)}, u32[]{:S(2)}) collective-permute-start(bf16[4,32,2304]{2,1,0:T(8,128)(2,1)S(1)} %get-tuple-element.73.refs_5_.refs_0_), channel_id=1, source_target_pairs={{0,2},{1,3},{2,0},{3,1},{4,6},{5,7},{6,4},{7,5},{8,10},{9,11},{10,... | collective-permute-start | bytes 1769480 | tf_op jit(solution)/shard_map/ppermute | solution.py:44
  141.2 15.8 %collective-permute-start.30 = (bf16[4,32,2304]{2,1,0:T(8,128)(2,1)S(1)}, bf16[4,32,2304]{2,1,0:T(8,128)(2,1)S(1)}, u32[]{:S(2)}, u32[]{:S(2)}) collective-permute-start(bf16[4,32,2304]{2,1,0:T(8,128)(2,1)S(1)} %get-tuple-element.74.refs_1_), channel_id=1, source_target_pairs={{0,6},{1,7},{2,4},{3,5},{4,2},{5,3},{6,0},{7,1},{8,14},{9,15},{10,... | collective-permute-start | bytes 1769480 | tf_op jit(solution)/shard_map/ppermute | solution.py:44
  (16 other events, 100.2 us)

commit v3 on v2

v3 whole, which is shorter than its diff:
```python
import functools

import jax
import jax.numpy as jnp
from jax import lax
from jax.experimental import pallas as pl
from jax.experimental.pallas import tpu as pltpu
from jax.sharding import PartitionSpec as P

NZ, NY, NC = 2, 4, 2
ROWS = 32
D = 16384
COLS = 640
NOTE = 128
ANY = pl.BlockSpec(memory_space=pl.ANY)
VMEM = pl.BlockSpec(memory_space=pltpu.VMEM)
MIB = 1024 * 1024
SUM_BYTES = 45 * MIB
ROW_BYTES = 16 * MIB
PRODUCT_BYTES = 41 * MIB


def index_of(z, y, c):
    return (z * NY + y % NY) * NC + c


def pairs(move):
    return [
        (index_of(z, y, c), index_of(*move(z, y, c)))
        for z in range(NZ)
        for y in range(NY)
        for c in range(NC)
    ]


MOVES = {"a": (0, 1), "b": (0, 3), "z": (1, 0)}
TO = {d: pairs(lambda z, y, c, m=m: (z ^ m[0], y ^ m[1], c)) for d, m in MOVES.items()}
TO_CORE = pairs(lambda z, y, c: (z, y, 1 - c))


def send(x, where):
    return lax.ppermute(x, "tensor", where)


def bf16(x):
    return x.astype(jnp.bfloat16)


def shape(*dims, dtype=jnp.bfloat16):
    return jax.ShapeDtypeStruct(dims, dtype)


class Copies:
    def __init__(self, sems):
        self.sems, self.count = sems, 0

    def start(self, source, target):
        copy = pltpu.make_async_copy(source, target, self.sems.at[self.count])
        self.count += 1
        copy.start()
        return copy


def by_columns(width, body):
    step = 512 if width % 512 == 0 else 256

    def at(i, carry):
        return body(pl.ds(pl.multiple_of(i * step, step), step), carry)

    return functools.partial(lax.fori_loop, 0, width // step, at)


def total_of(sources, columns):
    total = sources[0][:, columns].astype(jnp.float32)
    for ref in sources[1:]:
        total = total + ref[:, columns].astype(jnp.float32)
    return total


def where_am_i():
    t = lax.axis_index("tensor")
    return t // (NY * NC), t // NC % NY, t % NC


def call(name, kernel, ins, outs, scratch, copies, after, aliases={}, limit=SUM_BYTES):
    return pl.pallas_call(
        lambda *refs: kernel(where_am_i(), *refs),
        in_specs=[ANY] * (len(ins) - 1 + len(after)),
        out_specs=[ANY] * len(outs),
        name=name,
        out_shape=outs,
        scratch_shapes=scratch + [pltpu.SemaphoreType.DMA((copies,))],
        input_output_aliases=aliases,
        compiler_params=pltpu.CompilerParams(vmem_limit_bytes=limit),
        cost_estimate=pl.CostEstimate(flops=0, bytes_accessed=1024, transcendentals=0),
    )(*ins[1:], *after)


def copied(name, ins, outs, items, after):
    n = len(ins)

    def kernel(*refs):
        place, sources = refs[0], refs[1:n]
        targets, sems = refs[n + len(after) : -1], refs[-1]
        copies = Copies(sems)
        going = [
            copies.start(source, targets[k].at[index])
            for k, index, source in items(place, sources)
        ]
        for copy in going:
            copy.wait()

    return call(name, kernel, ins, outs, [], 36, after, limit=ROW_BYTES)


def added(name, ins, steps, others, stream, after):
    n, count = len(ins), len(steps)
    most = 1 + len(others([None] * n, 0))
    widest = max(part.features for part in stream.parts)

    def kernel(*refs):
        at, x, targets = refs[0], refs[1], refs[n + len(after) : n + len(after) + 3]
        taken, made, sems = refs[-3:]
        copies = Copies(sems)
        loads, storing = [], []
        for k, part in enumerate(stream.parts):
            inside = pl.ds(0, part.features)
            going = []
            for e, step in enumerate(steps):
                source = x.at[block(at, part.apart(*step), 0), :, part.columns]
                going.append(copies.start(source, taken.at[0, k, e, :, inside]))
            for j, source in enumerate(others(refs, k)):
                going.append(copies.start(source, taken.at[1 + j, k, :, :, inside]))
            loads.append(going)
        for k, part in enumerate(stream.parts):
            for copy in loads[k]:
                copy.wait()

            def one(e, carry, k=k, width=part.features):
                def body(columns, carry):
                    total = taken[0, k, e, :, columns].astype(jnp.float32)
                    for j in range(1, most):
                        total = total + taken[j, k, e, :, columns].astype(jnp.float32)
                    made[k, e, :, columns] = bf16(total)
                    return carry

                return by_columns(width, body)(carry)

            lax.fori_loop(0, count, one, 0)
            source = made.at[k, :, :, pl.ds(0, part.features)]
            storing.append(copies.start(source, targets[k]))
        for copy in storing:
            copy.wait()

    scratch = [
        pltpu.VMEM((most, 3, count, ROWS, widest), jnp.bfloat16),
        pltpu.VMEM((3, count, ROWS, widest), jnp.bfloat16),
    ]
    outs = [shape(count, ROWS, part.features) for part in stream.parts]
    return call(name, kernel, ins, outs, scratch, 3 * (count + most), after)


class Part:
    def __init__(self, start, features, dims, note=0):
        self.start, self.features, self.note = start, features, note
        self.sent = features + note
        self.columns = pl.ds(start, features)
        self.dims = dims

    def apart(self, *steps):
        z = y = 0
        for d, step in zip(self.dims, steps):
            if step:
                z, y = z ^ MOVES[d][0], y ^ MOVES[d][1]
        return z, y


class Stream:
    def __init__(self, parts, before):
        self.parts, self.before = parts, before
        self.features = sum(p.features for p in parts)
        self.note = sum(p.note for p in parts)
        self.offsets = [sum(p.features for p in parts[:k]) for k in range(len(parts))]

    def local(self, k, extra=False):
        return pl.ds(self.offsets[k], self.parts[k].sent if extra else self.parts[k].features)

    def beside(self, k):
        return pl.ds(sum(WIDTHS[:k]) + self.before[k], self.parts[k].sent)

    def place_of(self, k):
        return pl.ds(self.before[k], self.parts[k].sent)


def row_block(place, apart):
    z, y = place[0], place[1]
    return lax.bitwise_xor(z, apart[0]) * NY + lax.bitwise_xor(y, apart[1])


def block(place, apart, dc):
    c = place[2]
    return row_block(place, apart) * NC + lax.bitwise_xor(c, dc)


def give(place, terms, wanted, width, after):
    def items(at, x):
        return [
            (
                (e2 * 2 + e3, slice(None), pl.ds(position, part.features)),
                x.at[block(at, part.apart(first, e2, e3), 1), :, part.columns],
            )
            for part, first, position in wanted
            for e2 in (1, 0)
            for e3 in (0, 1)
        ]

    def kernel(*refs):
        at, x = refs[:2]
        target, held, sems = refs[-3:]
        copies = Copies(sems)
        todo = []
        for index, source in items(at, x):
            todo.append((index, copies.start(source, held.at[index])))
        storing = []
        for index, copy in todo:
            copy.wait()
            storing.append(copies.start(held.at[index], target.at[index]))
        for copy in storing:
            copy.wait()

    scratch = [pltpu.VMEM((4, ROWS, width), jnp.bfloat16)]
    out = shape(4, ROWS, width)
    return call("give", kernel, [place, terms], [out], scratch, 8 * len(wanted), after)


def from_core(ref, blocks, position, part):
    if ref is None:
        return None
    return ref.at[blocks, :, pl.ds(position, part.features)]


def pick(ref, index):
    return None if ref is None else ref.at[index]


QUARTERS = ((0, 0), (0, 1), (1, 0), (1, 1))


def first_step(place, terms, got, offset, stream, after):
    def others(refs, k):
        return [from_core(refs[2], pl.ds(0, 4), offset + stream.offsets[k], stream.parts[k])]

    steps = [(1, *q) for q in QUARTERS]
    return added("first", [place, terms, got], steps, others, stream, after)


def second_step(place, terms, rest, one, stream, after):
    def others(refs, k):
        some = pl.ds(2, 2)
        return [from_core(refs[2], some, stream.parts[k].start, stream.parts[k]), pick(refs[3 + k], some)]

    steps = [(0, 1, 0), (0, 1, 1)]
    return added("second", [place, terms, rest, *one], steps, others, stream, after)


def third_step(place, terms, rest, one, two, stream, after):
    def others(refs, k):
        some = pl.ds(1, 1)
        got = from_core(refs[2], some, stream.parts[k].start, stream.parts[k])
        return [got, pick(refs[3 + k], some), pick(refs[6 + k], some)]

    steps = [(0, 0, 1)]
    return added("third", [place, terms, rest, *one, *two], steps, others, stream, after)


def finish(place, terms, rest, one, two, three, stream, residual, gain, so_far, after):
    ins = [place, terms, rest, *one, *two, *three, residual, gain, *so_far]
    widest = max(part.features for part in stream.parts)

    def kernel(*refs):
        at, x = refs[0], refs[1]
        r, v, w, u = refs[2], refs[3:6], refs[6:9], refs[9:12]
        residual_ref, gain_ref = refs[12:14]
        base = len(ins) + len(after)
        stream_out, gained_out, squares_out = refs[base], refs[base + 1 : base + 4], refs[base + 4]
        taken, old, gains, news, made, sums, sems = refs[base + 5 :]
        copies = Copies(sems)
        first = []
        for k, part in enumerate(stream.parts):
            here = stream.local(k)
            first.append(copies.start(residual_ref.at[:, part.columns], old.at[:, here]))
            first.append(copies.start(gain_ref.at[:, part.columns], gains.at[:, here]))
        if so_far:
            first.append(copies.start(refs[18], sums))
        else:
            sums[...] = jnp.zeros_like(sums)
        loads, slots = [], []
        for k, part in enumerate(stream.parts):
            mine = x.at[block(at, part.apart(0, 0, 0), 0), :, part.columns]
            blocks = [mine, from_core(r, 0, part.start, part), v[k].at[0], w[k].at[0], u[k].at[0]]
            slots.append([taken.at[k, j, :, pl.ds(0, part.features)] for j in range(5)])
            loads.append([copies.start(b, s) for b, s in zip(blocks, slots[k])])
        for copy in first:
            copy.wait()
        total = sums[...]
        storing = []
        for k, part in enumerate(stream.parts):
            for copy in loads[k]:
                copy.wait()

            def body(columns, carry, k=k, offset=stream.offsets[k]):
                here = pl.ds(pl.multiple_of(offset + columns.start, 128), columns.size)
                x = total_of(slots[k], columns) + old[:, here].astype(jnp.float32)
                news[:, here] = bf16(x)
                made[k, :, columns] = bf16(x * gains[:, here])
                square = x * x
                return carry + sum(square[:, i : i + 128] for i in range(0, columns.size, 128))

            total = by_columns(part.features, body)(total)
            here = news.at[:, stream.local(k)]
            storing.append(copies.start(here, stream_out.at[:, part.columns]))
            if not part.note:
                here = made.at[k, :, pl.ds(0, part.features)]
                storing.append(copies.start(here, gained_out[k].at[:, stream.place_of(k)]))
        sums[...] = total
        storing.append(copies.start(sums, squares_out))
        for k, part in enumerate(stream.parts):
            if part.note:
                mean = jnp.sum(total, axis=1, keepdims=True) / D
                scale = jnp.broadcast_to(lax.rsqrt(mean + 1e-05), (ROWS, NOTE))
                high = bf16(scale).astype(jnp.float32)
                middle = bf16(scale - high).astype(jnp.float32)
                low = scale - high - middle
                lane = lax.broadcasted_iota(jnp.int32, (ROWS, NOTE), 1)
                parts = jnp.where(lane == 0, high, jnp.where(lane == 1, middle, low))
                made[k, :, pl.ds(part.features, NOTE)] = bf16(jnp.where(lane < 3, parts, 0.0))
                here = made.at[k, :, pl.ds(0, part.sent)]
                storing.append(copies.start(here, gained_out[k].at[:, stream.place_of(k)]))
        for copy in storing:
            copy.wait()

    outs = [shape(ROWS, D)]
    outs += [shape(ROWS, w) for w in WIDTHS]
    outs += [shape(ROWS, 128, dtype=jnp.float32)]
    scratch = [
        pltpu.VMEM((3, 5, ROWS, widest), jnp.bfloat16),
        pltpu.VMEM((ROWS, stream.features), jnp.bfloat16),
        pltpu.VMEM((1, stream.features), jnp.float32),
        pltpu.VMEM((ROWS, stream.features), jnp.bfloat16),
        pltpu.VMEM((3, ROWS, widest + NOTE), jnp.bfloat16),
        pltpu.VMEM((ROWS, 128), jnp.float32),
    ]
    aliases = {13: 0, 14: 1, 15: 2, 16: 3} if so_far else {}
    out = call("finish", kernel, ins, outs, scratch, 3 * 5 + 14, after, aliases)
    return out


def four_blocks(place, held, after):
    def items(at, refs):
        found = []
        for i, stream in enumerate((ONE, TWO)):
            for k in range(3):
                for e in range(4):
                    found.append((3 * i + k, e, refs[e * 3 + k].at[:, stream.place_of(k)]))
        for k in range(3):
            for e in range(4):
                to = pl.ds(sum(WIDTHS[:k]), WIDTHS[k])
                found.append((6, (e, slice(None), to), refs[e * 3 + k]))
        return found

    outs = [shape(4, ROWS, part.sent) for s in (ONE, TWO) for part in s.parts]
    outs.append(shape(4, ROWS, sum(WIDTHS)))
    out = copied("four", [place, *held], outs, items, after)
    return out[:3], out[3:6], out[6]


def multiplied(place, side, own, other, weight, total, stream, notes, after):
    last = bool(notes)
    half = NZ * NY * ROWS
    ins = [*own, *other, *notes]
    n = len(ins)
    more = [] if total is None else [total]

    def position(part, e1, e2, e3, c):
        z, y = part.apart(e1, e2, e3)
        return pl.ds((c * NZ * NY + z * NY + y) * ROWS, ROWS)

    def kernel(*refs):
        weight_ref = refs[n]
        at = n + 1 + len(more) + len(after)
        target = refs[at]
        rows, held, out, sems = refs[at + 1], refs[at + 2], refs[at + 3], refs[-1]
        copies = Copies(sems)
        loads = []
        for k, part in enumerate(stream.parts):
            columns = stream.local(k, True)
            half_depth = part.features // 2
            going = []
            for h in range(2):
                there = pl.ds(part.start + h * half_depth, half_depth)
                here = pl.ds(stream.offsets[k] + h * half_depth, half_depth)
                going.append(copies.start(weight_ref.at[there], held.at[here]))
            for e in range(4):
                to = rows.at[pl.ds(e * ROWS, ROWS), columns]
                going.append(copies.start(refs[k].at[e], to))
                source = refs[3 + k].at[e] if len(other) > 1 else refs[3].at[e, :, stream.beside(k)]
                to = rows.at[pl.ds((4 + e) * ROWS, ROWS), columns]
                going.append(copies.start(source, to))
            loads.append(going)
        if last:
            part = stream.parts[2]
            near, beside, notes_held = refs[n - 2], refs[n - 1], refs[at + 4]
            first = [
                copies.start(near.at[:, :, pl.ds(part.features, NOTE)], notes_held.at[0]),
                copies.start(beside.at[:, :, pl.ds(sum(WIDTHS) - NOTE, NOTE)], notes_held.at[1]),
            ]
        if more:
            before = copies.start(refs[n + 1], out)
        else:
            out[...] = jnp.zeros_like(out)
        for k, part in enumerate(stream.parts):
            half_depth = part.features // 2
            start = stream.offsets[k]
            for copy in [loads[k][0], *loads[k][2:]]:
                copy.wait()
            here = pl.ds(start, half_depth)
            product = jnp.dot(rows[:, here], held[here, :], preferred_element_type=jnp.float32)
            loads[k][1].wait()
            here = pl.ds(start + half_depth, half_depth)
            product += jnp.dot(rows[:, here], held[here, :], preferred_element_type=jnp.float32)
            if more and k == 0:
                before.wait()
            for c in range(NC):
                for e in range(4):
                    some = (c * 4 + e) * ROWS
                    out[position(part, side, e // 2, e % 2, c), :] += product[some : some + ROWS]
        if not last:
            copies.start(out, target).wait()
        else:
            for copy in first:
                copy.wait()
            part, place_now = stream.parts[2], where_am_i()
            for e1 in range(2):
                for e in range(4):
                    for c in range(NC):
                        if e1 == side:
                            some = pl.ds((c * 4 + e) * ROWS, ROWS)
                            note = rows[some, pl.ds(stream.features, NOTE)]
                        else:
                            note = notes_held[c, e]
                        scale = jnp.sum(note.astype(jnp.float32), axis=1, keepdims=True)
                        apart = part.apart(e1, e // 2, e % 2)
                        to = row_block(place_now, apart) * NC + lax.bitwise_xor(place_now[2], c)
                        to = pl.ds(pl.multiple_of(to * ROWS, ROWS), ROWS)
                        here = position(part, e1, e // 2, e % 2, c)
                        target[to, :] = bf16(out[here, :] * scale)

    scratch = [
        pltpu.VMEM((half, stream.features + stream.note), jnp.bfloat16),
        pltpu.VMEM((stream.features, COLS), jnp.bfloat16),
    ]
    scratch.append(pltpu.VMEM((2 * half, COLS), jnp.float32))
    if last:
        scratch.append(pltpu.VMEM((NC, 4, ROWS, NOTE), jnp.bfloat16))
    dtype = jnp.bfloat16 if last else jnp.float32
    return pl.pallas_call(
        kernel,
        in_specs=[ANY] * (n + 1 + len(more) + len(after)),
        name="multiply",
        out_specs=VMEM if last else ANY,
        out_shape=shape(2 * half, COLS, dtype=dtype),
        scratch_shapes=scratch + [pltpu.SemaphoreType.DMA((34,))],
        compiler_params=pltpu.CompilerParams(vmem_limit_bytes=PRODUCT_BYTES),
        cost_estimate=pl.CostEstimate(flops=0, bytes_accessed=1024, transcendentals=0),
    )(*ins, weight, *more, *after)


ORDERS = (("a", "b", "z"), ("b", "z", "a"), ("z", "a", "b"))


def streams_of(first, second, note):
    runs, start = ([], []), 0
    for k, dims in enumerate(ORDERS):
        runs[0].append(Part(start, first[k], dims))
        runs[1].append(Part(start + first[k], second[k], dims, note if k == 2 else 0))
        start += first[k] + second[k]
    return Stream(runs[0], (0, 0, 0)), Stream(runs[1], first)


FIRST, SECOND = streams_of((2560, 4096, 4096), (3072, 1024, 1536), NOTE)
ONE, TWO = streams_of((4096, 4096, 4096), (1536, 1024, 1536), NOTE)
WIDTHS = [a.sent + b.sent for a, b in zip(FIRST.parts, SECOND.parts)]


def per_device(partials, residual, norm_gain, qkv_weight):
    place = None
    terms = partials.reshape(NZ * NY * NC, ROWS, D)
    gain = norm_gain.astype(jnp.float32).reshape(1, D)

    def along(step, arrays):
        return [send(x, TO[ORDERS[k][step]]) for k, x in enumerate(arrays)]

    def across(arrays):
        return [send(x, TO_CORE) for x in arrays]

    a, b = FIRST, SECOND
    wanted = [(part, 1, a.offsets[k]) for k, part in enumerate(a.parts)]
    a_give = give(place, terms, wanted, a.features, [])
    a_got = across(a_give)[0]
    wanted = [(part, 0, part.start) for part in (*a.parts, *b.parts)]
    wanted += [(part, 1, D + b.offsets[k]) for k, part in enumerate(b.parts)]
    give_rest = give(place, terms, wanted, D + b.features, [a_give[0]])
    give_rest, _ = lax.optimization_barrier((give_rest[0], a_got))
    rest = send(give_rest, TO_CORE)
    a_out = first_step(place, terms, a_got, 0, a, [give_rest])
    a_one = along(0, a_out)
    b_out = first_step(place, terms, rest, D, b, [a_out[0]])
    b_one = along(0, b_out)
    a_out = second_step(place, terms, rest, a_one, a, [b_out[0]])
    a_two = along(1, a_out)
    b_out = second_step(place, terms, rest, b_one, b, [a_out[0]])
    b_two = along(1, b_out)
    a_out = third_step(place, terms, rest, a_one, a_two, a, [b_out[0]])
    a_three = along(2, a_out)
    b_out = third_step(place, terms, rest, b_one, b_two, b, [a_out[0]])
    b_three = along(2, b_out)
    so_far = finish(
        place, terms, rest, a_one, a_two, a_three, a, residual, gain, (), [b_out[0]]
    )
    stream, *rows, _ = finish(
        place, terms, rest, b_one, b_two, b_three, b, residual, gain, so_far, []
    )
    rows_z = along(2, rows)
    rows_y = along(1, rows)
    rows_zy = along(1, rows_z)
    held = [*rows, *rows_z, *rows_y, *rows_zy]
    a_near, b_near, beside = four_blocks(place, held, [])
    a_far = along(0, a_near)
    b_far = along(0, b_near)
    beside = send(beside, TO_CORE)

    near = functools.partial(multiplied, place, 0)
    far = functools.partial(multiplied, place, 1)
    total = near(a_near, [beside], qkv_weight, None, ONE, [], [])
    total = near(b_near, [beside], qkv_weight, total, TWO, [], [])
    *a_ready, _ = lax.optimization_barrier((*a_far, total))
    total = far(a_far, across(a_ready), qkv_weight, total, ONE, [], [])
    *b_ready, _ = lax.optimization_barrier((*b_far, total))
    notes = [b_near[2], beside]
    projected = far(b_far, across(b_ready), qkv_weight, total, TWO, notes, [])
    return stream, projected


def solution(mesh):
    in_specs = (P("tensor", "dp", None), P(("dp", "tensor"), None), P(), P(None, "tensor"))
    out_specs = (P(("dp", "tensor"), None), P("dp", "tensor"))
    return jax.shard_map(
        per_device, mesh=mesh, in_specs=in_specs, out_specs=out_specs, check_vma=False
    )
```

time: 169 us -> 159 us (0.941)
  Pallas kernels: 72.6 us -> 54.1 us
  waiting for transfers between devices: 46 us -> 58 us
  starting transfers between devices: 49.1 us -> 43.7 us
  local copies, waits for them, and re-layouts: 0.02 us -> 1.87 us
    pallas_call x16 -> x15, Pallas kernels: 72.6 us -> 54.1 us  [the longest x4 27.3 us: multiplied(): pl.pallas_call(kernel, in_specs=[ANY] * (n + 1 + len(more) + len(after)),...]
    ppermute x43 -> x42, waiting for transfers between devices: 46 us -> 58 us  [send(): return lax.ppermute(x, 'tensor', where)]
    ppermute x43 -> x42, starting transfers between devices: 49.1 us -> 43.7 us  [send(): return lax.ppermute(x, 'tensor', where)]
    unnamed x10 -> x26, local copies, waits for them, and re-layouts: 0.02 us -> 1.87 us
  transfers between devices with their start and end apart: 43 -> 42, of which waited for: 22 -> 25; matrix products, arithmetic and copies ran while one was open for 0% -> 0% of each run, Pallas kernels for 34% -> 27%
where the time goes in v3:
time: 159 us
  waiting for transfers between devices  58 us (36%)
  Pallas kernels  54.1 us (34%)
  starting transfers between devices  43.7 us (27%)
  local copies, waits for them, and re-layouts  1.87 us (1%)
    ppermute x42, waiting for transfers between devices, send(): return lax.ppermute(x, 'tensor', where)  58 us
    ppermute x42, starting transfers between devices, send(): return lax.ppermute(x, 'tensor', where)  43.7 us
    pallas_call x4, Pallas kernels, multiplied(): pl.pallas_call(kernel, in_specs=[ANY] * (n + 1 + len(more) + len(after)),...  27.3 us
    pallas_call x11, Pallas kernels, call(): pl.pallas_call(lambda *refs: kernel(where_am_i(), *refs), in_specs=[ANY]...  26.8 us
  transfers between devices with their start and end apart: 42, of which 25 were waited for; matrix products, arithmetic and copies ran while one was open for 0% of the time, Pallas kernels for 27%

profile of v3, /device:TPU:1, one launch (start us, length us, event | category | flops | bytes accessed | tf_op | source)
XLA Modules:
  0.0 158.7 jit_solution(4639512270304220783)
XLA Ops:
  0.6 2.1 %give.2.refs_1_ = bf16[4,32,10752]{2,1,0:T(8,128)(2,1)S(1)} custom-call(bf16[16,32,16384]{2,1,0:T(8,128)(2,1)} %bitcast.8), custom_call_target="tpu_custom_call" | custom-call | bytes 1024 | tf_op jit(solution)/shard_map/give/pallas_call | solution.py:86
  4.2 3.5 %give.3.refs_2_ = bf16[4,32,22016]{2,1,0:T(8,128)(2,1)S(1)} custom-call(bf16[16,32,16384]{2,1,0:T(8,128)(2,1)} %bitcast.9, bf16[4,32,10752]{2,1,0:T(8,128)(2,1)S(1)} %give.2.refs_1_), custom_call_target="tpu_custom_call" | custom-call | bytes 1024 | tf_op jit(solution)/shard_map/give/pallas_call | solution.py:86
  10.2 2.7 %first.2 = (bf16[4,32,2560]{2,1,0:T(8,128)(2,1)S(1)}, bf16[4,32,4096]{2,1,0:T(8,128)(2,1)S(1)}, bf16[4,32,4096]{2,1,0:T(8,128)(2,1)S(1)}) custom-call(bf16[16,32,16384]{2,1,0:T(8,128)(2,1)} %bitcast.10, bf16[4,32,10752]{2,1,0:T(8,128)(2,1)S(1)} %collective-permute-done.refs_1_, bf16[4,32,22016]{2,1,0:T(8,128)(2,1)} %copy-done.1), custom_call_target="tpu_custom_call" | custom-call | bytes 1024 | tf_op jit(solution)/shard_map/first/pallas_call | solution.py:86
  13.9 2.8 %collective-permute-start.6 = (bf16[4,32,4096]{2,1,0:T(8,128)(2,1)S(1)}, bf16[4,32,4096]{2,1,0:T(8,128)(2,1)S(1)}, u32[]{:S(2)}, u32[]{:S(2)}) collective-permute-start(bf16[4,32,4096]{2,1,0:T(8,128)(2,1)S(1)} %get-tuple-element.48), channel_id=1, source_target_pairs={{0,6},{1,7},{2,4},{3,5},{4,2},{5,3},{6,0},{7,1},{8,14},{9,15},{10,... | collective-permute-start | bytes 3145736 | tf_op jit(solution)/shard_map/ppermute | solution.py:42
  18.4 3.1 %first.3 = (bf16[4,32,3072]{2,1,0:T(8,128)(2,1)S(1)}, bf16[4,32,1024]{2,1,0:T(8,128)(2,1)S(1)}, bf16[4,32,1536]{2,1,0:T(8,128)(2,1)S(1)}) custom-call(bf16[16,32,16384]{2,1,0:T(8,128)(2,1)} %bitcast.11, bf16[4,32,22016]{2,1,0:T(8,128)(2,1)S(1)} %collective-permute-done.1.refs_1_, bf16[4,32,2560]{2,1,0:T(8,128)(2,1)S(1)} %get-tuple-element.44.refs_2_), custom_call_target="tpu_custom_call" | custom-call | bytes 1024 | tf_op jit(solution)/shard_map/first/pallas_call | solution.py:86
  24.4 9.7 %collective-permute-done.5.refs_2_ = bf16[4,32,2560]{2,1,0:T(8,128)(2,1)S(1)} collective-permute-done((bf16[4,32,2560]{2,1,0:T(8,128)(2,1)S(1)}, bf16[4,32,2560]{2,1,0:T(8,128)(2,1)S(1)}, u32[]{:S(2)}, u32[]{:S(2)}) %collective-permute-start.5) | collective-permute-done | bytes 655392 | tf_op jit(solution)/shard_map/ppermute | solution.py:42
  34.1 6.0 %collective-permute-done.6.refs_3_ = bf16[4,32,4096]{2,1,0:T(8,128)(2,1)S(1)} collective-permute-done((bf16[4,32,4096]{2,1,0:T(8,128)(2,1)S(1)}, bf16[4,32,4096]{2,1,0:T(8,128)(2,1)S(1)}, u32[]{:S(2)}, u32[]{:S(2)}) %collective-permute-start.6) | collective-permute-done | bytes 1048608 | tf_op jit(solution)/shard_map/ppermute | solution.py:42
  41.7 2.3 %second.2 = (bf16[2,32,2560]{2,1,0:T(8,128)(2,1)S(1)}, bf16[2,32,4096]{2,1,0:T(8,128)(2,1)S(1)}, bf16[2,32,4096]{2,1,0:T(8,128)(2,1)S(1)}) custom-call(bf16[16,32,16384]{2,1,0:T(8,128)(2,1)} %bitcast.12, bf16[4,32,22016]{2,1,0:T(8,128)(2,1)} %copy-done, bf16[4,32,2560]{2,1,0:T(8,128)(2,1)S(1)} %collective-permute-done.5.refs_2_, ...), custom_call_target="tpu_custom_call" | custom-call | bytes 1024 | tf_op jit(solution)/shard_map/second/pallas_call | solution.py:86
  45.5 2.8 %collective-permute-start.11 = (bf16[2,32,2560]{2,1,0:T(8,128)(2,1)S(1)}, bf16[2,32,2560]{2,1,0:T(8,128)(2,1)S(1)}, u32[]{:S(2)}, u32[]{:S(2)}) collective-permute-start(bf16[2,32,2560]{2,1,0:T(8,128)(2,1)S(1)} %get-tuple-element.50.refs_5_), channel_id=1, source_target_pairs={{0,6},{1,7},{2,4},{3,5},{4,2},{5,3},{6,0},{7,1},{8,14},{9,15},{10,... | collective-permute-start | bytes 983048 | tf_op jit(solution)/shard_map/ppermute | solution.py:42
  48.3 1.9 %collective-permute-done.4.refs_4_ = bf16[4,32,1536]{2,1,0:T(8,128)(2,1)S(1)} collective-permute-done((bf16[4,32,1536]{2,1,0:T(8,128)(2,1)S(1)}, bf16[4,32,1536]{2,1,0:T(8,128)(2,1)S(1)}, u32[]{:S(2)}, u32[]{:S(2)}) %collective-permute-start.4) | collective-permute-done | bytes 393248 | tf_op jit(solution)/shard_map/ppermute | solution.py:42
  50.9 1.9 %second.3 = (bf16[2,32,3072]{2,1,0:T(8,128)(2,1)S(1)}, bf16[2,32,1024]{2,1,0:T(8,128)(2,1)S(1)}, bf16[2,32,1536]{2,1,0:T(8,128)(2,1)S(1)}) custom-call(bf16[16,32,16384]{2,1,0:T(8,128)(2,1)} %bitcast.13, bf16[4,32,22016]{2,1,0:T(8,128)(2,1)S(1)} %bitcast.3, bf16[4,32,3072]{2,1,0:T(8,128)(2,1)S(1)} %collective-permute-done.2.refs_2_, ...), custom_call_target="tpu_custom_call" | custom-call | bytes 1024 | tf_op jit(solution)/shard_map/second/pallas_call | solution.py:86
  54.5 2.5 %collective-permute-start.9 = (bf16[2,32,1024]{2,1,0:T(8,128)(2,1)S(1)}, bf16[2,32,1024]{2,1,0:T(8,128)(2,1)S(1)}, u32[]{:S(2)}, u32[]{:S(2)}) collective-permute-start(bf16[2,32,1024]{2,1,0:T(8,128)(2,1)S(1)} %get-tuple-element.52), channel_id=1, source_target_pairs={{0,8},{1,9},{2,10},{3,11},{4,12},{5,13},{6,14},{7,15},{8,0},{9,1},... | collective-permute-start | bytes 393224 | tf_op jit(solution)/shard_map/ppermute | solution.py:42
  57.0 4.4 %collective-permute-done.12.refs_6_ = bf16[2,32,4096]{2,1,0:T(8,128)(2,1)S(1)} collective-permute-done((bf16[2,32,4096]{2,1,0:T(8,128)(2,1)S(1)}, bf16[2,32,4096]{2,1,0:T(8,128)(2,1)S(1)}, u32[]{:S(2)}, u32[]{:S(2)}) %collective-permute-start.12) | collective-permute-done | bytes 524320 | tf_op jit(solution)/shard_map/ppermute | solution.py:42
  62.1 1.8 %third.2 = (bf16[1,32,2560]{2,1,0:T(8,128)(2,1)S(1)}, bf16[1,32,4096]{2,1,0:T(8,128)(2,1)S(1)}, bf16[1,32,4096]{2,1,0:T(8,128)(2,1)S(1)}) custom-call(bf16[16,32,16384]{2,1,0:T(8,128)(2,1)} %bitcast.14, bf16[4,32,22016]{2,1,0:T(8,128)(2,1)} %copy-done, bf16[4,32,2560]{2,1,0:T(8,128)(2,1)S(1)} %copy-done.5, bf16[4,32,4096]{2,1,0:T(8,128)(2,1)S(1)} %copy-done.3, ...), custom_call_target="tpu_custom_call" | custom-call | bytes 1024 | tf_op jit(solution)/shard_map/third/pallas_call | solution.py:86
  66.4 1.8 %third.3 = (bf16[1,32,3072]{2,1,0:T(8,128)(2,1)S(1)}, bf16[1,32,1024]{2,1,0:T(8,128)(2,1)S(1)}, bf16[1,32,1536]{2,1,0:T(8,128)(2,1)S(1)}) custom-call(bf16[16,32,16384]{2,1,0:T(8,128)(2,1)} %bitcast.15, bf16[4,32,22016]{2,1,0:T(8,128)(2,1)S(1)} %bitcast.5, bf16[4,32,3072]{2,1,0:T(8,128)(2,1)S(1)} %collective-permute-done.2.refs_2_, ...), custom_call_target="tpu_custom_call" | custom-call | bytes 1024 | tf_op jit(solution)/shard_map/third/pallas_call | solution.py:86
  68.5 1.8 %collective-permute-start.16 = (bf16[1,32,1536]{2,1,0:T(8,128)(2,1)S(1)}, bf16[1,32,1536]{2,1,0:T(8,128)(2,1)S(1)}, u32[]{:S(2)}, u32[]{:S(2)}) collective-permute-start(bf16[1,32,1536]{2,1,0:T(8,128)(2,1)S(1)} %get-tuple-element.59), channel_id=1, source_target_pairs={{0,6},{1,7},{2,4},{3,5},{4,2},{5,3},{6,0},{7,1},{8,14},{9,15},{10,... | collective-permute-start | bytes 294920 | tf_op jit(solution)/shard_map/ppermute | solution.py:42
  70.7 3.0 %finish.2 = (bf16[32,16384]{1,0:T(8,128)(2,1)}, bf16[32,5632]{1,0:T(8,128)(2,1)S(1)}, bf16[32,5120]{1,0:T(8,128)(2,1)S(1)}, bf16[32,5760]{1,0:T(8,128)(2,1)S(1)}, f32[32,128]{1,0:T(8,128)S(1)}) custom-call(bf16[16,32,16384]{2,1,0:T(8,128)(2,1)} %bitcast.16, bf16[4,32,22016]{2,1,0:T(8,128)(2,1)} %copy-done, bf16[4,32,2560]{2,1,0:T(8,128)(2,1)S(1)} %copy-done.5, ...), custom_call_target="tpu_custom_call" | custom-call | bytes 1024 | tf_op jit(solution)/shard_map/finish/pallas_call | solution.py:86
  75.2 3.1 %finish.3 = (bf16[32,16384]{1,0:T(8,128)(2,1)}, bf16[32,5632]{1,0:T(8,128)(2,1)S(1)}, bf16[32,5120]{1,0:T(8,128)(2,1)S(1)}, bf16[32,5760]{1,0:T(8,128)(2,1)S(1)}, f32[32,128]{1,0:T(8,128)}) custom-call(bf16[16,32,16384]{2,1,0:T(8,128)(2,1)} %bitcast.17, ...), custom_call_target="tpu_custom_call", output_to_operand_aliasing={{0}: (13, {}), {1}: (14, {}), {2}: (15, {}), {3}: (16, {})} | custom-call | bytes 1024 | tf_op jit(solution)/shard_map/finish/pallas_call | solution.py:86
  81.5 4.4 %collective-permute-done.22.refs_5_ = bf16[32,5760]{1,0:T(8,128)(2,1)S(1)} collective-permute-done((bf16[32,5760]{1,0:T(8,128)(2,1)S(1)}, bf16[32,5760]{1,0:T(8,128)(2,1)S(1)}, u32[]{:S(2)}, u32[]{:S(2)}) %collective-permute-start.22) | collective-permute-done | bytes 368672 | tf_op jit(solution)/shard_map/ppermute | solution.py:42
  87.0 1.7 %collective-permute-start.26 = (bf16[32,5632]{1,0:T(8,128)(2,1)S(1)}, bf16[32,5632]{1,0:T(8,128)(2,1)S(1)}, u32[]{:S(2)}, u32[]{:S(2)}) collective-permute-start(bf16[32,5632]{1,0:T(8,128)(2,1)S(1)} %collective-permute-done.20.refs_3_), channel_id=1, source_target_pairs={{0,6},{1,7},{2,4},{3,5},{4,2},{5,3},{6,0},{7,1},{8,14},{9,15},{10,... | collective-permute-start | bytes 1081352 | tf_op jit(solution)/shard_map/ppermute | solution.py:42
  90.2 1.8 %collective-permute-start.27 = (bf16[32,5120]{1,0:T(8,128)(2,1)S(1)}, bf16[32,5120]{1,0:T(8,128)(2,1)S(1)}, u32[]{:S(2)}, u32[]{:S(2)}) collective-permute-start(bf16[32,5120]{1,0:T(8,128)(2,1)S(1)} %collective-permute-done.21.refs_4_), channel_id=1, source_target_pairs={{0,8},{1,9},{2,10},{3,11},{4,12},{5,13},{6,14},{7,15},{8,0},{9,1},... | collective-permute-start | bytes 983048 | tf_op jit(solution)/shard_map/ppermute | solution.py:42
  92.0 2.0 %collective-permute-done.23.refs_6_ = bf16[32,5632]{1,0:T(8,128)(2,1)S(1)} collective-permute-done((bf16[32,5632]{1,0:T(8,128)(2,1)S(1)}, bf16[32,5632]{1,0:T(8,128)(2,1)S(1)}, u32[]{:S(2)}, u32[]{:S(2)}) %collective-permute-start.23) | collective-permute-done | bytes 360480 | tf_op jit(solution)/shard_map/ppermute | solution.py:42
  94.0 5.5 %collective-permute-done.27.refs_10_ = bf16[32,5120]{1,0:T(8,128)(2,1)S(1)} collective-permute-done((bf16[32,5120]{1,0:T(8,128)(2,1)S(1)}, bf16[32,5120]{1,0:T(8,128)(2,1)S(1)}, u32[]{:S(2)}, u32[]{:S(2)}) %collective-permute-start.27) | collective-permute-done | bytes 327712 | tf_op jit(solution)/shard_map/ppermute | solution.py:42
  101.4 8.2 %collective-permute-start.35 = (bf16[4,32,16512]{2,1,0:T(8,128)(2,1)S(1)}, bf16[4,32,16512]{2,1,0:T(8,128)(2,1)S(1)}, u32[]{:S(2)}, u32[]{:S(2)}) collective-permute-start(bf16[4,32,16512]{2,1,0:T(8,128)(2,1)S(1)} %get-tuple-element.77), channel_id=1, source_target_pairs={{0,1},{1,0},{2,3},{3,2},{4,5},{5,4},{6,7},{7,6},{8,9},{9,8},{10,11... | collective-permute-start | bytes 12681224 | tf_op jit(solution)/shard_map/ppermute | solution.py:42
  109.9 1.7 %collective-permute-start.34 = (bf16[4,32,4096]{2,1,0:T(8,128)(2,1)S(1)}, bf16[4,32,4096]{2,1,0:T(8,128)(2,1)S(1)}, u32[]{:S(2)}, u32[]{:S(2)}) collective-permute-start(bf16[4,32,4096]{2,1,0:T(8,128)(2,1)S(1)} %get-tuple-element.76.refs_2_), channel_id=1, source_target_pairs={{0,8},{1,9},{2,10},{3,11},{4,12},{5,13},{6,14},{7,15},{8,0},{9,1},... | collective-permute-start | bytes 3145736 | tf_op jit(solution)/shard_map/ppermute | solution.py:42
  111.6 4.8 %collective-permute-done.35.refs_3_.refs_7_ = bf16[4,32,16512]{2,1,0:T(8,128)(2,1)S(1)} collective-permute-done((bf16[4,32,16512]{2,1,0:T(8,128)(2,1)S(1)}, bf16[4,32,16512]{2,1,0:T(8,128)(2,1)S(1)}, u32[]{:S(2)}, u32[]{:S(2)}) %collective-permute-start.35) | collective-permute-done | bytes 4227104 | tf_op jit(solution)/shard_map/ppermute | solution.py:42
  116.4 8.9 %multiply.4.refs_5_ = f32[512,640]{1,0:T(8,128)S(1)} custom-call(bf16[4,32,4096]{2,1,0:T(8,128)(2,1)S(1)} %get-tuple-element.74.refs_0_, bf16[4,32,4096]{2,1,0:T(8,128)(2,1)S(1)} %get-tuple-element.75.refs_1_, bf16[4,32,4096]{2,1,0:T(8,128)(2,1)S(1)} %get-tuple-element.76.refs_2_, bf16[4,32,16512]{2,1,0:T(8,128)(2,1)S(1)} %collective-permute-done.35.refs_3_.refs_7_, ...), custom_call_target="tpu_custom_call" | custom-call | bytes 1024 | tf_op jit(solution)/shard_map/multiply/pallas_call | solution.py:466
  125.3 4.3 %multiply.5.refs_7_ = f32[512,640]{1,0:T(8,128)S(1)} custom-call(bf16[4,32,1536]{2,1,0:T(8,128)(2,1)S(1)} %get-tuple-element.71.refs_0_, bf16[4,32,1024]{2,1,0:T(8,128)(2,1)S(1)} %get-tuple-element.72.refs_1_, bf16[4,32,1664]{2,1,0:T(8,128)(2,1)S(1)} %get-tuple-element.73.refs_2_.refs_6_, bf16[4,32,16512]{2,1,0:T(8,128)(2,1)S(1)} %collective-permute-done.35.refs_3_.refs_7_, ...), custom_call_target="tpu_custom_call" | custom-call | bytes 1024 | tf_op jit(solution)/shard_map/multiply/pallas_call | solution.py:466
  129.6 4.7 %collective-permute-done.32.refs_0_ = bf16[4,32,4096]{2,1,0:T(8,128)(2,1)S(1)} collective-permute-done((bf16[4,32,4096]{2,1,0:T(8,128)(2,1)S(1)}, bf16[4,32,4096]{2,1,0:T(8,128)(2,1)S(1)}, u32[]{:S(2)}, u32[]{:S(2)}) %collective-permute-start.32) | collective-permute-done | bytes 1048608 | tf_op jit(solution)/shard_map/ppermute | solution.py:42
  141.6 9.0 %multiply.6.refs_9_ = f32[512,640]{1,0:T(8,128)S(1)} custom-call(bf16[4,32,4096]{2,1,0:T(8,128)(2,1)S(1)} %collective-permute-done.32.refs_0_, bf16[4,32,4096]{2,1,0:T(8,128)(2,1)S(1)} %collective-permute-done.33.refs_1_, bf16[4,32,4096]{2,1,0:T(8,128)(2,1)S(1)} %collective-permute-done.34.refs_2_, bf16[4,32,4096]{2,1,0:T(8,128)(2,1)S(1)} %collective-permute-done.36.refs_3_, ...), custom_call_target="tpu_custom_call" | custom-call | bytes 1024 | tf_op jit(solution)/shard_map/multiply/pallas_call | solution.py:466
  151.6 1.8 %collective-permute-done.40.refs_4_ = bf16[4,32,1024]{2,1,0:T(8,128)(2,1)S(1)} collective-permute-done((bf16[4,32,1024]{2,1,0:T(8,128)(2,1)S(1)}, bf16[4,32,1024]{2,1,0:T(8,128)(2,1)S(1)}, u32[]{:S(2)}, u32[]{:S(2)}) %collective-permute-start.40) | collective-permute-done | bytes 262176 | tf_op jit(solution)/shard_map/ppermute | solution.py:42
  153.4 5.1 %multiply.7 = bf16[512,640]{1,0:T(8,128)(2,1)} custom-call(bf16[4,32,1536]{2,1,0:T(8,128)(2,1)S(1)} %collective-permute-done.29.refs_0_, bf16[4,32,1024]{2,1,0:T(8,128)(2,1)S(1)} %collective-permute-done.30.refs_1_, bf16[4,32,1664]{2,1,0:T(8,128)(2,1)S(1)} %collective-permute-done.31.refs_2_, bf16[4,32,1536]{2,1,0:T(8,128)(2,1)S(1)} %collective-permute-done.39.refs_3_, ...), custom_call_target="tpu_custom_call" | custom-call | bytes 1024 | tf_op jit(solution)/shard_map/multiply/pallas_call | solution.py:466
  (96 shorter events, 36.6 us)
Async XLA Ops:
  2.7 6.2 %collective-permute-start = (bf16[4,32,10752]{2,1,0:T(8,128)(2,1)S(1)}, bf16[4,32,10752]{2,1,0:T(8,128)(2,1)S(1)}, u32[]{:S(2)}, u32[]{:S(2)}) collective-permute-start(bf16[4,32,10752]{2,1,0:T(8,128)(2,1)S(1)} %give.2.refs_1_), channel_id=1, source_target_pairs={{0,1},{1,0},{2,3},{3,2},{4,5},{5,4},{6,7},{7,6},{8,9},{9,8},{10,11... | collective-permute-start | bytes 8257544 | tf_op jit(solution)/shard_map/ppermute | solution.py:42
  9.0 9.4 %collective-permute-start.1 = (bf16[4,32,22016]{2,1,0:T(8,128)(2,1)S(1)}, bf16[4,32,22016]{2,1,0:T(8,128)(2,1)S(1)}, u32[]{:S(2)}, u32[]{:S(2)}) collective-permute-start(bf16[4,32,22016]{2,1,0:T(8,128)(2,1)S(1)} %give.3.refs_2_), channel_id=1, source_target_pairs={{0,1},{1,0},{2,3},{3,2},{4,5},{5,4},{6,7},{7,6},{8,9},{9,8},{10,11... | collective-permute-start | bytes 16908296 | tf_op jit(solution)/shard_map/ppermute | solution.py:42
  13.9 26.3 %collective-permute-start.6 = (bf16[4,32,4096]{2,1,0:T(8,128)(2,1)S(1)}, bf16[4,32,4096]{2,1,0:T(8,128)(2,1)S(1)}, u32[]{:S(2)}, u32[]{:S(2)}) collective-permute-start(bf16[4,32,4096]{2,1,0:T(8,128)(2,1)S(1)} %get-tuple-element.48), channel_id=1, source_target_pairs={{0,6},{1,7},{2,4},{3,5},{4,2},{5,3},{6,0},{7,1},{8,14},{9,15},{10,... | collective-permute-start | bytes 3145736 | tf_op jit(solution)/shard_map/ppermute | solution.py:42
  16.7 25.0 %collective-permute-start.7 = (bf16[4,32,4096]{2,1,0:T(8,128)(2,1)}, bf16[4,32,4096]{2,1,0:T(8,128)(2,1)S(1)}, u32[]{:S(2)}, u32[]{:S(2)}) collective-permute-start(bf16[4,32,4096]{2,1,0:T(8,128)(2,1)} %copy-done.7), channel_id=1, source_target_pairs={{0,8},{1,9},{2,10},{3,11},{4,12},{5,13},{6,14},{7,15},{8,0},{9,1},... | collective-permute-start | bytes 3145736 | tf_op jit(solution)/shard_map/ppermute | solution.py:42
  18.4 15.7 %collective-permute-start.5 = (bf16[4,32,2560]{2,1,0:T(8,128)(2,1)S(1)}, bf16[4,32,2560]{2,1,0:T(8,128)(2,1)S(1)}, u32[]{:S(2)}, u32[]{:S(2)}) collective-permute-start(bf16[4,32,2560]{2,1,0:T(8,128)(2,1)S(1)} %get-tuple-element.44.refs_2_), channel_id=1, source_target_pairs={{0,2},{1,3},{2,0},{3,1},{4,6},{5,7},{6,4},{7,5},{8,10},{9,11},{10,... | collective-permute-start | bytes 1966088 | tf_op jit(solution)/shard_map/ppermute | solution.py:42
  21.5 29.4 %collective-permute-start.2 = (bf16[4,32,3072]{2,1,0:T(8,128)(2,1)S(1)}, bf16[4,32,3072]{2,1,0:T(8,128)(2,1)S(1)}, u32[]{:S(2)}, u32[]{:S(2)}) collective-permute-start(bf16[4,32,3072]{2,1,0:T(8,128)(2,1)S(1)} %get-tuple-element.45.refs_5_), channel_id=1, source_target_pairs={{0,2},{1,3},{2,0},{3,1},{4,6},{5,7},{6,4},{7,5},{8,10},{9,11},{10,... | collective-permute-start | bytes 2359304 | tf_op jit(solution)/shard_map/ppermute | solution.py:42
  23.0 27.1 %collective-permute-start.4 = (bf16[4,32,1536]{2,1,0:T(8,128)(2,1)S(1)}, bf16[4,32,1536]{2,1,0:T(8,128)(2,1)S(1)}, u32[]{:S(2)}, u32[]{:S(2)}) collective-permute-start(bf16[4,32,1536]{2,1,0:T(8,128)(2,1)S(1)} %get-tuple-element.47), channel_id=1, source_target_pairs={{0,8},{1,9},{2,10},{3,11},{4,12},{5,13},{6,14},{7,15},{8,0},{9,1},... | collective-permute-start | bytes 1179656 | tf_op jit(solution)/shard_map/ppermute | solution.py:42
  34.1 11.4 %collective-permute-start.3 = (bf16[4,32,1024]{2,1,0:T(8,128)(2,1)S(1)}, bf16[4,32,1024]{2,1,0:T(8,128)(2,1)S(1)}, u32[]{:S(2)}, u32[]{:S(2)}) collective-permute-start(bf16[4,32,1024]{2,1,0:T(8,128)(2,1)S(1)} %get-tuple-element.46), channel_id=1, source_target_pairs={{0,6},{1,7},{2,4},{3,5},{4,2},{5,3},{6,0},{7,1},{8,14},{9,15},{10,... | collective-permute-start | bytes 786440 | tf_op jit(solution)/shard_map/ppermute | solution.py:42
  44.0 17.4 %collective-permute-start.12 = (bf16[2,32,4096]{2,1,0:T(8,128)(2,1)S(1)}, bf16[2,32,4096]{2,1,0:T(8,128)(2,1)S(1)}, u32[]{:S(2)}, u32[]{:S(2)}) collective-permute-start(bf16[2,32,4096]{2,1,0:T(8,128)(2,1)S(1)} %get-tuple-element.54), channel_id=1, source_target_pairs={{0,8},{1,9},{2,10},{3,11},{4,12},{5,13},{6,14},{7,15},{8,0},{9,1},... | collective-permute-start | bytes 1572872 | tf_op jit(solution)/shard_map/ppermute | solution.py:42
  45.4 16.7 %collective-permute-start.13 = (bf16[2,32,4096]{2,1,0:T(8,128)(2,1)S(1)}, bf16[2,32,4096]{2,1,0:T(8,128)(2,1)S(1)}, u32[]{:S(2)}, u32[]{:S(2)}) collective-permute-start(bf16[2,32,4096]{2,1,0:T(8,128)(2,1)S(1)} %get-tuple-element.55), channel_id=1, source_target_pairs={{0,2},{1,3},{2,0},{3,1},{4,6},{5,7},{6,4},{7,5},{8,10},{9,11},{10,... | collective-permute-start | bytes 1572872 | tf_op jit(solution)/shard_map/ppermute | solution.py:42
  45.5 9.0 %collective-permute-start.11 = (bf16[2,32,2560]{2,1,0:T(8,128)(2,1)S(1)}, bf16[2,32,2560]{2,1,0:T(8,128)(2,1)S(1)}, u32[]{:S(2)}, u32[]{:S(2)}) collective-permute-start(bf16[2,32,2560]{2,1,0:T(8,128)(2,1)S(1)} %get-tuple-element.50.refs_5_), channel_id=1, source_target_pairs={{0,6},{1,7},{2,4},{3,5},{4,2},{5,3},{6,0},{7,1},{8,14},{9,15},{10,... | collective-permute-start | bytes 983048 | tf_op jit(solution)/shard_map/ppermute | solution.py:42
  52.8 13.6 %collective-permute-start.8 = (bf16[2,32,3072]{2,1,0:T(8,128)(2,1)S(1)}, bf16[2,32,3072]{2,1,0:T(8,128)(2,1)S(1)}, u32[]{:S(2)}, u32[]{:S(2)}) collective-permute-start(bf16[2,32,3072]{2,1,0:T(8,128)(2,1)S(1)} %get-tuple-element.51.refs_8_), channel_id=1, source_target_pairs={{0,6},{1,7},{2,4},{3,5},{4,2},{5,3},{6,0},{7,1},{8,14},{9,15},{10,... | collective-permute-start | bytes 1179656 | tf_op jit(solution)/shard_map/ppermute | solution.py:42
  52.9 13.4 %collective-permute-start.10 = (bf16[2,32,1536]{2,1,0:T(8,128)(2,1)S(1)}, bf16[2,32,1536]{2,1,0:T(8,128)(2,1)S(1)}, u32[]{:S(2)}, u32[]{:S(2)}) collective-permute-start(bf16[2,32,1536]{2,1,0:T(8,128)(2,1)S(1)} %get-tuple-element.53), channel_id=1, source_target_pairs={{0,2},{1,3},{2,0},{3,1},{4,6},{5,7},{6,4},{7,5},{8,10},{9,11},{10,... | collective-permute-start | bytes 589832 | tf_op jit(solution)/shard_map/ppermute | solution.py:42
  54.5 10.1 %collective-permute-start.9 = (bf16[2,32,1024]{2,1,0:T(8,128)(2,1)S(1)}, bf16[2,32,1024]{2,1,0:T(8,128)(2,1)S(1)}, u32[]{:S(2)}, u32[]{:S(2)}) collective-permute-start(bf16[2,32,1024]{2,1,0:T(8,128)(2,1)S(1)} %get-tuple-element.52), channel_id=1, source_target_pairs={{0,8},{1,9},{2,10},{3,11},{4,12},{5,13},{6,14},{7,15},{8,0},{9,1},... | collective-permute-start | bytes 393224 | tf_op jit(solution)/shard_map/ppermute | solution.py:42
  63.9 6.8 %collective-permute-start.18 = (bf16[1,32,4096]{2,1,0:T(8,128)(2,1)S(1)}, bf16[1,32,4096]{2,1,0:T(8,128)(2,1)S(1)}, u32[]{:S(2)}, u32[]{:S(2)}) collective-permute-start(bf16[1,32,4096]{2,1,0:T(8,128)(2,1)S(1)} %get-tuple-element.60), channel_id=1, source_target_pairs={{0,2},{1,3},{2,0},{3,1},{4,6},{5,7},{6,4},{7,5},{8,10},{9,11},{10,... | collective-permute-start | bytes 786440 | tf_op jit(solution)/shard_map/ppermute | solution.py:42
  64.2 6.6 %collective-permute-start.19 = (bf16[1,32,4096]{2,1,0:T(8,128)(2,1)S(1)}, bf16[1,32,4096]{2,1,0:T(8,128)(2,1)S(1)}, u32[]{:S(2)}, u32[]{:S(2)}) collective-permute-start(bf16[1,32,4096]{2,1,0:T(8,128)(2,1)S(1)} %get-tuple-element.61), channel_id=1, source_target_pairs={{0,6},{1,7},{2,4},{3,5},{4,2},{5,3},{6,0},{7,1},{8,14},{9,15},{10,... | collective-permute-start | bytes 786440 | tf_op jit(solution)/shard_map/ppermute | solution.py:42
  68.2 7.0 %collective-permute-start.14 = (bf16[1,32,3072]{2,1,0:T(8,128)(2,1)S(1)}, bf16[1,32,3072]{2,1,0:T(8,128)(2,1)S(1)}, u32[]{:S(2)}, u32[]{:S(2)}) collective-permute-start(bf16[1,32,3072]{2,1,0:T(8,128)(2,1)S(1)} %get-tuple-element.57.refs_13_), channel_id=1, source_target_pairs={{0,8},{1,9},{2,10},{3,11},{4,12},{5,13},{6,14},{7,15},{8,0},{9,1},... | collective-permute-start | bytes 589832 | tf_op jit(solution)/shard_map/ppermute | solution.py:42
  78.3 7.7 %collective-permute-start.22 = (bf16[32,5760]{1,0:T(8,128)(2,1)S(1)}, bf16[32,5760]{1,0:T(8,128)(2,1)S(1)}, u32[]{:S(2)}, u32[]{:S(2)}) collective-permute-start(bf16[32,5760]{1,0:T(8,128)(2,1)S(1)} %get-tuple-element.70.refs_2_), channel_id=1, source_target_pairs={{0,6},{1,7},{2,4},{3,5},{4,2},{5,3},{6,0},{7,1},{8,14},{9,15},{10,... | collective-permute-start | bytes 1105928 | tf_op jit(solution)/shard_map/ppermute | solution.py:42
  78.6 8.4 %collective-permute-start.20 = (bf16[32,5632]{1,0:T(8,128)(2,1)S(1)}, bf16[32,5632]{1,0:T(8,128)(2,1)S(1)}, u32[]{:S(2)}, u32[]{:S(2)}) collective-permute-start(bf16[32,5632]{1,0:T(8,128)(2,1)S(1)} %get-tuple-element.68.refs_0_), channel_id=1, source_target_pairs={{0,8},{1,9},{2,10},{3,11},{4,12},{5,13},{6,14},{7,15},{8,0},{9,1},... | collective-permute-start | bytes 1081352 | tf_op jit(solution)/shard_map/ppermute | solution.py:42
  79.8 10.4 %collective-permute-start.24 = (bf16[32,5120]{1,0:T(8,128)(2,1)S(1)}, bf16[32,5120]{1,0:T(8,128)(2,1)S(1)}, u32[]{:S(2)}, u32[]{:S(2)}) collective-permute-start(bf16[32,5120]{1,0:T(8,128)(2,1)S(1)} %get-tuple-element.69.refs_1_), channel_id=1, source_target_pairs={{0,8},{1,9},{2,10},{3,11},{4,12},{5,13},{6,14},{7,15},{8,0},{9,1},... | collective-permute-start | bytes 983048 | tf_op jit(solution)/shard_map/ppermute | solution.py:42
  80.1 13.9 %collective-permute-start.25 = (bf16[32,5760]{1,0:T(8,128)(2,1)S(1)}, bf16[32,5760]{1,0:T(8,128)(2,1)S(1)}, u32[]{:S(2)}, u32[]{:S(2)}) collective-permute-start(bf16[32,5760]{1,0:T(8,128)(2,1)S(1)} %get-tuple-element.70.refs_2_), channel_id=1, source_target_pairs={{0,2},{1,3},{2,0},{3,1},{4,6},{5,7},{6,4},{7,5},{8,10},{9,11},{10,... | collective-permute-start | bytes 1105928 | tf_op jit(solution)/shard_map/ppermute | solution.py:42
  85.9 13.9 %collective-permute-start.28 = (bf16[32,5760]{1,0:T(8,128)(2,1)S(1)}, bf16[32,5760]{1,0:T(8,128)(2,1)S(1)}, u32[]{:S(2)}, u32[]{:S(2)}) collective-permute-start(bf16[32,5760]{1,0:T(8,128)(2,1)S(1)} %collective-permute-done.22.refs_5_), channel_id=1, source_target_pairs={{0,2},{1,3},{2,0},{3,1},{4,6},{5,7},{6,4},{7,5},{8,10},{9,11},{10,... | collective-permute-start | bytes 1105928 | tf_op jit(solution)/shard_map/ppermute | solution.py:42
  86.0 8.1 %collective-permute-start.23 = (bf16[32,5632]{1,0:T(8,128)(2,1)S(1)}, bf16[32,5632]{1,0:T(8,128)(2,1)S(1)}, u32[]{:S(2)}, u32[]{:S(2)}) collective-permute-start(bf16[32,5632]{1,0:T(8,128)(2,1)S(1)} %get-tuple-element.68.refs_0_), channel_id=1, source_target_pairs={{0,6},{1,7},{2,4},{3,5},{4,2},{5,3},{6,0},{7,1},{8,14},{9,15},{10,... | collective-permute-start | bytes 1081352 | tf_op jit(solution)/shard_map/ppermute | solution.py:42
  87.0 12.6 %collective-permute-start.26 = (bf16[32,5632]{1,0:T(8,128)(2,1)S(1)}, bf16[32,5632]{1,0:T(8,128)(2,1)S(1)}, u32[]{:S(2)}, u32[]{:S(2)}) collective-permute-start(bf16[32,5632]{1,0:T(8,128)(2,1)S(1)} %collective-permute-done.20.refs_3_), channel_id=1, source_target_pairs={{0,6},{1,7},{2,4},{3,5},{4,2},{5,3},{6,0},{7,1},{8,14},{9,15},{10,... | collective-permute-start | bytes 1081352 | tf_op jit(solution)/shard_map/ppermute | solution.py:42
  90.2 9.4 %collective-permute-start.27 = (bf16[32,5120]{1,0:T(8,128)(2,1)S(1)}, bf16[32,5120]{1,0:T(8,128)(2,1)S(1)}, u32[]{:S(2)}, u32[]{:S(2)}) collective-permute-start(bf16[32,5120]{1,0:T(8,128)(2,1)S(1)} %collective-permute-done.21.refs_4_), channel_id=1, source_target_pairs={{0,8},{1,9},{2,10},{3,11},{4,12},{5,13},{6,14},{7,15},{8,0},{9,1},... | collective-permute-start | bytes 983048 | tf_op jit(solution)/shard_map/ppermute | solution.py:42
  101.4 15.0 %collective-permute-start.35 = (bf16[4,32,16512]{2,1,0:T(8,128)(2,1)S(1)}, bf16[4,32,16512]{2,1,0:T(8,128)(2,1)S(1)}, u32[]{:S(2)}, u32[]{:S(2)}) collective-permute-start(bf16[4,32,16512]{2,1,0:T(8,128)(2,1)S(1)} %get-tuple-element.77), channel_id=1, source_target_pairs={{0,1},{1,0},{2,3},{3,2},{4,5},{5,4},{6,7},{7,6},{8,9},{9,8},{10,11... | collective-permute-start | bytes 12681224 | tf_op jit(solution)/shard_map/ppermute | solution.py:42
  109.5 24.7 %collective-permute-start.32 = (bf16[4,32,4096]{2,1,0:T(8,128)(2,1)S(1)}, bf16[4,32,4096]{2,1,0:T(8,128)(2,1)S(1)}, u32[]{:S(2)}, u32[]{:S(2)}) collective-permute-start(bf16[4,32,4096]{2,1,0:T(8,128)(2,1)S(1)} %get-tuple-element.74.refs_0_), channel_id=1, source_target_pairs={{0,2},{1,3},{2,0},{3,1},{4,6},{5,7},{6,4},{7,5},{8,10},{9,11},{10,... | collective-permute-start | bytes 3145736 | tf_op jit(solution)/shard_map/ppermute | solution.py:42
  109.5 25.8 %collective-permute-start.33 = (bf16[4,32,4096]{2,1,0:T(8,128)(2,1)S(1)}, bf16[4,32,4096]{2,1,0:T(8,128)(2,1)S(1)}, u32[]{:S(2)}, u32[]{:S(2)}) collective-permute-start(bf16[4,32,4096]{2,1,0:T(8,128)(2,1)S(1)} %get-tuple-element.75.refs_1_), channel_id=1, source_target_pairs={{0,6},{1,7},{2,4},{3,5},{4,2},{5,3},{6,0},{7,1},{8,14},{9,15},{10,... | collective-permute-start | bytes 3145736 | tf_op jit(solution)/shard_map/ppermute | solution.py:42
  109.9 25.5 %collective-permute-start.34 = (bf16[4,32,4096]{2,1,0:T(8,128)(2,1)S(1)}, bf16[4,32,4096]{2,1,0:T(8,128)(2,1)S(1)}, u32[]{:S(2)}, u32[]{:S(2)}) collective-permute-start(bf16[4,32,4096]{2,1,0:T(8,128)(2,1)S(1)} %get-tuple-element.76.refs_2_), channel_id=1, source_target_pairs={{0,8},{1,9},{2,10},{3,11},{4,12},{5,13},{6,14},{7,15},{8,0},{9,1},... | collective-permute-start | bytes 3145736 | tf_op jit(solution)/shard_map/ppermute | solution.py:42
  136.8 13.8 %collective-permute-start.31 = (bf16[4,32,1664]{2,1,0:T(8,128)(2,1)S(1)}, bf16[4,32,1664]{2,1,0:T(8,128)(2,1)S(1)}, u32[]{:S(2)}, u32[]{:S(2)}) collective-permute-start(bf16[4,32,1664]{2,1,0:T(8,128)(2,1)S(1)} %get-tuple-element.73.refs_2_.refs_6_), channel_id=1, source_target_pairs={{0,8},{1,9},{2,10},{3,11},{4,12},{5,13},{6,14},{7,15},{8,0},{9,1},... | collective-permute-start | bytes 1277960 | tf_op jit(solution)/shard_map/ppermute | solution.py:42
  137.8 12.8 %collective-permute-start.29 = (bf16[4,32,1536]{2,1,0:T(8,128)(2,1)S(1)}, bf16[4,32,1536]{2,1,0:T(8,128)(2,1)S(1)}, u32[]{:S(2)}, u32[]{:S(2)}) collective-permute-start(bf16[4,32,1536]{2,1,0:T(8,128)(2,1)S(1)} %get-tuple-element.71.refs_0_), channel_id=1, source_target_pairs={{0,2},{1,3},{2,0},{3,1},{4,6},{5,7},{6,4},{7,5},{8,10},{9,11},{10,... | collective-permute-start | bytes 1179656 | tf_op jit(solution)/shard_map/ppermute | solution.py:42
  138.6 12.0 %collective-permute-start.30 = (bf16[4,32,1024]{2,1,0:T(8,128)(2,1)S(1)}, bf16[4,32,1024]{2,1,0:T(8,128)(2,1)S(1)}, u32[]{:S(2)}, u32[]{:S(2)}) collective-permute-start(bf16[4,32,1024]{2,1,0:T(8,128)(2,1)S(1)} %get-tuple-element.72.refs_1_), channel_id=1, source_target_pairs={{0,6},{1,7},{2,4},{3,5},{4,2},{5,3},{6,0},{7,1},{8,14},{9,15},{10,... | collective-permute-start | bytes 786440 | tf_op jit(solution)/shard_map/ppermute | solution.py:42
  (23 other events, 164.0 us)

commit v4 on v3

--- a/solution.py
+++ b/solution.py
@@ -67,7 +67,9 @@
     def at(i, carry):
         return body(pl.ds(pl.multiple_of(i * step, step), step), carry)
 
-    return functools.partial(lax.fori_loop, 0, width // step, at)
+    steps = width // step
+    unroll = next(u for u in (3, 7, 5, 2, 1) if steps % u == 0)
+    return functools.partial(lax.fori_loop, 0, steps, at, unroll=unroll)
 
 
 def total_of(sources, columns):
@@ -487,7 +489,7 @@
     return Stream(runs[0], (0, 0, 0)), Stream(runs[1], first)
 
 
-FIRST, SECOND = streams_of((2560, 4096, 4096), (3072, 1024, 1536), NOTE)
+FIRST, SECOND = streams_of((2560, 3584, 3584), (3072, 1536, 2048), NOTE)
 ONE, TWO = streams_of((4096, 4096, 4096), (1536, 1024, 1536), NOTE)
 WIDTHS = [a.sent + b.sent for a, b in zip(FIRST.parts, SECOND.parts)]
 

time: 159 us -> 158 us (level)
  waiting for transfers between devices: 58 us -> 50.7 us
  starting transfers between devices: 43.7 us -> 48 us
  Pallas kernels: 54.1 us -> 58.3 us
  local copies, waits for them, and re-layouts: 1.87 us -> 0.03 us
    ppermute x42, waiting for transfers between devices: 58 us -> 50.7 us  [send(): return lax.ppermute(x, 'tensor', where)]
    ppermute x42, starting transfers between devices: 43.7 us -> 48 us  [send(): return lax.ppermute(x, 'tensor', where)]
    pallas_call x11, Pallas kernels: 26.8 us -> 31 us  [call(): pl.pallas_call(lambda *refs: kernel(where_am_i(), *refs), in_specs=[ANY]...]
    unnamed x26 -> x14, local copies, waits for them, and re-layouts: 1.87 us -> 0.03 us
  transfers between devices with their start and end apart: 42 -> 42, of which waited for: 25 -> 22; matrix products, arithmetic and copies ran while one was open for 0% -> 0% of each run, Pallas kernels for 27% -> 29%
where the time goes in v4:
time: 158 us
  Pallas kernels  58.3 us (37%)
  waiting for transfers between devices  50.7 us (32%)
  starting transfers between devices  48 us (30%)
    ppermute x42, waiting for transfers between devices, send(): return lax.ppermute(x, 'tensor', where)  50.7 us
    ppermute x42, starting transfers between devices, send(): return lax.ppermute(x, 'tensor', where)  48 us
    pallas_call x11, Pallas kernels, call(): pl.pallas_call(lambda *refs: kernel(where_am_i(), *refs), in_specs=[ANY]...  31 us
    pallas_call x4, Pallas kernels, multiplied(): pl.pallas_call(kernel, in_specs=[ANY] * (n + 1 + len(more) + len(after)),...  27.3 us
  transfers between devices with their start and end apart: 42, of which 22 were waited for; matrix products, arithmetic and copies ran while one was open for 0% of the time, Pallas kernels for 29%

profile of v4, /device:TPU:1, one launch (start us, length us, event | category | flops | bytes accessed | tf_op | source)
XLA Modules:
  0.0 158.1 jit_solution(8858761030142802446)
XLA Ops:
  0.6 2.1 %give.2.refs_1_ = bf16[4,32,9728]{2,1,0:T(8,128)(2,1)S(1)} custom-call(bf16[16,32,16384]{2,1,0:T(8,128)(2,1)} %bitcast.8), custom_call_target="tpu_custom_call" | custom-call | bytes 1024 | tf_op jit(solution)/shard_map/give/pallas_call | solution.py:88
  4.2 5.6 %give.3.refs_2_ = bf16[4,32,23040]{2,1,0:T(8,128)(2,1)} custom-call(bf16[16,32,16384]{2,1,0:T(8,128)(2,1)} %bitcast.9, bf16[4,32,9728]{2,1,0:T(8,128)(2,1)S(1)} %give.2.refs_1_), custom_call_target="tpu_custom_call" | custom-call | bytes 1024 | tf_op jit(solution)/shard_map/give/pallas_call | solution.py:88
  10.0 2.6 %first.2 = (bf16[4,32,2560]{2,1,0:T(8,128)(2,1)S(1)}, bf16[4,32,3584]{2,1,0:T(8,128)(2,1)S(1)}, bf16[4,32,3584]{2,1,0:T(8,128)(2,1)S(1)}) custom-call(bf16[16,32,16384]{2,1,0:T(8,128)(2,1)} %bitcast.10, bf16[4,32,9728]{2,1,0:T(8,128)(2,1)S(1)} %collective-permute-done.refs_1_, bf16[4,32,23040]{2,1,0:T(8,128)(2,1)} %give.3.refs_2_), custom_call_target="tpu_custom_call" | custom-call | bytes 1024 | tf_op jit(solution)/shard_map/first/pallas_call | solution.py:88
  14.0 1.9 %collective-permute-start.6 = (bf16[4,32,3584]{2,1,0:T(8,128)(2,1)S(1)}, bf16[4,32,3584]{2,1,0:T(8,128)(2,1)S(1)}, u32[]{:S(2)}, u32[]{:S(2)}) collective-permute-start(bf16[4,32,3584]{2,1,0:T(8,128)(2,1)S(1)} %get-tuple-element.48), channel_id=1, source_target_pairs={{0,6},{1,7},{2,4},{3,5},{4,2},{5,3},{6,0},{7,1},{8,14},{9,15},{10,... | collective-permute-start | bytes 2752520 | tf_op jit(solution)/shard_map/ppermute | solution.py:42
  17.5 2.2 %collective-permute-done.1.refs_1_ = bf16[4,32,23040]{2,1,0:T(8,128)(2,1)S(1)} collective-permute-done((bf16[4,32,23040]{2,1,0:T(8,128)(2,1)}, bf16[4,32,23040]{2,1,0:T(8,128)(2,1)S(1)}, u32[]{:S(2)}, u32[]{:S(2)}) %collective-permute-start.1) | collective-permute-done | bytes 5898272 | tf_op jit(solution)/shard_map/ppermute | solution.py:42
  19.7 3.4 %first.3 = (bf16[4,32,3072]{2,1,0:T(8,128)(2,1)S(1)}, bf16[4,32,1536]{2,1,0:T(8,128)(2,1)S(1)}, bf16[4,32,2048]{2,1,0:T(8,128)(2,1)S(1)}) custom-call(bf16[16,32,16384]{2,1,0:T(8,128)(2,1)} %bitcast.11, bf16[4,32,23040]{2,1,0:T(8,128)(2,1)S(1)} %collective-permute-done.1.refs_1_, bf16[4,32,2560]{2,1,0:T(8,128)(2,1)S(1)} %get-tuple-element.44.refs_2_), custom_call_target="tpu_custom_call" | custom-call | bytes 1024 | tf_op jit(solution)/shard_map/first/pallas_call | solution.py:88
  24.6 1.9 %collective-permute-start.3 = (bf16[4,32,1536]{2,1,0:T(8,128)(2,1)S(1)}, bf16[4,32,1536]{2,1,0:T(8,128)(2,1)S(1)}, u32[]{:S(2)}, u32[]{:S(2)}) collective-permute-start(bf16[4,32,1536]{2,1,0:T(8,128)(2,1)S(1)} %get-tuple-element.46), channel_id=1, source_target_pairs={{0,6},{1,7},{2,4},{3,5},{4,2},{5,3},{6,0},{7,1},{8,14},{9,15},{10,... | collective-permute-start | bytes 1179656 | tf_op jit(solution)/shard_map/ppermute | solution.py:42
  26.5 2.0 %collective-permute-done.5.refs_2_ = bf16[4,32,2560]{2,1,0:T(8,128)(2,1)S(1)} collective-permute-done((bf16[4,32,2560]{2,1,0:T(8,128)(2,1)S(1)}, bf16[4,32,2560]{2,1,0:T(8,128)(2,1)S(1)}, u32[]{:S(2)}, u32[]{:S(2)}) %collective-permute-start.5) | collective-permute-done | bytes 655392 | tf_op jit(solution)/shard_map/ppermute | solution.py:42
  30.2 6.2 %collective-permute-done.6.refs_3_ = bf16[4,32,3584]{2,1,0:T(8,128)(2,1)S(1)} collective-permute-done((bf16[4,32,3584]{2,1,0:T(8,128)(2,1)S(1)}, bf16[4,32,3584]{2,1,0:T(8,128)(2,1)S(1)}, u32[]{:S(2)}, u32[]{:S(2)}) %collective-permute-start.6) | collective-permute-done | bytes 917536 | tf_op jit(solution)/shard_map/ppermute | solution.py:42
  37.1 2.6 %second.2 = (bf16[2,32,2560]{2,1,0:T(8,128)(2,1)S(1)}, bf16[2,32,3584]{2,1,0:T(8,128)(2,1)S(1)}, bf16[2,32,3584]{2,1,0:T(8,128)(2,1)S(1)}) custom-call(bf16[16,32,16384]{2,1,0:T(8,128)(2,1)} %bitcast.12, bf16[4,32,23040]{2,1,0:T(8,128)(2,1)} %copy-done, bf16[4,32,2560]{2,1,0:T(8,128)(2,1)S(1)} %collective-permute-done.5.refs_2_, ...), custom_call_target="tpu_custom_call" | custom-call | bytes 1024 | tf_op jit(solution)/shard_map/second/pallas_call | solution.py:88
  42.5 2.2 %collective-permute-done.3.refs_3_ = bf16[4,32,1536]{2,1,0:T(8,128)(2,1)S(1)} collective-permute-done((bf16[4,32,1536]{2,1,0:T(8,128)(2,1)S(1)}, bf16[4,32,1536]{2,1,0:T(8,128)(2,1)S(1)}, u32[]{:S(2)}, u32[]{:S(2)}) %collective-permute-start.3) | collective-permute-done | bytes 393248 | tf_op jit(solution)/shard_map/ppermute | solution.py:42
  44.8 3.5 %collective-permute-done.4.refs_4_ = bf16[4,32,2048]{2,1,0:T(8,128)(2,1)S(1)} collective-permute-done((bf16[4,32,2048]{2,1,0:T(8,128)(2,1)S(1)}, bf16[4,32,2048]{2,1,0:T(8,128)(2,1)S(1)}, u32[]{:S(2)}, u32[]{:S(2)}) %collective-permute-start.4) | collective-permute-done | bytes 524320 | tf_op jit(solution)/shard_map/ppermute | solution.py:42
  48.3 1.9 %second.3 = (bf16[2,32,3072]{2,1,0:T(8,128)(2,1)S(1)}, bf16[2,32,1536]{2,1,0:T(8,128)(2,1)S(1)}, bf16[2,32,2048]{2,1,0:T(8,128)(2,1)S(1)}) custom-call(bf16[16,32,16384]{2,1,0:T(8,128)(2,1)} %bitcast.13, bf16[4,32,23040]{2,1,0:T(8,128)(2,1)S(1)} %bitcast.3, bf16[4,32,3072]{2,1,0:T(8,128)(2,1)S(1)} %collective-permute-done.2.refs_2_, ...), custom_call_target="tpu_custom_call" | custom-call | bytes 1024 | tf_op jit(solution)/shard_map/second/pallas_call | solution.py:88
  53.4 4.8 %collective-permute-done.12.refs_6_ = bf16[2,32,3584]{2,1,0:T(8,128)(2,1)S(1)} collective-permute-done((bf16[2,32,3584]{2,1,0:T(8,128)(2,1)S(1)}, bf16[2,32,3584]{2,1,0:T(8,128)(2,1)S(1)}, u32[]{:S(2)}, u32[]{:S(2)}) %collective-permute-start.12) | collective-permute-done | bytes 458784 | tf_op jit(solution)/shard_map/ppermute | solution.py:42
  58.1 2.4 %third.2 = (bf16[1,32,2560]{2,1,0:T(8,128)(2,1)S(1)}, bf16[1,32,3584]{2,1,0:T(8,128)(2,1)S(1)}, bf16[1,32,3584]{2,1,0:T(8,128)(2,1)S(1)}) custom-call(bf16[16,32,16384]{2,1,0:T(8,128)(2,1)} %bitcast.14, bf16[4,32,23040]{2,1,0:T(8,128)(2,1)} %copy-done, bf16[4,32,2560]{2,1,0:T(8,128)(2,1)S(1)} %collective-permute-done.5.refs_2_, ...), custom_call_target="tpu_custom_call" | custom-call | bytes 1024 | tf_op jit(solution)/shard_map/third/pallas_call | solution.py:88
  63.2 1.9 %third.3 = (bf16[1,32,3072]{2,1,0:T(8,128)(2,1)S(1)}, bf16[1,32,1536]{2,1,0:T(8,128)(2,1)S(1)}, bf16[1,32,2048]{2,1,0:T(8,128)(2,1)S(1)}) custom-call(bf16[16,32,16384]{2,1,0:T(8,128)(2,1)} %bitcast.15, bf16[4,32,23040]{2,1,0:T(8,128)(2,1)S(1)} %bitcast.5, bf16[4,32,3072]{2,1,0:T(8,128)(2,1)S(1)} %collective-permute-done.2.refs_2_, ...), custom_call_target="tpu_custom_call" | custom-call | bytes 1024 | tf_op jit(solution)/shard_map/third/pallas_call | solution.py:88
  66.4 1.9 %collective-permute-start.16 = (bf16[1,32,2048]{2,1,0:T(8,128)(2,1)S(1)}, bf16[1,32,2048]{2,1,0:T(8,128)(2,1)S(1)}, u32[]{:S(2)}, u32[]{:S(2)}) collective-permute-start(bf16[1,32,2048]{2,1,0:T(8,128)(2,1)S(1)} %get-tuple-element.59), channel_id=1, source_target_pairs={{0,6},{1,7},{2,4},{3,5},{4,2},{5,3},{6,0},{7,1},{8,14},{9,15},{10,... | collective-permute-start | bytes 393224 | tf_op jit(solution)/shard_map/ppermute | solution.py:42
  68.4 3.9 %finish.2 = (bf16[32,16384]{1,0:T(8,128)(2,1)}, bf16[32,5632]{1,0:T(8,128)(2,1)S(1)}, bf16[32,5120]{1,0:T(8,128)(2,1)S(1)}, bf16[32,5760]{1,0:T(8,128)(2,1)S(1)}, f32[32,128]{1,0:T(8,128)S(1)}) custom-call(bf16[16,32,16384]{2,1,0:T(8,128)(2,1)} %bitcast.16, bf16[4,32,23040]{2,1,0:T(8,128)(2,1)} %copy-done, ...), custom_call_target="tpu_custom_call" | custom-call | bytes 1024 | tf_op jit(solution)/shard_map/finish/pallas_call | solution.py:88
  72.8 3.2 %finish.3 = (bf16[32,16384]{1,0:T(8,128)(2,1)}, bf16[32,5632]{1,0:T(8,128)(2,1)S(1)}, bf16[32,5120]{1,0:T(8,128)(2,1)S(1)}, bf16[32,5760]{1,0:T(8,128)(2,1)S(1)}, f32[32,128]{1,0:T(8,128)}) custom-call(bf16[16,32,16384]{2,1,0:T(8,128)(2,1)} %bitcast.17, ...), custom_call_target="tpu_custom_call", output_to_operand_aliasing={{0}: (13, {}), {1}: (14, {}), {2}: (15, {}), {3}: (16, {})} | custom-call | bytes 1024 | tf_op jit(solution)/shard_map/finish/pallas_call | solution.py:88
  76.1 2.2 %collective-permute-start.22 = (bf16[32,5760]{1,0:T(8,128)(2,1)S(1)}, bf16[32,5760]{1,0:T(8,128)(2,1)S(1)}, u32[]{:S(2)}, u32[]{:S(2)}) collective-permute-start(bf16[32,5760]{1,0:T(8,128)(2,1)S(1)} %get-tuple-element.70.refs_2_), channel_id=1, source_target_pairs={{0,6},{1,7},{2,4},{3,5},{4,2},{5,3},{6,0},{7,1},{8,14},{9,15},{10,... | collective-permute-start | bytes 1105928 | tf_op jit(solution)/shard_map/ppermute | solution.py:42
  81.2 2.5 %collective-permute-done.22.refs_5_ = bf16[32,5760]{1,0:T(8,128)(2,1)S(1)} collective-permute-done((bf16[32,5760]{1,0:T(8,128)(2,1)S(1)}, bf16[32,5760]{1,0:T(8,128)(2,1)S(1)}, u32[]{:S(2)}, u32[]{:S(2)}) %collective-permute-start.22) | collective-permute-done | bytes 368672 | tf_op jit(solution)/shard_map/ppermute | solution.py:42
  87.2 2.9 %collective-permute-done.24.refs_7_ = bf16[32,5120]{1,0:T(8,128)(2,1)S(1)} collective-permute-done((bf16[32,5120]{1,0:T(8,128)(2,1)S(1)}, bf16[32,5120]{1,0:T(8,128)(2,1)S(1)}, u32[]{:S(2)}, u32[]{:S(2)}) %collective-permute-start.24) | collective-permute-done | bytes 327712 | tf_op jit(solution)/shard_map/ppermute | solution.py:42
  90.8 3.0 %collective-permute-done.23.refs_6_ = bf16[32,5632]{1,0:T(8,128)(2,1)S(1)} collective-permute-done((bf16[32,5632]{1,0:T(8,128)(2,1)S(1)}, bf16[32,5632]{1,0:T(8,128)(2,1)S(1)}, u32[]{:S(2)}, u32[]{:S(2)}) %collective-permute-start.23) | collective-permute-done | bytes 360480 | tf_op jit(solution)/shard_map/ppermute | solution.py:42
  93.8 5.5 %collective-permute-done.27.refs_10_ = bf16[32,5120]{1,0:T(8,128)(2,1)S(1)} collective-permute-done((bf16[32,5120]{1,0:T(8,128)(2,1)S(1)}, bf16[32,5120]{1,0:T(8,128)(2,1)S(1)}, u32[]{:S(2)}, u32[]{:S(2)}) %collective-permute-start.27) | collective-permute-done | bytes 327712 | tf_op jit(solution)/shard_map/ppermute | solution.py:42
  100.8 7.5 %collective-permute-start.35 = (bf16[4,32,16512]{2,1,0:T(8,128)(2,1)S(1)}, bf16[4,32,16512]{2,1,0:T(8,128)(2,1)S(1)}, u32[]{:S(2)}, u32[]{:S(2)}) collective-permute-start(bf16[4,32,16512]{2,1,0:T(8,128)(2,1)S(1)} %get-tuple-element.77), channel_id=1, source_target_pairs={{0,1},{1,0},{2,3},{3,2},{4,5},{5,4},{6,7},{7,6},{8,9},{9,8},{10,11... | collective-permute-start | bytes 12681224 | tf_op jit(solution)/shard_map/ppermute | solution.py:42
  111.4 3.8 %collective-permute-done.35.refs_3_.refs_7_ = bf16[4,32,16512]{2,1,0:T(8,128)(2,1)S(1)} collective-permute-done((bf16[4,32,16512]{2,1,0:T(8,128)(2,1)S(1)}, bf16[4,32,16512]{2,1,0:T(8,128)(2,1)S(1)}, u32[]{:S(2)}, u32[]{:S(2)}) %collective-permute-start.35) | collective-permute-done | bytes 4227104 | tf_op jit(solution)/shard_map/ppermute | solution.py:42
  115.1 8.9 %multiply.4.refs_5_ = f32[512,640]{1,0:T(8,128)S(1)} custom-call(bf16[4,32,4096]{2,1,0:T(8,128)(2,1)S(1)} %get-tuple-element.74.refs_0_, bf16[4,32,4096]{2,1,0:T(8,128)(2,1)S(1)} %get-tuple-element.75.refs_1_, bf16[4,32,4096]{2,1,0:T(8,128)(2,1)S(1)} %get-tuple-element.76.refs_2_, bf16[4,32,16512]{2,1,0:T(8,128)(2,1)S(1)} %collective-permute-done.35.refs_3_.refs_7_, ...), custom_call_target="tpu_custom_call" | custom-call | bytes 1024 | tf_op jit(solution)/shard_map/multiply/pallas_call | solution.py:468
  124.1 4.3 %multiply.5.refs_7_ = f32[512,640]{1,0:T(8,128)S(1)} custom-call(bf16[4,32,1536]{2,1,0:T(8,128)(2,1)S(1)} %get-tuple-element.71.refs_0_, bf16[4,32,1024]{2,1,0:T(8,128)(2,1)S(1)} %get-tuple-element.72.refs_1_, bf16[4,32,1664]{2,1,0:T(8,128)(2,1)S(1)} %get-tuple-element.73.refs_2_.refs_6_, bf16[4,32,16512]{2,1,0:T(8,128)(2,1)S(1)} %collective-permute-done.35.refs_3_.refs_7_, ...), custom_call_target="tpu_custom_call" | custom-call | bytes 1024 | tf_op jit(solution)/shard_map/multiply/pallas_call | solution.py:468
  128.4 4.7 %collective-permute-done.32.refs_0_ = bf16[4,32,4096]{2,1,0:T(8,128)(2,1)S(1)} collective-permute-done((bf16[4,32,4096]{2,1,0:T(8,128)(2,1)S(1)}, bf16[4,32,4096]{2,1,0:T(8,128)(2,1)S(1)}, u32[]{:S(2)}, u32[]{:S(2)}) %collective-permute-start.32) | collective-permute-done | bytes 1048608 | tf_op jit(solution)/shard_map/ppermute | solution.py:42
  141.0 9.0 %multiply.6.refs_9_ = f32[512,640]{1,0:T(8,128)S(1)} custom-call(bf16[4,32,4096]{2,1,0:T(8,128)(2,1)S(1)} %collective-permute-done.32.refs_0_, bf16[4,32,4096]{2,1,0:T(8,128)(2,1)S(1)} %collective-permute-done.33.refs_1_, bf16[4,32,4096]{2,1,0:T(8,128)(2,1)S(1)} %collective-permute-done.34.refs_2_, bf16[4,32,4096]{2,1,0:T(8,128)(2,1)S(1)} %collective-permute-done.36.refs_3_, ...), custom_call_target="tpu_custom_call" | custom-call | bytes 1024 | tf_op jit(solution)/shard_map/multiply/pallas_call | solution.py:468
  151.0 1.8 %collective-permute-done.40.refs_4_ = bf16[4,32,1024]{2,1,0:T(8,128)(2,1)S(1)} collective-permute-done((bf16[4,32,1024]{2,1,0:T(8,128)(2,1)S(1)}, bf16[4,32,1024]{2,1,0:T(8,128)(2,1)S(1)}, u32[]{:S(2)}, u32[]{:S(2)}) %collective-permute-start.40) | collective-permute-done | bytes 262176 | tf_op jit(solution)/shard_map/ppermute | solution.py:42
  152.8 5.1 %multiply.7 = bf16[512,640]{1,0:T(8,128)(2,1)} custom-call(bf16[4,32,1536]{2,1,0:T(8,128)(2,1)S(1)} %collective-permute-done.29.refs_0_, bf16[4,32,1024]{2,1,0:T(8,128)(2,1)S(1)} %collective-permute-done.30.refs_1_, bf16[4,32,1664]{2,1,0:T(8,128)(2,1)S(1)} %collective-permute-done.31.refs_2_, bf16[4,32,1536]{2,1,0:T(8,128)(2,1)S(1)} %collective-permute-done.39.refs_3_, ...), custom_call_target="tpu_custom_call" | custom-call | bytes 1024 | tf_op jit(solution)/shard_map/multiply/pallas_call | solution.py:468
  (84 shorter events, 39.8 us)
Async XLA Ops:
  2.7 7.1 %collective-permute-start = (bf16[4,32,9728]{2,1,0:T(8,128)(2,1)S(1)}, bf16[4,32,9728]{2,1,0:T(8,128)(2,1)S(1)}, u32[]{:S(2)}, u32[]{:S(2)}) collective-permute-start(bf16[4,32,9728]{2,1,0:T(8,128)(2,1)S(1)} %give.2.refs_1_), channel_id=1, source_target_pairs={{0,1},{1,0},{2,3},{3,2},{4,5},{5,4},{6,7},{7,6},{8,9},{9,8},{10,11... | collective-permute-start | bytes 7471112 | tf_op jit(solution)/shard_map/ppermute | solution.py:42
  9.8 9.9 %collective-permute-start.1 = (bf16[4,32,23040]{2,1,0:T(8,128)(2,1)}, bf16[4,32,23040]{2,1,0:T(8,128)(2,1)S(1)}, u32[]{:S(2)}, u32[]{:S(2)}) collective-permute-start(bf16[4,32,23040]{2,1,0:T(8,128)(2,1)} %give.3.refs_2_), channel_id=1, source_target_pairs={{0,1},{1,0},{2,3},{3,2},{4,5},{5,4},{6,7},{7,6},{8,9},{9,8},{10,11... | collective-permute-start | bytes 17694728 | tf_op jit(solution)/shard_map/ppermute | solution.py:42
  12.5 15.9 %collective-permute-start.5 = (bf16[4,32,2560]{2,1,0:T(8,128)(2,1)S(1)}, bf16[4,32,2560]{2,1,0:T(8,128)(2,1)S(1)}, u32[]{:S(2)}, u32[]{:S(2)}) collective-permute-start(bf16[4,32,2560]{2,1,0:T(8,128)(2,1)S(1)} %get-tuple-element.44.refs_2_), channel_id=1, source_target_pairs={{0,2},{1,3},{2,0},{3,1},{4,6},{5,7},{6,4},{7,5},{8,10},{9,11},{10,... | collective-permute-start | bytes 1966088 | tf_op jit(solution)/shard_map/ppermute | solution.py:42
  14.0 22.3 %collective-permute-start.6 = (bf16[4,32,3584]{2,1,0:T(8,128)(2,1)S(1)}, bf16[4,32,3584]{2,1,0:T(8,128)(2,1)S(1)}, u32[]{:S(2)}, u32[]{:S(2)}) collective-permute-start(bf16[4,32,3584]{2,1,0:T(8,128)(2,1)S(1)} %get-tuple-element.48), channel_id=1, source_target_pairs={{0,6},{1,7},{2,4},{3,5},{4,2},{5,3},{6,0},{7,1},{8,14},{9,15},{10,... | collective-permute-start | bytes 2752520 | tf_op jit(solution)/shard_map/ppermute | solution.py:42
  15.9 21.2 %collective-permute-start.7 = (bf16[4,32,3584]{2,1,0:T(8,128)(2,1)S(1)}, bf16[4,32,3584]{2,1,0:T(8,128)(2,1)S(1)}, u32[]{:S(2)}, u32[]{:S(2)}) collective-permute-start(bf16[4,32,3584]{2,1,0:T(8,128)(2,1)S(1)} %get-tuple-element.49), channel_id=1, source_target_pairs={{0,8},{1,9},{2,10},{3,11},{4,12},{5,13},{6,14},{7,15},{8,0},{9,1},... | collective-permute-start | bytes 2752520 | tf_op jit(solution)/shard_map/ppermute | solution.py:42
  23.1 25.2 %collective-permute-start.2 = (bf16[4,32,3072]{2,1,0:T(8,128)(2,1)S(1)}, bf16[4,32,3072]{2,1,0:T(8,128)(2,1)S(1)}, u32[]{:S(2)}, u32[]{:S(2)}) collective-permute-start(bf16[4,32,3072]{2,1,0:T(8,128)(2,1)S(1)} %get-tuple-element.45.refs_5_), channel_id=1, source_target_pairs={{0,2},{1,3},{2,0},{3,1},{4,6},{5,7},{6,4},{7,5},{8,10},{9,11},{10,... | collective-permute-start | bytes 2359304 | tf_op jit(solution)/shard_map/ppermute | solution.py:42
  24.6 20.2 %collective-permute-start.3 = (bf16[4,32,1536]{2,1,0:T(8,128)(2,1)S(1)}, bf16[4,32,1536]{2,1,0:T(8,128)(2,1)S(1)}, u32[]{:S(2)}, u32[]{:S(2)}) collective-permute-start(bf16[4,32,1536]{2,1,0:T(8,128)(2,1)S(1)} %get-tuple-element.46), channel_id=1, source_target_pairs={{0,6},{1,7},{2,4},{3,5},{4,2},{5,3},{6,0},{7,1},{8,14},{9,15},{10,... | collective-permute-start | bytes 1179656 | tf_op jit(solution)/shard_map/ppermute | solution.py:42
  28.4 19.9 %collective-permute-start.4 = (bf16[4,32,2048]{2,1,0:T(8,128)(2,1)S(1)}, bf16[4,32,2048]{2,1,0:T(8,128)(2,1)S(1)}, u32[]{:S(2)}, u32[]{:S(2)}) collective-permute-start(bf16[4,32,2048]{2,1,0:T(8,128)(2,1)S(1)} %get-tuple-element.47), channel_id=1, source_target_pairs={{0,8},{1,9},{2,10},{3,11},{4,12},{5,13},{6,14},{7,15},{8,0},{9,1},... | collective-permute-start | bytes 1572872 | tf_op jit(solution)/shard_map/ppermute | solution.py:42
  39.6 12.1 %collective-permute-start.11 = (bf16[2,32,2560]{2,1,0:T(8,128)(2,1)S(1)}, bf16[2,32,2560]{2,1,0:T(8,128)(2,1)S(1)}, u32[]{:S(2)}, u32[]{:S(2)}) collective-permute-start(bf16[2,32,2560]{2,1,0:T(8,128)(2,1)S(1)} %get-tuple-element.50.refs_5_), channel_id=1, source_target_pairs={{0,6},{1,7},{2,4},{3,5},{4,2},{5,3},{6,0},{7,1},{8,14},{9,15},{10,... | collective-permute-start | bytes 983048 | tf_op jit(solution)/shard_map/ppermute | solution.py:42
  40.9 17.3 %collective-permute-start.12 = (bf16[2,32,3584]{2,1,0:T(8,128)(2,1)S(1)}, bf16[2,32,3584]{2,1,0:T(8,128)(2,1)S(1)}, u32[]{:S(2)}, u32[]{:S(2)}) collective-permute-start(bf16[2,32,3584]{2,1,0:T(8,128)(2,1)S(1)} %get-tuple-element.54), channel_id=1, source_target_pairs={{0,8},{1,9},{2,10},{3,11},{4,12},{5,13},{6,14},{7,15},{8,0},{9,1},... | collective-permute-start | bytes 1376264 | tf_op jit(solution)/shard_map/ppermute | solution.py:42
  44.8 13.4 %collective-permute-start.13 = (bf16[2,32,3584]{2,1,0:T(8,128)(2,1)S(1)}, bf16[2,32,3584]{2,1,0:T(8,128)(2,1)S(1)}, u32[]{:S(2)}, u32[]{:S(2)}) collective-permute-start(bf16[2,32,3584]{2,1,0:T(8,128)(2,1)S(1)} %get-tuple-element.55), channel_id=1, source_target_pairs={{0,2},{1,3},{2,0},{3,1},{4,6},{5,7},{6,4},{7,5},{8,10},{9,11},{10,... | collective-permute-start | bytes 1376264 | tf_op jit(solution)/shard_map/ppermute | solution.py:42
  50.2 13.0 %collective-permute-start.8 = (bf16[2,32,3072]{2,1,0:T(8,128)(2,1)S(1)}, bf16[2,32,3072]{2,1,0:T(8,128)(2,1)S(1)}, u32[]{:S(2)}, u32[]{:S(2)}) collective-permute-start(bf16[2,32,3072]{2,1,0:T(8,128)(2,1)S(1)} %get-tuple-element.51.refs_8_), channel_id=1, source_target_pairs={{0,6},{1,7},{2,4},{3,5},{4,2},{5,3},{6,0},{7,1},{8,14},{9,15},{10,... | collective-permute-start | bytes 1179656 | tf_op jit(solution)/shard_map/ppermute | solution.py:42
  51.0 12.2 %collective-permute-start.10 = (bf16[2,32,2048]{2,1,0:T(8,128)(2,1)S(1)}, bf16[2,32,2048]{2,1,0:T(8,128)(2,1)S(1)}, u32[]{:S(2)}, u32[]{:S(2)}) collective-permute-start(bf16[2,32,2048]{2,1,0:T(8,128)(2,1)S(1)} %get-tuple-element.53), channel_id=1, source_target_pairs={{0,2},{1,3},{2,0},{3,1},{4,6},{5,7},{6,4},{7,5},{8,10},{9,11},{10,... | collective-permute-start | bytes 786440 | tf_op jit(solution)/shard_map/ppermute | solution.py:42
  51.8 10.6 %collective-permute-start.9 = (bf16[2,32,1536]{2,1,0:T(8,128)(2,1)S(1)}, bf16[2,32,1536]{2,1,0:T(8,128)(2,1)S(1)}, u32[]{:S(2)}, u32[]{:S(2)}) collective-permute-start(bf16[2,32,1536]{2,1,0:T(8,128)(2,1)S(1)} %get-tuple-element.52), channel_id=1, source_target_pairs={{0,8},{1,9},{2,10},{3,11},{4,12},{5,13},{6,14},{7,15},{8,0},{9,1},... | collective-permute-start | bytes 589832 | tf_op jit(solution)/shard_map/ppermute | solution.py:42
  60.5 7.8 %collective-permute-start.17 = (bf16[1,32,2560]{2,1,0:T(8,128)(2,1)S(1)}, bf16[1,32,2560]{2,1,0:T(8,128)(2,1)S(1)}, u32[]{:S(2)}, u32[]{:S(2)}) collective-permute-start(bf16[1,32,2560]{2,1,0:T(8,128)(2,1)S(1)} %get-tuple-element.56.refs_8_), channel_id=1, source_target_pairs={{0,8},{1,9},{2,10},{3,11},{4,12},{5,13},{6,14},{7,15},{8,0},{9,1},... | collective-permute-start | bytes 491528 | tf_op jit(solution)/shard_map/ppermute | solution.py:42
  61.9 6.5 %collective-permute-start.18 = (bf16[1,32,3584]{2,1,0:T(8,128)(2,1)S(1)}, bf16[1,32,3584]{2,1,0:T(8,128)(2,1)S(1)}, u32[]{:S(2)}, u32[]{:S(2)}) collective-permute-start(bf16[1,32,3584]{2,1,0:T(8,128)(2,1)S(1)} %get-tuple-element.60), channel_id=1, source_target_pairs={{0,2},{1,3},{2,0},{3,1},{4,6},{5,7},{6,4},{7,5},{8,10},{9,11},{10,... | collective-permute-start | bytes 688136 | tf_op jit(solution)/shard_map/ppermute | solution.py:42
  65.2 7.7 %collective-permute-start.14 = (bf16[1,32,3072]{2,1,0:T(8,128)(2,1)S(1)}, bf16[1,32,3072]{2,1,0:T(8,128)(2,1)S(1)}, u32[]{:S(2)}, u32[]{:S(2)}) collective-permute-start(bf16[1,32,3072]{2,1,0:T(8,128)(2,1)S(1)} %get-tuple-element.57.refs_13_), channel_id=1, source_target_pairs={{0,8},{1,9},{2,10},{3,11},{4,12},{5,13},{6,14},{7,15},{8,0},{9,1},... | collective-permute-start | bytes 589832 | tf_op jit(solution)/shard_map/ppermute | solution.py:42
  76.1 7.7 %collective-permute-start.22 = (bf16[32,5760]{1,0:T(8,128)(2,1)S(1)}, bf16[32,5760]{1,0:T(8,128)(2,1)S(1)}, u32[]{:S(2)}, u32[]{:S(2)}) collective-permute-start(bf16[32,5760]{1,0:T(8,128)(2,1)S(1)} %get-tuple-element.70.refs_2_), channel_id=1, source_target_pairs={{0,6},{1,7},{2,4},{3,5},{4,2},{5,3},{6,0},{7,1},{8,14},{9,15},{10,... | collective-permute-start | bytes 1105928 | tf_op jit(solution)/shard_map/ppermute | solution.py:42
  78.3 7.6 %collective-permute-start.20 = (bf16[32,5632]{1,0:T(8,128)(2,1)S(1)}, bf16[32,5632]{1,0:T(8,128)(2,1)S(1)}, u32[]{:S(2)}, u32[]{:S(2)}) collective-permute-start(bf16[32,5632]{1,0:T(8,128)(2,1)S(1)} %get-tuple-element.68.refs_0_), channel_id=1, source_target_pairs={{0,8},{1,9},{2,10},{3,11},{4,12},{5,13},{6,14},{7,15},{8,0},{9,1},... | collective-permute-start | bytes 1081352 | tf_op jit(solution)/shard_map/ppermute | solution.py:42
  78.5 11.5 %collective-permute-start.24 = (bf16[32,5120]{1,0:T(8,128)(2,1)S(1)}, bf16[32,5120]{1,0:T(8,128)(2,1)S(1)}, u32[]{:S(2)}, u32[]{:S(2)}) collective-permute-start(bf16[32,5120]{1,0:T(8,128)(2,1)S(1)} %get-tuple-element.69.refs_1_), channel_id=1, source_target_pairs={{0,8},{1,9},{2,10},{3,11},{4,12},{5,13},{6,14},{7,15},{8,0},{9,1},... | collective-permute-start | bytes 983048 | tf_op jit(solution)/shard_map/ppermute | solution.py:42
  79.8 14.0 %collective-permute-start.25 = (bf16[32,5760]{1,0:T(8,128)(2,1)S(1)}, bf16[32,5760]{1,0:T(8,128)(2,1)S(1)}, u32[]{:S(2)}, u32[]{:S(2)}) collective-permute-start(bf16[32,5760]{1,0:T(8,128)(2,1)S(1)} %get-tuple-element.70.refs_2_), channel_id=1, source_target_pairs={{0,2},{1,3},{2,0},{3,1},{4,6},{5,7},{6,4},{7,5},{8,10},{9,11},{10,... | collective-permute-start | bytes 1105928 | tf_op jit(solution)/shard_map/ppermute | solution.py:42
  83.7 15.6 %collective-permute-start.28 = (bf16[32,5760]{1,0:T(8,128)(2,1)S(1)}, bf16[32,5760]{1,0:T(8,128)(2,1)S(1)}, u32[]{:S(2)}, u32[]{:S(2)}) collective-permute-start(bf16[32,5760]{1,0:T(8,128)(2,1)S(1)} %collective-permute-done.22.refs_5_), channel_id=1, source_target_pairs={{0,2},{1,3},{2,0},{3,1},{4,6},{5,7},{6,4},{7,5},{8,10},{9,11},{10,... | collective-permute-start | bytes 1105928 | tf_op jit(solution)/shard_map/ppermute | solution.py:42
  84.5 9.3 %collective-permute-start.23 = (bf16[32,5632]{1,0:T(8,128)(2,1)S(1)}, bf16[32,5632]{1,0:T(8,128)(2,1)S(1)}, u32[]{:S(2)}, u32[]{:S(2)}) collective-permute-start(bf16[32,5632]{1,0:T(8,128)(2,1)S(1)} %get-tuple-element.68.refs_0_), channel_id=1, source_target_pairs={{0,6},{1,7},{2,4},{3,5},{4,2},{5,3},{6,0},{7,1},{8,14},{9,15},{10,... | collective-permute-start | bytes 1081352 | tf_op jit(solution)/shard_map/ppermute | solution.py:42
  85.9 13.4 %collective-permute-start.26 = (bf16[32,5632]{1,0:T(8,128)(2,1)S(1)}, bf16[32,5632]{1,0:T(8,128)(2,1)S(1)}, u32[]{:S(2)}, u32[]{:S(2)}) collective-permute-start(bf16[32,5632]{1,0:T(8,128)(2,1)S(1)} %collective-permute-done.20.refs_3_), channel_id=1, source_target_pairs={{0,6},{1,7},{2,4},{3,5},{4,2},{5,3},{6,0},{7,1},{8,14},{9,15},{10,... | collective-permute-start | bytes 1081352 | tf_op jit(solution)/shard_map/ppermute | solution.py:42
  90.1 9.2 %collective-permute-start.27 = (bf16[32,5120]{1,0:T(8,128)(2,1)S(1)}, bf16[32,5120]{1,0:T(8,128)(2,1)S(1)}, u32[]{:S(2)}, u32[]{:S(2)}) collective-permute-start(bf16[32,5120]{1,0:T(8,128)(2,1)S(1)} %collective-permute-done.21.refs_4_), channel_id=1, source_target_pairs={{0,8},{1,9},{2,10},{3,11},{4,12},{5,13},{6,14},{7,15},{8,0},{9,1},... | collective-permute-start | bytes 983048 | tf_op jit(solution)/shard_map/ppermute | solution.py:42
  100.8 14.3 %collective-permute-start.35 = (bf16[4,32,16512]{2,1,0:T(8,128)(2,1)S(1)}, bf16[4,32,16512]{2,1,0:T(8,128)(2,1)S(1)}, u32[]{:S(2)}, u32[]{:S(2)}) collective-permute-start(bf16[4,32,16512]{2,1,0:T(8,128)(2,1)S(1)} %get-tuple-element.77), channel_id=1, source_target_pairs={{0,1},{1,0},{2,3},{3,2},{4,5},{5,4},{6,7},{7,6},{8,9},{9,8},{10,11... | collective-permute-start | bytes 12681224 | tf_op jit(solution)/shard_map/ppermute | solution.py:42
  108.3 24.7 %collective-permute-start.32 = (bf16[4,32,4096]{2,1,0:T(8,128)(2,1)S(1)}, bf16[4,32,4096]{2,1,0:T(8,128)(2,1)S(1)}, u32[]{:S(2)}, u32[]{:S(2)}) collective-permute-start(bf16[4,32,4096]{2,1,0:T(8,128)(2,1)S(1)} %get-tuple-element.74.refs_0_), channel_id=1, source_target_pairs={{0,2},{1,3},{2,0},{3,1},{4,6},{5,7},{6,4},{7,5},{8,10},{9,11},{10,... | collective-permute-start | bytes 3145736 | tf_op jit(solution)/shard_map/ppermute | solution.py:42
  108.3 25.8 %collective-permute-start.33 = (bf16[4,32,4096]{2,1,0:T(8,128)(2,1)S(1)}, bf16[4,32,4096]{2,1,0:T(8,128)(2,1)S(1)}, u32[]{:S(2)}, u32[]{:S(2)}) collective-permute-start(bf16[4,32,4096]{2,1,0:T(8,128)(2,1)S(1)} %get-tuple-element.75.refs_1_), channel_id=1, source_target_pairs={{0,6},{1,7},{2,4},{3,5},{4,2},{5,3},{6,0},{7,1},{8,14},{9,15},{10,... | collective-permute-start | bytes 3145736 | tf_op jit(solution)/shard_map/ppermute | solution.py:42
  110.1 24.3 %collective-permute-start.34 = (bf16[4,32,4096]{2,1,0:T(8,128)(2,1)S(1)}, bf16[4,32,4096]{2,1,0:T(8,128)(2,1)S(1)}, u32[]{:S(2)}, u32[]{:S(2)}) collective-permute-start(bf16[4,32,4096]{2,1,0:T(8,128)(2,1)S(1)} %get-tuple-element.76.refs_2_), channel_id=1, source_target_pairs={{0,8},{1,9},{2,10},{3,11},{4,12},{5,13},{6,14},{7,15},{8,0},{9,1},... | collective-permute-start | bytes 3145736 | tf_op jit(solution)/shard_map/ppermute | solution.py:42
  136.2 13.8 %collective-permute-start.31 = (bf16[4,32,1664]{2,1,0:T(8,128)(2,1)S(1)}, bf16[4,32,1664]{2,1,0:T(8,128)(2,1)S(1)}, u32[]{:S(2)}, u32[]{:S(2)}) collective-permute-start(bf16[4,32,1664]{2,1,0:T(8,128)(2,1)S(1)} %get-tuple-element.73.refs_2_.refs_6_), channel_id=1, source_target_pairs={{0,8},{1,9},{2,10},{3,11},{4,12},{5,13},{6,14},{7,15},{8,0},{9,1},... | collective-permute-start | bytes 1277960 | tf_op jit(solution)/shard_map/ppermute | solution.py:42
  137.5 12.5 %collective-permute-start.29 = (bf16[4,32,1536]{2,1,0:T(8,128)(2,1)S(1)}, bf16[4,32,1536]{2,1,0:T(8,128)(2,1)S(1)}, u32[]{:S(2)}, u32[]{:S(2)}) collective-permute-start(bf16[4,32,1536]{2,1,0:T(8,128)(2,1)S(1)} %get-tuple-element.71.refs_0_), channel_id=1, source_target_pairs={{0,2},{1,3},{2,0},{3,1},{4,6},{5,7},{6,4},{7,5},{8,10},{9,11},{10,... | collective-permute-start | bytes 1179656 | tf_op jit(solution)/shard_map/ppermute | solution.py:42
  138.3 11.6 %collective-permute-start.30 = (bf16[4,32,1024]{2,1,0:T(8,128)(2,1)S(1)}, bf16[4,32,1024]{2,1,0:T(8,128)(2,1)S(1)}, u32[]{:S(2)}, u32[]{:S(2)}) collective-permute-start(bf16[4,32,1024]{2,1,0:T(8,128)(2,1)S(1)} %get-tuple-element.72.refs_1_), channel_id=1, source_target_pairs={{0,6},{1,7},{2,4},{3,5},{4,2},{5,3},{6,0},{7,1},{8,14},{9,15},{10,... | collective-permute-start | bytes 786440 | tf_op jit(solution)/shard_map/ppermute | solution.py:42
  (17 other events, 121.1 us)

commit v5 on v4

--- a/solution.py
+++ b/solution.py
@@ -423,13 +423,17 @@
         for k, part in enumerate(stream.parts):
             half_depth = part.features // 2
             start = stream.offsets[k]
+            depth = part.features if k else half_depth
             for copy in [loads[k][0], *loads[k][2:]]:
                 copy.wait()
-            here = pl.ds(start, half_depth)
+            if k:
+                loads[k][1].wait()
+            here = pl.ds(start, depth)
             product = jnp.dot(rows[:, here], held[here, :], preferred_element_type=jnp.float32)
-            loads[k][1].wait()
-            here = pl.ds(start + half_depth, half_depth)
-            product += jnp.dot(rows[:, here], held[here, :], preferred_element_type=jnp.float32)
+            if not k:
+                loads[k][1].wait()
+                here = pl.ds(start + depth, depth)
+                product += jnp.dot(rows[:, here], held[here, :], preferred_element_type=jnp.float32)
             if more and k == 0:
                 before.wait()
             for c in range(NC):

time: 158 us -> 158 us (level)
  no operation moved by 1% of the time
where the time goes in v5:
time: 158 us; the launch traced here: 157 us
  Pallas kernels  56.8 us (36%)
  waiting for transfers between devices  51.4 us (33%)
  starting transfers between devices  48 us (30%)
    ppermute x42, waiting for transfers between devices, send(): return lax.ppermute(x, 'tensor', where)  51.4 us
    ppermute x42, starting transfers between devices, send(): return lax.ppermute(x, 'tensor', where)  48 us
    pallas_call x11, Pallas kernels, call(): pl.pallas_call(lambda *refs: kernel(where_am_i(), *refs), in_specs=[ANY]...  31 us
    pallas_call x4, Pallas kernels, multiplied(): pl.pallas_call(kernel, in_specs=[ANY] * (n + 1 + len(more) + len(after)),...  25.8 us
  transfers between devices with their start and end apart: 42, of which 22 were waited for; matrix products, arithmetic and copies ran while one was open for 0% of the time, Pallas kernels for 29%

profile of v5, /device:TPU:1, one launch (start us, length us, event | category | flops | bytes accessed | tf_op | source)
XLA Modules:
  0.0 157.4 jit_solution(995266659645661786)
XLA Ops:
  0.6 2.1 %give.2.refs_1_ = bf16[4,32,9728]{2,1,0:T(8,128)(2,1)S(1)} custom-call(bf16[16,32,16384]{2,1,0:T(8,128)(2,1)} %bitcast.8), custom_call_target="tpu_custom_call" | custom-call | bytes 1024 | tf_op jit(solution)/shard_map/give/pallas_call | solution.py:88
  4.2 5.6 %give.3.refs_2_ = bf16[4,32,23040]{2,1,0:T(8,128)(2,1)} custom-call(bf16[16,32,16384]{2,1,0:T(8,128)(2,1)} %bitcast.9, bf16[4,32,9728]{2,1,0:T(8,128)(2,1)S(1)} %give.2.refs_1_), custom_call_target="tpu_custom_call" | custom-call | bytes 1024 | tf_op jit(solution)/shard_map/give/pallas_call | solution.py:88
  10.0 2.6 %first.2 = (bf16[4,32,2560]{2,1,0:T(8,128)(2,1)S(1)}, bf16[4,32,3584]{2,1,0:T(8,128)(2,1)S(1)}, bf16[4,32,3584]{2,1,0:T(8,128)(2,1)S(1)}) custom-call(bf16[16,32,16384]{2,1,0:T(8,128)(2,1)} %bitcast.10, bf16[4,32,9728]{2,1,0:T(8,128)(2,1)S(1)} %collective-permute-done.refs_1_, bf16[4,32,23040]{2,1,0:T(8,128)(2,1)} %give.3.refs_2_), custom_call_target="tpu_custom_call" | custom-call | bytes 1024 | tf_op jit(solution)/shard_map/first/pallas_call | solution.py:88
  14.0 1.9 %collective-permute-start.6 = (bf16[4,32,3584]{2,1,0:T(8,128)(2,1)S(1)}, bf16[4,32,3584]{2,1,0:T(8,128)(2,1)S(1)}, u32[]{:S(2)}, u32[]{:S(2)}) collective-permute-start(bf16[4,32,3584]{2,1,0:T(8,128)(2,1)S(1)} %get-tuple-element.48), channel_id=1, source_target_pairs={{0,6},{1,7},{2,4},{3,5},{4,2},{5,3},{6,0},{7,1},{8,14},{9,15},{10,... | collective-permute-start | bytes 2752520 | tf_op jit(solution)/shard_map/ppermute | solution.py:42
  17.5 2.2 %collective-permute-done.1.refs_1_ = bf16[4,32,23040]{2,1,0:T(8,128)(2,1)S(1)} collective-permute-done((bf16[4,32,23040]{2,1,0:T(8,128)(2,1)}, bf16[4,32,23040]{2,1,0:T(8,128)(2,1)S(1)}, u32[]{:S(2)}, u32[]{:S(2)}) %collective-permute-start.1) | collective-permute-done | bytes 5898272 | tf_op jit(solution)/shard_map/ppermute | solution.py:42
  19.7 3.4 %first.3 = (bf16[4,32,3072]{2,1,0:T(8,128)(2,1)S(1)}, bf16[4,32,1536]{2,1,0:T(8,128)(2,1)S(1)}, bf16[4,32,2048]{2,1,0:T(8,128)(2,1)S(1)}) custom-call(bf16[16,32,16384]{2,1,0:T(8,128)(2,1)} %bitcast.11, bf16[4,32,23040]{2,1,0:T(8,128)(2,1)S(1)} %collective-permute-done.1.refs_1_, bf16[4,32,2560]{2,1,0:T(8,128)(2,1)S(1)} %get-tuple-element.44.refs_2_), custom_call_target="tpu_custom_call" | custom-call | bytes 1024 | tf_op jit(solution)/shard_map/first/pallas_call | solution.py:88
  24.6 1.9 %collective-permute-start.3 = (bf16[4,32,1536]{2,1,0:T(8,128)(2,1)S(1)}, bf16[4,32,1536]{2,1,0:T(8,128)(2,1)S(1)}, u32[]{:S(2)}, u32[]{:S(2)}) collective-permute-start(bf16[4,32,1536]{2,1,0:T(8,128)(2,1)S(1)} %get-tuple-element.46), channel_id=1, source_target_pairs={{0,6},{1,7},{2,4},{3,5},{4,2},{5,3},{6,0},{7,1},{8,14},{9,15},{10,... | collective-permute-start | bytes 1179656 | tf_op jit(solution)/shard_map/ppermute | solution.py:42
  26.5 2.0 %collective-permute-done.5.refs_2_ = bf16[4,32,2560]{2,1,0:T(8,128)(2,1)S(1)} collective-permute-done((bf16[4,32,2560]{2,1,0:T(8,128)(2,1)S(1)}, bf16[4,32,2560]{2,1,0:T(8,128)(2,1)S(1)}, u32[]{:S(2)}, u32[]{:S(2)}) %collective-permute-start.5) | collective-permute-done | bytes 655392 | tf_op jit(solution)/shard_map/ppermute | solution.py:42
  30.2 6.2 %collective-permute-done.6.refs_3_ = bf16[4,32,3584]{2,1,0:T(8,128)(2,1)S(1)} collective-permute-done((bf16[4,32,3584]{2,1,0:T(8,128)(2,1)S(1)}, bf16[4,32,3584]{2,1,0:T(8,128)(2,1)S(1)}, u32[]{:S(2)}, u32[]{:S(2)}) %collective-permute-start.6) | collective-permute-done | bytes 917536 | tf_op jit(solution)/shard_map/ppermute | solution.py:42
  37.1 2.6 %second.2 = (bf16[2,32,2560]{2,1,0:T(8,128)(2,1)S(1)}, bf16[2,32,3584]{2,1,0:T(8,128)(2,1)S(1)}, bf16[2,32,3584]{2,1,0:T(8,128)(2,1)S(1)}) custom-call(bf16[16,32,16384]{2,1,0:T(8,128)(2,1)} %bitcast.12, bf16[4,32,23040]{2,1,0:T(8,128)(2,1)} %copy-done, bf16[4,32,2560]{2,1,0:T(8,128)(2,1)S(1)} %collective-permute-done.5.refs_2_, ...), custom_call_target="tpu_custom_call" | custom-call | bytes 1024 | tf_op jit(solution)/shard_map/second/pallas_call | solution.py:88
  42.5 2.2 %collective-permute-done.3.refs_3_ = bf16[4,32,1536]{2,1,0:T(8,128)(2,1)S(1)} collective-permute-done((bf16[4,32,1536]{2,1,0:T(8,128)(2,1)S(1)}, bf16[4,32,1536]{2,1,0:T(8,128)(2,1)S(1)}, u32[]{:S(2)}, u32[]{:S(2)}) %collective-permute-start.3) | collective-permute-done | bytes 393248 | tf_op jit(solution)/shard_map/ppermute | solution.py:42
  44.8 3.5 %collective-permute-done.4.refs_4_ = bf16[4,32,2048]{2,1,0:T(8,128)(2,1)S(1)} collective-permute-done((bf16[4,32,2048]{2,1,0:T(8,128)(2,1)S(1)}, bf16[4,32,2048]{2,1,0:T(8,128)(2,1)S(1)}, u32[]{:S(2)}, u32[]{:S(2)}) %collective-permute-start.4) | collective-permute-done | bytes 524320 | tf_op jit(solution)/shard_map/ppermute | solution.py:42
  48.3 1.9 %second.3 = (bf16[2,32,3072]{2,1,0:T(8,128)(2,1)S(1)}, bf16[2,32,1536]{2,1,0:T(8,128)(2,1)S(1)}, bf16[2,32,2048]{2,1,0:T(8,128)(2,1)S(1)}) custom-call(bf16[16,32,16384]{2,1,0:T(8,128)(2,1)} %bitcast.13, bf16[4,32,23040]{2,1,0:T(8,128)(2,1)S(1)} %bitcast.3, bf16[4,32,3072]{2,1,0:T(8,128)(2,1)S(1)} %collective-permute-done.2.refs_2_, ...), custom_call_target="tpu_custom_call" | custom-call | bytes 1024 | tf_op jit(solution)/shard_map/second/pallas_call | solution.py:88
  53.4 4.8 %collective-permute-done.12.refs_6_ = bf16[2,32,3584]{2,1,0:T(8,128)(2,1)S(1)} collective-permute-done((bf16[2,32,3584]{2,1,0:T(8,128)(2,1)S(1)}, bf16[2,32,3584]{2,1,0:T(8,128)(2,1)S(1)}, u32[]{:S(2)}, u32[]{:S(2)}) %collective-permute-start.12) | collective-permute-done | bytes 458784 | tf_op jit(solution)/shard_map/ppermute | solution.py:42
  58.1 2.4 %third.2 = (bf16[1,32,2560]{2,1,0:T(8,128)(2,1)S(1)}, bf16[1,32,3584]{2,1,0:T(8,128)(2,1)S(1)}, bf16[1,32,3584]{2,1,0:T(8,128)(2,1)S(1)}) custom-call(bf16[16,32,16384]{2,1,0:T(8,128)(2,1)} %bitcast.14, bf16[4,32,23040]{2,1,0:T(8,128)(2,1)} %copy-done, bf16[4,32,2560]{2,1,0:T(8,128)(2,1)S(1)} %collective-permute-done.5.refs_2_, ...), custom_call_target="tpu_custom_call" | custom-call | bytes 1024 | tf_op jit(solution)/shard_map/third/pallas_call | solution.py:88
  63.2 1.9 %third.3 = (bf16[1,32,3072]{2,1,0:T(8,128)(2,1)S(1)}, bf16[1,32,1536]{2,1,0:T(8,128)(2,1)S(1)}, bf16[1,32,2048]{2,1,0:T(8,128)(2,1)S(1)}) custom-call(bf16[16,32,16384]{2,1,0:T(8,128)(2,1)} %bitcast.15, bf16[4,32,23040]{2,1,0:T(8,128)(2,1)S(1)} %bitcast.5, bf16[4,32,3072]{2,1,0:T(8,128)(2,1)S(1)} %collective-permute-done.2.refs_2_, ...), custom_call_target="tpu_custom_call" | custom-call | bytes 1024 | tf_op jit(solution)/shard_map/third/pallas_call | solution.py:88
  66.4 1.9 %collective-permute-start.16 = (bf16[1,32,2048]{2,1,0:T(8,128)(2,1)S(1)}, bf16[1,32,2048]{2,1,0:T(8,128)(2,1)S(1)}, u32[]{:S(2)}, u32[]{:S(2)}) collective-permute-start(bf16[1,32,2048]{2,1,0:T(8,128)(2,1)S(1)} %get-tuple-element.59), channel_id=1, source_target_pairs={{0,6},{1,7},{2,4},{3,5},{4,2},{5,3},{6,0},{7,1},{8,14},{9,15},{10,... | collective-permute-start | bytes 393224 | tf_op jit(solution)/shard_map/ppermute | solution.py:42
  68.4 3.9 %finish.2 = (bf16[32,16384]{1,0:T(8,128)(2,1)}, bf16[32,5632]{1,0:T(8,128)(2,1)S(1)}, bf16[32,5120]{1,0:T(8,128)(2,1)S(1)}, bf16[32,5760]{1,0:T(8,128)(2,1)S(1)}, f32[32,128]{1,0:T(8,128)S(1)}) custom-call(bf16[16,32,16384]{2,1,0:T(8,128)(2,1)} %bitcast.16, bf16[4,32,23040]{2,1,0:T(8,128)(2,1)} %copy-done, ...), custom_call_target="tpu_custom_call" | custom-call | bytes 1024 | tf_op jit(solution)/shard_map/finish/pallas_call | solution.py:88
  72.8 3.2 %finish.3 = (bf16[32,16384]{1,0:T(8,128)(2,1)}, bf16[32,5632]{1,0:T(8,128)(2,1)S(1)}, bf16[32,5120]{1,0:T(8,128)(2,1)S(1)}, bf16[32,5760]{1,0:T(8,128)(2,1)S(1)}, f32[32,128]{1,0:T(8,128)}) custom-call(bf16[16,32,16384]{2,1,0:T(8,128)(2,1)} %bitcast.17, ...), custom_call_target="tpu_custom_call", output_to_operand_aliasing={{0}: (13, {}), {1}: (14, {}), {2}: (15, {}), {3}: (16, {})} | custom-call | bytes 1024 | tf_op jit(solution)/shard_map/finish/pallas_call | solution.py:88
  76.1 2.2 %collective-permute-start.22 = (bf16[32,5760]{1,0:T(8,128)(2,1)S(1)}, bf16[32,5760]{1,0:T(8,128)(2,1)S(1)}, u32[]{:S(2)}, u32[]{:S(2)}) collective-permute-start(bf16[32,5760]{1,0:T(8,128)(2,1)S(1)} %get-tuple-element.70.refs_2_), channel_id=1, source_target_pairs={{0,6},{1,7},{2,4},{3,5},{4,2},{5,3},{6,0},{7,1},{8,14},{9,15},{10,... | collective-permute-start | bytes 1105928 | tf_op jit(solution)/shard_map/ppermute | solution.py:42
  81.2 2.5 %collective-permute-done.22.refs_5_ = bf16[32,5760]{1,0:T(8,128)(2,1)S(1)} collective-permute-done((bf16[32,5760]{1,0:T(8,128)(2,1)S(1)}, bf16[32,5760]{1,0:T(8,128)(2,1)S(1)}, u32[]{:S(2)}, u32[]{:S(2)}) %collective-permute-start.22) | collective-permute-done | bytes 368672 | tf_op jit(solution)/shard_map/ppermute | solution.py:42
  87.2 2.9 %collective-permute-done.24.refs_7_ = bf16[32,5120]{1,0:T(8,128)(2,1)S(1)} collective-permute-done((bf16[32,5120]{1,0:T(8,128)(2,1)S(1)}, bf16[32,5120]{1,0:T(8,128)(2,1)S(1)}, u32[]{:S(2)}, u32[]{:S(2)}) %collective-permute-start.24) | collective-permute-done | bytes 327712 | tf_op jit(solution)/shard_map/ppermute | solution.py:42
  90.8 3.0 %collective-permute-done.23.refs_6_ = bf16[32,5632]{1,0:T(8,128)(2,1)S(1)} collective-permute-done((bf16[32,5632]{1,0:T(8,128)(2,1)S(1)}, bf16[32,5632]{1,0:T(8,128)(2,1)S(1)}, u32[]{:S(2)}, u32[]{:S(2)}) %collective-permute-start.23) | collective-permute-done | bytes 360480 | tf_op jit(solution)/shard_map/ppermute | solution.py:42
  93.8 5.5 %collective-permute-done.27.refs_10_ = bf16[32,5120]{1,0:T(8,128)(2,1)S(1)} collective-permute-done((bf16[32,5120]{1,0:T(8,128)(2,1)S(1)}, bf16[32,5120]{1,0:T(8,128)(2,1)S(1)}, u32[]{:S(2)}, u32[]{:S(2)}) %collective-permute-start.27) | collective-permute-done | bytes 327712 | tf_op jit(solution)/shard_map/ppermute | solution.py:42
  100.8 7.5 %collective-permute-start.35 = (bf16[4,32,16512]{2,1,0:T(8,128)(2,1)S(1)}, bf16[4,32,16512]{2,1,0:T(8,128)(2,1)S(1)}, u32[]{:S(2)}, u32[]{:S(2)}) collective-permute-start(bf16[4,32,16512]{2,1,0:T(8,128)(2,1)S(1)} %get-tuple-element.77), channel_id=1, source_target_pairs={{0,1},{1,0},{2,3},{3,2},{4,5},{5,4},{6,7},{7,6},{8,9},{9,8},{10,11... | collective-permute-start | bytes 12681224 | tf_op jit(solution)/shard_map/ppermute | solution.py:42
  111.4 3.8 %collective-permute-done.35.refs_3_.refs_7_ = bf16[4,32,16512]{2,1,0:T(8,128)(2,1)S(1)} collective-permute-done((bf16[4,32,16512]{2,1,0:T(8,128)(2,1)S(1)}, bf16[4,32,16512]{2,1,0:T(8,128)(2,1)S(1)}, u32[]{:S(2)}, u32[]{:S(2)}) %collective-permute-start.35) | collective-permute-done | bytes 4227104 | tf_op jit(solution)/shard_map/ppermute | solution.py:42
  115.1 8.3 %multiply.4.refs_5_ = f32[512,640]{1,0:T(8,128)S(1)} custom-call(bf16[4,32,4096]{2,1,0:T(8,128)(2,1)S(1)} %get-tuple-element.74.refs_0_, bf16[4,32,4096]{2,1,0:T(8,128)(2,1)S(1)} %get-tuple-element.75.refs_1_, bf16[4,32,4096]{2,1,0:T(8,128)(2,1)S(1)} %get-tuple-element.76.refs_2_, bf16[4,32,16512]{2,1,0:T(8,128)(2,1)S(1)} %collective-permute-done.35.refs_3_.refs_7_, ...), custom_call_target="tpu_custom_call" | custom-call | bytes 1024 | tf_op jit(solution)/shard_map/multiply/pallas_call | solution.py:472
  123.5 4.1 %multiply.5.refs_7_ = f32[512,640]{1,0:T(8,128)S(1)} custom-call(bf16[4,32,1536]{2,1,0:T(8,128)(2,1)S(1)} %get-tuple-element.71.refs_0_, bf16[4,32,1024]{2,1,0:T(8,128)(2,1)S(1)} %get-tuple-element.72.refs_1_, bf16[4,32,1664]{2,1,0:T(8,128)(2,1)S(1)} %get-tuple-element.73.refs_2_.refs_6_, bf16[4,32,16512]{2,1,0:T(8,128)(2,1)S(1)} %collective-permute-done.35.refs_3_.refs_7_, ...), custom_call_target="tpu_custom_call" | custom-call | bytes 1024 | tf_op jit(solution)/shard_map/multiply/pallas_call | solution.py:472
  127.6 5.4 %collective-permute-done.32.refs_0_ = bf16[4,32,4096]{2,1,0:T(8,128)(2,1)S(1)} collective-permute-done((bf16[4,32,4096]{2,1,0:T(8,128)(2,1)S(1)}, bf16[4,32,4096]{2,1,0:T(8,128)(2,1)S(1)}, u32[]{:S(2)}, u32[]{:S(2)}) %collective-permute-start.32) | collective-permute-done | bytes 1048608 | tf_op jit(solution)/shard_map/ppermute | solution.py:42
  141.0 8.4 %multiply.6.refs_9_ = f32[512,640]{1,0:T(8,128)S(1)} custom-call(bf16[4,32,4096]{2,1,0:T(8,128)(2,1)S(1)} %collective-permute-done.32.refs_0_, bf16[4,32,4096]{2,1,0:T(8,128)(2,1)S(1)} %collective-permute-done.33.refs_1_, bf16[4,32,4096]{2,1,0:T(8,128)(2,1)S(1)} %collective-permute-done.34.refs_2_, bf16[4,32,4096]{2,1,0:T(8,128)(2,1)S(1)} %collective-permute-done.36.refs_3_, ...), custom_call_target="tpu_custom_call" | custom-call | bytes 1024 | tf_op jit(solution)/shard_map/multiply/pallas_call | solution.py:472
  150.4 1.8 %collective-permute-done.40.refs_4_ = bf16[4,32,1024]{2,1,0:T(8,128)(2,1)S(1)} collective-permute-done((bf16[4,32,1024]{2,1,0:T(8,128)(2,1)S(1)}, bf16[4,32,1024]{2,1,0:T(8,128)(2,1)S(1)}, u32[]{:S(2)}, u32[]{:S(2)}) %collective-permute-start.40) | collective-permute-done | bytes 262176 | tf_op jit(solution)/shard_map/ppermute | solution.py:42
  152.2 5.0 %multiply.7 = bf16[512,640]{1,0:T(8,128)(2,1)} custom-call(bf16[4,32,1536]{2,1,0:T(8,128)(2,1)S(1)} %collective-permute-done.29.refs_0_, bf16[4,32,1024]{2,1,0:T(8,128)(2,1)S(1)} %collective-permute-done.30.refs_1_, bf16[4,32,1664]{2,1,0:T(8,128)(2,1)S(1)} %collective-permute-done.31.refs_2_, bf16[4,32,1536]{2,1,0:T(8,128)(2,1)S(1)} %collective-permute-done.39.refs_3_, ...), custom_call_target="tpu_custom_call" | custom-call | bytes 1024 | tf_op jit(solution)/shard_map/multiply/pallas_call | solution.py:472
  (84 shorter events, 39.8 us)
Async XLA Ops:
  2.7 7.1 %collective-permute-start = (bf16[4,32,9728]{2,1,0:T(8,128)(2,1)S(1)}, bf16[4,32,9728]{2,1,0:T(8,128)(2,1)S(1)}, u32[]{:S(2)}, u32[]{:S(2)}) collective-permute-start(bf16[4,32,9728]{2,1,0:T(8,128)(2,1)S(1)} %give.2.refs_1_), channel_id=1, source_target_pairs={{0,1},{1,0},{2,3},{3,2},{4,5},{5,4},{6,7},{7,6},{8,9},{9,8},{10,11... | collective-permute-start | bytes 7471112 | tf_op jit(solution)/shard_map/ppermute | solution.py:42
  9.8 9.9 %collective-permute-start.1 = (bf16[4,32,23040]{2,1,0:T(8,128)(2,1)}, bf16[4,32,23040]{2,1,0:T(8,128)(2,1)S(1)}, u32[]{:S(2)}, u32[]{:S(2)}) collective-permute-start(bf16[4,32,23040]{2,1,0:T(8,128)(2,1)} %give.3.refs_2_), channel_id=1, source_target_pairs={{0,1},{1,0},{2,3},{3,2},{4,5},{5,4},{6,7},{7,6},{8,9},{9,8},{10,11... | collective-permute-start | bytes 17694728 | tf_op jit(solution)/shard_map/ppermute | solution.py:42
  12.5 15.9 %collective-permute-start.5 = (bf16[4,32,2560]{2,1,0:T(8,128)(2,1)S(1)}, bf16[4,32,2560]{2,1,0:T(8,128)(2,1)S(1)}, u32[]{:S(2)}, u32[]{:S(2)}) collective-permute-start(bf16[4,32,2560]{2,1,0:T(8,128)(2,1)S(1)} %get-tuple-element.44.refs_2_), channel_id=1, source_target_pairs={{0,2},{1,3},{2,0},{3,1},{4,6},{5,7},{6,4},{7,5},{8,10},{9,11},{10,... | collective-permute-start | bytes 1966088 | tf_op jit(solution)/shard_map/ppermute | solution.py:42
  14.0 22.3 %collective-permute-start.6 = (bf16[4,32,3584]{2,1,0:T(8,128)(2,1)S(1)}, bf16[4,32,3584]{2,1,0:T(8,128)(2,1)S(1)}, u32[]{:S(2)}, u32[]{:S(2)}) collective-permute-start(bf16[4,32,3584]{2,1,0:T(8,128)(2,1)S(1)} %get-tuple-element.48), channel_id=1, source_target_pairs={{0,6},{1,7},{2,4},{3,5},{4,2},{5,3},{6,0},{7,1},{8,14},{9,15},{10,... | collective-permute-start | bytes 2752520 | tf_op jit(solution)/shard_map/ppermute | solution.py:42
  15.9 21.2 %collective-permute-start.7 = (bf16[4,32,3584]{2,1,0:T(8,128)(2,1)S(1)}, bf16[4,32,3584]{2,1,0:T(8,128)(2,1)S(1)}, u32[]{:S(2)}, u32[]{:S(2)}) collective-permute-start(bf16[4,32,3584]{2,1,0:T(8,128)(2,1)S(1)} %get-tuple-element.49), channel_id=1, source_target_pairs={{0,8},{1,9},{2,10},{3,11},{4,12},{5,13},{6,14},{7,15},{8,0},{9,1},... | collective-permute-start | bytes 2752520 | tf_op jit(solution)/shard_map/ppermute | solution.py:42
  23.1 25.2 %collective-permute-start.2 = (bf16[4,32,3072]{2,1,0:T(8,128)(2,1)S(1)}, bf16[4,32,3072]{2,1,0:T(8,128)(2,1)S(1)}, u32[]{:S(2)}, u32[]{:S(2)}) collective-permute-start(bf16[4,32,3072]{2,1,0:T(8,128)(2,1)S(1)} %get-tuple-element.45.refs_5_), channel_id=1, source_target_pairs={{0,2},{1,3},{2,0},{3,1},{4,6},{5,7},{6,4},{7,5},{8,10},{9,11},{10,... | collective-permute-start | bytes 2359304 | tf_op jit(solution)/shard_map/ppermute | solution.py:42
  24.6 20.2 %collective-permute-start.3 = (bf16[4,32,1536]{2,1,0:T(8,128)(2,1)S(1)}, bf16[4,32,1536]{2,1,0:T(8,128)(2,1)S(1)}, u32[]{:S(2)}, u32[]{:S(2)}) collective-permute-start(bf16[4,32,1536]{2,1,0:T(8,128)(2,1)S(1)} %get-tuple-element.46), channel_id=1, source_target_pairs={{0,6},{1,7},{2,4},{3,5},{4,2},{5,3},{6,0},{7,1},{8,14},{9,15},{10,... | collective-permute-start | bytes 1179656 | tf_op jit(solution)/shard_map/ppermute | solution.py:42
  28.4 19.9 %collective-permute-start.4 = (bf16[4,32,2048]{2,1,0:T(8,128)(2,1)S(1)}, bf16[4,32,2048]{2,1,0:T(8,128)(2,1)S(1)}, u32[]{:S(2)}, u32[]{:S(2)}) collective-permute-start(bf16[4,32,2048]{2,1,0:T(8,128)(2,1)S(1)} %get-tuple-element.47), channel_id=1, source_target_pairs={{0,8},{1,9},{2,10},{3,11},{4,12},{5,13},{6,14},{7,15},{8,0},{9,1},... | collective-permute-start | bytes 1572872 | tf_op jit(solution)/shard_map/ppermute | solution.py:42
  39.6 12.1 %collective-permute-start.11 = (bf16[2,32,2560]{2,1,0:T(8,128)(2,1)S(1)}, bf16[2,32,2560]{2,1,0:T(8,128)(2,1)S(1)}, u32[]{:S(2)}, u32[]{:S(2)}) collective-permute-start(bf16[2,32,2560]{2,1,0:T(8,128)(2,1)S(1)} %get-tuple-element.50.refs_5_), channel_id=1, source_target_pairs={{0,6},{1,7},{2,4},{3,5},{4,2},{5,3},{6,0},{7,1},{8,14},{9,15},{10,... | collective-permute-start | bytes 983048 | tf_op jit(solution)/shard_map/ppermute | solution.py:42
  40.9 17.3 %collective-permute-start.12 = (bf16[2,32,3584]{2,1,0:T(8,128)(2,1)S(1)}, bf16[2,32,3584]{2,1,0:T(8,128)(2,1)S(1)}, u32[]{:S(2)}, u32[]{:S(2)}) collective-permute-start(bf16[2,32,3584]{2,1,0:T(8,128)(2,1)S(1)} %get-tuple-element.54), channel_id=1, source_target_pairs={{0,8},{1,9},{2,10},{3,11},{4,12},{5,13},{6,14},{7,15},{8,0},{9,1},... | collective-permute-start | bytes 1376264 | tf_op jit(solution)/shard_map/ppermute | solution.py:42
  44.8 13.4 %collective-permute-start.13 = (bf16[2,32,3584]{2,1,0:T(8,128)(2,1)S(1)}, bf16[2,32,3584]{2,1,0:T(8,128)(2,1)S(1)}, u32[]{:S(2)}, u32[]{:S(2)}) collective-permute-start(bf16[2,32,3584]{2,1,0:T(8,128)(2,1)S(1)} %get-tuple-element.55), channel_id=1, source_target_pairs={{0,2},{1,3},{2,0},{3,1},{4,6},{5,7},{6,4},{7,5},{8,10},{9,11},{10,... | collective-permute-start | bytes 1376264 | tf_op jit(solution)/shard_map/ppermute | solution.py:42
  50.2 13.0 %collective-permute-start.8 = (bf16[2,32,3072]{2,1,0:T(8,128)(2,1)S(1)}, bf16[2,32,3072]{2,1,0:T(8,128)(2,1)S(1)}, u32[]{:S(2)}, u32[]{:S(2)}) collective-permute-start(bf16[2,32,3072]{2,1,0:T(8,128)(2,1)S(1)} %get-tuple-element.51.refs_8_), channel_id=1, source_target_pairs={{0,6},{1,7},{2,4},{3,5},{4,2},{5,3},{6,0},{7,1},{8,14},{9,15},{10,... | collective-permute-start | bytes 1179656 | tf_op jit(solution)/shard_map/ppermute | solution.py:42
  51.0 12.2 %collective-permute-start.10 = (bf16[2,32,2048]{2,1,0:T(8,128)(2,1)S(1)}, bf16[2,32,2048]{2,1,0:T(8,128)(2,1)S(1)}, u32[]{:S(2)}, u32[]{:S(2)}) collective-permute-start(bf16[2,32,2048]{2,1,0:T(8,128)(2,1)S(1)} %get-tuple-element.53), channel_id=1, source_target_pairs={{0,2},{1,3},{2,0},{3,1},{4,6},{5,7},{6,4},{7,5},{8,10},{9,11},{10,... | collective-permute-start | bytes 786440 | tf_op jit(solution)/shard_map/ppermute | solution.py:42
  51.8 10.6 %collective-permute-start.9 = (bf16[2,32,1536]{2,1,0:T(8,128)(2,1)S(1)}, bf16[2,32,1536]{2,1,0:T(8,128)(2,1)S(1)}, u32[]{:S(2)}, u32[]{:S(2)}) collective-permute-start(bf16[2,32,1536]{2,1,0:T(8,128)(2,1)S(1)} %get-tuple-element.52), channel_id=1, source_target_pairs={{0,8},{1,9},{2,10},{3,11},{4,12},{5,13},{6,14},{7,15},{8,0},{9,1},... | collective-permute-start | bytes 589832 | tf_op jit(solution)/shard_map/ppermute | solution.py:42
  60.5 7.8 %collective-permute-start.17 = (bf16[1,32,2560]{2,1,0:T(8,128)(2,1)S(1)}, bf16[1,32,2560]{2,1,0:T(8,128)(2,1)S(1)}, u32[]{:S(2)}, u32[]{:S(2)}) collective-permute-start(bf16[1,32,2560]{2,1,0:T(8,128)(2,1)S(1)} %get-tuple-element.56.refs_8_), channel_id=1, source_target_pairs={{0,8},{1,9},{2,10},{3,11},{4,12},{5,13},{6,14},{7,15},{8,0},{9,1},... | collective-permute-start | bytes 491528 | tf_op jit(solution)/shard_map/ppermute | solution.py:42
  61.9 6.5 %collective-permute-start.18 = (bf16[1,32,3584]{2,1,0:T(8,128)(2,1)S(1)}, bf16[1,32,3584]{2,1,0:T(8,128)(2,1)S(1)}, u32[]{:S(2)}, u32[]{:S(2)}) collective-permute-start(bf16[1,32,3584]{2,1,0:T(8,128)(2,1)S(1)} %get-tuple-element.60), channel_id=1, source_target_pairs={{0,2},{1,3},{2,0},{3,1},{4,6},{5,7},{6,4},{7,5},{8,10},{9,11},{10,... | collective-permute-start | bytes 688136 | tf_op jit(solution)/shard_map/ppermute | solution.py:42
  65.2 7.7 %collective-permute-start.14 = (bf16[1,32,3072]{2,1,0:T(8,128)(2,1)S(1)}, bf16[1,32,3072]{2,1,0:T(8,128)(2,1)S(1)}, u32[]{:S(2)}, u32[]{:S(2)}) collective-permute-start(bf16[1,32,3072]{2,1,0:T(8,128)(2,1)S(1)} %get-tuple-element.57.refs_13_), channel_id=1, source_target_pairs={{0,8},{1,9},{2,10},{3,11},{4,12},{5,13},{6,14},{7,15},{8,0},{9,1},... | collective-permute-start | bytes 589832 | tf_op jit(solution)/shard_map/ppermute | solution.py:42
  76.1 7.7 %collective-permute-start.22 = (bf16[32,5760]{1,0:T(8,128)(2,1)S(1)}, bf16[32,5760]{1,0:T(8,128)(2,1)S(1)}, u32[]{:S(2)}, u32[]{:S(2)}) collective-permute-start(bf16[32,5760]{1,0:T(8,128)(2,1)S(1)} %get-tuple-element.70.refs_2_), channel_id=1, source_target_pairs={{0,6},{1,7},{2,4},{3,5},{4,2},{5,3},{6,0},{7,1},{8,14},{9,15},{10,... | collective-permute-start | bytes 1105928 | tf_op jit(solution)/shard_map/ppermute | solution.py:42
  78.3 7.6 %collective-permute-start.20 = (bf16[32,5632]{1,0:T(8,128)(2,1)S(1)}, bf16[32,5632]{1,0:T(8,128)(2,1)S(1)}, u32[]{:S(2)}, u32[]{:S(2)}) collective-permute-start(bf16[32,5632]{1,0:T(8,128)(2,1)S(1)} %get-tuple-element.68.refs_0_), channel_id=1, source_target_pairs={{0,8},{1,9},{2,10},{3,11},{4,12},{5,13},{6,14},{7,15},{8,0},{9,1},... | collective-permute-start | bytes 1081352 | tf_op jit(solution)/shard_map/ppermute | solution.py:42
  78.5 11.5 %collective-permute-start.24 = (bf16[32,5120]{1,0:T(8,128)(2,1)S(1)}, bf16[32,5120]{1,0:T(8,128)(2,1)S(1)}, u32[]{:S(2)}, u32[]{:S(2)}) collective-permute-start(bf16[32,5120]{1,0:T(8,128)(2,1)S(1)} %get-tuple-element.69.refs_1_), channel_id=1, source_target_pairs={{0,8},{1,9},{2,10},{3,11},{4,12},{5,13},{6,14},{7,15},{8,0},{9,1},... | collective-permute-start | bytes 983048 | tf_op jit(solution)/shard_map/ppermute | solution.py:42
  79.8 14.0 %collective-permute-start.25 = (bf16[32,5760]{1,0:T(8,128)(2,1)S(1)}, bf16[32,5760]{1,0:T(8,128)(2,1)S(1)}, u32[]{:S(2)}, u32[]{:S(2)}) collective-permute-start(bf16[32,5760]{1,0:T(8,128)(2,1)S(1)} %get-tuple-element.70.refs_2_), channel_id=1, source_target_pairs={{0,2},{1,3},{2,0},{3,1},{4,6},{5,7},{6,4},{7,5},{8,10},{9,11},{10,... | collective-permute-start | bytes 1105928 | tf_op jit(solution)/shard_map/ppermute | solution.py:42
  83.7 15.6 %collective-permute-start.28 = (bf16[32,5760]{1,0:T(8,128)(2,1)S(1)}, bf16[32,5760]{1,0:T(8,128)(2,1)S(1)}, u32[]{:S(2)}, u32[]{:S(2)}) collective-permute-start(bf16[32,5760]{1,0:T(8,128)(2,1)S(1)} %collective-permute-done.22.refs_5_), channel_id=1, source_target_pairs={{0,2},{1,3},{2,0},{3,1},{4,6},{5,7},{6,4},{7,5},{8,10},{9,11},{10,... | collective-permute-start | bytes 1105928 | tf_op jit(solution)/shard_map/ppermute | solution.py:42
  84.5 9.3 %collective-permute-start.23 = (bf16[32,5632]{1,0:T(8,128)(2,1)S(1)}, bf16[32,5632]{1,0:T(8,128)(2,1)S(1)}, u32[]{:S(2)}, u32[]{:S(2)}) collective-permute-start(bf16[32,5632]{1,0:T(8,128)(2,1)S(1)} %get-tuple-element.68.refs_0_), channel_id=1, source_target_pairs={{0,6},{1,7},{2,4},{3,5},{4,2},{5,3},{6,0},{7,1},{8,14},{9,15},{10,... | collective-permute-start | bytes 1081352 | tf_op jit(solution)/shard_map/ppermute | solution.py:42
  85.9 13.4 %collective-permute-start.26 = (bf16[32,5632]{1,0:T(8,128)(2,1)S(1)}, bf16[32,5632]{1,0:T(8,128)(2,1)S(1)}, u32[]{:S(2)}, u32[]{:S(2)}) collective-permute-start(bf16[32,5632]{1,0:T(8,128)(2,1)S(1)} %collective-permute-done.20.refs_3_), channel_id=1, source_target_pairs={{0,6},{1,7},{2,4},{3,5},{4,2},{5,3},{6,0},{7,1},{8,14},{9,15},{10,... | collective-permute-start | bytes 1081352 | tf_op jit(solution)/shard_map/ppermute | solution.py:42
  90.1 9.2 %collective-permute-start.27 = (bf16[32,5120]{1,0:T(8,128)(2,1)S(1)}, bf16[32,5120]{1,0:T(8,128)(2,1)S(1)}, u32[]{:S(2)}, u32[]{:S(2)}) collective-permute-start(bf16[32,5120]{1,0:T(8,128)(2,1)S(1)} %collective-permute-done.21.refs_4_), channel_id=1, source_target_pairs={{0,8},{1,9},{2,10},{3,11},{4,12},{5,13},{6,14},{7,15},{8,0},{9,1},... | collective-permute-start | bytes 983048 | tf_op jit(solution)/shard_map/ppermute | solution.py:42
  100.8 14.3 %collective-permute-start.35 = (bf16[4,32,16512]{2,1,0:T(8,128)(2,1)S(1)}, bf16[4,32,16512]{2,1,0:T(8,128)(2,1)S(1)}, u32[]{:S(2)}, u32[]{:S(2)}) collective-permute-start(bf16[4,32,16512]{2,1,0:T(8,128)(2,1)S(1)} %get-tuple-element.77), channel_id=1, source_target_pairs={{0,1},{1,0},{2,3},{3,2},{4,5},{5,4},{6,7},{7,6},{8,9},{9,8},{10,11... | collective-permute-start | bytes 12681224 | tf_op jit(solution)/shard_map/ppermute | solution.py:42
  108.3 24.7 %collective-permute-start.32 = (bf16[4,32,4096]{2,1,0:T(8,128)(2,1)S(1)}, bf16[4,32,4096]{2,1,0:T(8,128)(2,1)S(1)}, u32[]{:S(2)}, u32[]{:S(2)}) collective-permute-start(bf16[4,32,4096]{2,1,0:T(8,128)(2,1)S(1)} %get-tuple-element.74.refs_0_), channel_id=1, source_target_pairs={{0,2},{1,3},{2,0},{3,1},{4,6},{5,7},{6,4},{7,5},{8,10},{9,11},{10,... | collective-permute-start | bytes 3145736 | tf_op jit(solution)/shard_map/ppermute | solution.py:42
  108.3 25.8 %collective-permute-start.33 = (bf16[4,32,4096]{2,1,0:T(8,128)(2,1)S(1)}, bf16[4,32,4096]{2,1,0:T(8,128)(2,1)S(1)}, u32[]{:S(2)}, u32[]{:S(2)}) collective-permute-start(bf16[4,32,4096]{2,1,0:T(8,128)(2,1)S(1)} %get-tuple-element.75.refs_1_), channel_id=1, source_target_pairs={{0,6},{1,7},{2,4},{3,5},{4,2},{5,3},{6,0},{7,1},{8,14},{9,15},{10,... | collective-permute-start | bytes 3145736 | tf_op jit(solution)/shard_map/ppermute | solution.py:42
  110.1 24.3 %collective-permute-start.34 = (bf16[4,32,4096]{2,1,0:T(8,128)(2,1)S(1)}, bf16[4,32,4096]{2,1,0:T(8,128)(2,1)S(1)}, u32[]{:S(2)}, u32[]{:S(2)}) collective-permute-start(bf16[4,32,4096]{2,1,0:T(8,128)(2,1)S(1)} %get-tuple-element.76.refs_2_), channel_id=1, source_target_pairs={{0,8},{1,9},{2,10},{3,11},{4,12},{5,13},{6,14},{7,15},{8,0},{9,1},... | collective-permute-start | bytes 3145736 | tf_op jit(solution)/shard_map/ppermute | solution.py:42
  136.2 13.2 %collective-permute-start.31 = (bf16[4,32,1664]{2,1,0:T(8,128)(2,1)S(1)}, bf16[4,32,1664]{2,1,0:T(8,128)(2,1)S(1)}, u32[]{:S(2)}, u32[]{:S(2)}) collective-permute-start(bf16[4,32,1664]{2,1,0:T(8,128)(2,1)S(1)} %get-tuple-element.73.refs_2_.refs_6_), channel_id=1, source_target_pairs={{0,8},{1,9},{2,10},{3,11},{4,12},{5,13},{6,14},{7,15},{8,0},{9,1},... | collective-permute-start | bytes 1277960 | tf_op jit(solution)/shard_map/ppermute | solution.py:42
  137.5 11.9 %collective-permute-start.29 = (bf16[4,32,1536]{2,1,0:T(8,128)(2,1)S(1)}, bf16[4,32,1536]{2,1,0:T(8,128)(2,1)S(1)}, u32[]{:S(2)}, u32[]{:S(2)}) collective-permute-start(bf16[4,32,1536]{2,1,0:T(8,128)(2,1)S(1)} %get-tuple-element.71.refs_0_), channel_id=1, source_target_pairs={{0,2},{1,3},{2,0},{3,1},{4,6},{5,7},{6,4},{7,5},{8,10},{9,11},{10,... | collective-permute-start | bytes 1179656 | tf_op jit(solution)/shard_map/ppermute | solution.py:42
  138.3 11.0 %collective-permute-start.30 = (bf16[4,32,1024]{2,1,0:T(8,128)(2,1)S(1)}, bf16[4,32,1024]{2,1,0:T(8,128)(2,1)S(1)}, u32[]{:S(2)}, u32[]{:S(2)}) collective-permute-start(bf16[4,32,1024]{2,1,0:T(8,128)(2,1)S(1)} %get-tuple-element.72.refs_1_), channel_id=1, source_target_pairs={{0,6},{1,7},{2,4},{3,5},{4,2},{5,3},{6,0},{7,1},{8,14},{9,15},{10,... | collective-permute-start | bytes 786440 | tf_op jit(solution)/shard_map/ppermute | solution.py:42
  (17 other events, 121.1 us)
